TPU v7x, 32 devices: a whole 2x2x4 slice. The times are simulated.
32 devices in a mesh: groups: 2 (over y), tm: 4 (over z), space: 2 (over x), chan: 2 (over core).
Axes of the slice: x: 2, y: 2, z: 4, core: 2. Of those that a mesh axis runs over, the one named last changes fastest.
Arguments:
- latents: bfloat16 [4, 8, 4, 8, 512], P('groups', 'tm', 'space', None, 'chan'), parts along dimension 0, may hold values from -60 to 60
- conv_weight: bfloat16 [3, 3, 3, 512, 512], P(None, None, None, 'tm', 'chan'), may hold values from -0.0546875 to 0.0546875
- conv_bias: float32 [512], P('chan'), may hold values from -4 to 4
- gn_gain: float32 [512], P('chan'), may hold values from 0.5 to 1.5
- gn_shift: float32 [512], P('chan'), may hold values from -3 to 3
- up_weight: bfloat16 [3, 3, 512, 512], P(None, None, None, 'chan'), may hold values from -0.09375 to 0.09375
- up_bias: float32 [512], P('chan'), may hold values from -3 to 3
Outputs:
- decoded: bfloat16 [4, 8, 8, 16, 512], P('groups', None, 'space', 'tm', 'chan'), parts along dimension 0
There are 2 independent parts, one for each index of `groups`. A program takes and returns all parts, laid end to end along the dimension named above; an argument that names none is the same for every part. Nothing has to cross between parts.
All inputs are finite; a program needn't handle non-finite values.
Results may differ from a plain program's by a relative error of at most 0.0052.
The roundings to bfloat16 on the way count: a program that leaves them out, or rounds other values in their place, can miss the bound.
Values may be sent and summed in bfloat16 or wider, within the bound.
No kernel may reach another device: no remote copies, remote signals or barrier semaphores. Data moves between devices by JAX's collectives and lax.ppermute only.
A program may use at most 64 MiB of HBM per device.

v0:
```python
import jax
import jax.numpy as jnp
from jax import lax
from jax.sharding import PartitionSpec as P

C = 512
GROUPS = 32


def from_behind(value, axis, steps):
    count = lax.axis_size(axis)
    pairs = [(source, (source + steps) % count) for source in range(count)]
    return lax.ppermute(value, axis, pairs)


def with_halo(block, sides, width):
    for axis, dim in sides:
        count = lax.axis_size(axis)
        forward = [(i, i + 1) for i in range(count - 1)]
        backward = [(target, source) for source, target in forward]
        low = lax.ppermute(
            lax.slice_in_dim(block, block.shape[dim] - width, None, axis=dim), axis, forward
        )
        high = lax.ppermute(lax.slice_in_dim(block, 0, width, axis=dim), axis, backward)
        block = jnp.concatenate([low, block, high], axis=dim)
    return block


def causal_frames(latents):
    clip_count = latents.shape[0]
    span_count = lax.axis_size("tm")
    span_index = lax.axis_index("tm")
    tail_frames = from_behind(latents, "tm", 1)
    clip_order = jnp.arange(clip_count, dtype=jnp.int32)
    opening = (span_index - clip_order) % span_count == 0
    tail_frames = jnp.where(
        opening[:, None, None, None, None], jnp.zeros_like(tail_frames), tail_frames
    )
    return jnp.concatenate([tail_frames, latents], axis=1)


def causal_conv(latents, conv_weight, conv_bias):
    framed = causal_frames(latents)
    bordered = with_halo(framed, (("space", 2),), 1)
    gathered = lax.all_gather(bordered, "chan", axis=4, tiled=True)
    padded = jnp.pad(gathered, ((0, 0), (0, 0), (0, 0), (1, 1), (0, 0)))
    initial = jnp.zeros(latents.shape[:4] + (conv_weight.shape[4],), jnp.float32)
    summed = initial + lax.conv_general_dilated(
        padded,
        lax.all_gather(conv_weight, "tm", axis=3, tiled=True),
        (1, 1, 1),
        "VALID",
        dimension_numbers=("NDHWC", "DHWIO", "NDHWC"),
        preferred_element_type=jnp.float32,
    )
    return (summed + conv_bias).astype(jnp.bfloat16)


def moments(block):
    clip_count, frame_count, row_count, col_count, chan_count = block.shape
    group_width = C // GROUPS
    grouped_values = block.astype(jnp.float32).reshape(
        clip_count, frame_count, row_count, col_count, chan_count // group_width, group_width
    )
    group_sums = jnp.sum(grouped_values, axis=(1, 2, 3, 5))
    squared_sums = jnp.sum(grouped_values * grouped_values, axis=(1, 2, 3, 5))
    group_sums, squared_sums = lax.psum((group_sums, squared_sums), ("tm", "space"))
    element_count = float(
        frame_count
        * row_count
        * col_count
        * group_width
        * lax.axis_size("tm")
        * lax.axis_size("space")
    )
    group_mean = group_sums / element_count
    group_variance = squared_sums / element_count - group_mean * group_mean
    return (group_mean, lax.rsqrt(group_variance + 1e-06))


def activate(block, group_mean, factor, gn_gain, gn_shift):
    clip_count, frame_count, row_count, col_count, chan_count = block.shape
    group_width = C // GROUPS
    grouped_values = block.astype(jnp.float32).reshape(
        clip_count, frame_count, row_count, col_count, chan_count // group_width, group_width
    )
    normed = (grouped_values - group_mean[:, None, None, None, :, None]) * factor[
        :, None, None, None, :, None
    ]
    normed = normed.reshape(block.shape) * gn_gain + gn_shift
    return jax.nn.silu(normed).astype(jnp.bfloat16)


def relayout(block):
    return lax.all_to_all(block, "tm", split_axis=3, concat_axis=1, tiled=True)


def widen(rimmed, up_weight, up_bias):
    gathered = lax.all_gather(rimmed, "chan", axis=4, tiled=True)
    widened = jnp.repeat(jnp.repeat(gathered, 2, axis=2), 2, axis=3)[:, :, 1:-1, 1:-1]
    clip_count, frame_count, tall_count, broad_count, depth_count = widened.shape
    flat = widened.reshape(clip_count * frame_count, tall_count, broad_count, depth_count)
    output = lax.conv_general_dilated(
        flat,
        up_weight,
        (1, 1),
        "VALID",
        dimension_numbers=("NHWC", "HWIO", "NHWC"),
        preferred_element_type=jnp.float32,
    )
    output = output + up_bias
    return output.reshape(
        clip_count, frame_count, tall_count - 2, broad_count - 2, up_weight.shape[3]
    ).astype(jnp.bfloat16)


def on_device(latents, conv_weight, conv_bias, gn_gain, gn_shift, up_weight, up_bias):
    conved = causal_conv(latents, conv_weight, conv_bias)
    tiled = relayout(conved)
    group_mean, factor = moments(tiled)
    active = activate(tiled, group_mean, factor, gn_gain, gn_shift)
    rimmed = with_halo(active, (("tm", 3), ("space", 2)), 1)
    return widen(rimmed, up_weight, up_bias)


def solution(mesh):
    placed = (
        P("groups", "tm", "space", None, "chan"),
        P(None, None, None, "tm", "chan"),
        P("chan"),
        P("chan"),
        P("chan"),
        P(None, None, None, "chan"),
        P("chan"),
    )
    return jax.shard_map(
        on_device,
        mesh=mesh,
        in_specs=placed,
        out_specs=P("groups", None, "space", "tm", "chan"),
        check_vma=False,
    )
```

profile of v0, /device:TPU:0, one launch (start us, length us, event | category | flops | bytes accessed | tf_op | source)
XLA Modules:
  0.0 199.0 jit_solution(7038103814849547957)
XLA Ops:
  6.5 0.0 copy-start
  6.5 0.0 all-gather.2.cloned.1.call-start
  6.5 0.7 all-gather.2.cloned.1.call-update
  7.3 0.8 copy.28
  8.1 3.1 %collective-permute-start = (bf16[2,2,2,8,256]{4,0,3,2,1:T(2,128)(2,1)S(1)}, bf16[2,2,2,8,256]{4,0,3,2,1:T(2,128)(2,1)S(1)}, u32[]{:S(2)}, u32[]{:S(2)}) collective-permute-start(bf16[2,2,2,8,256]{4,0,3,2,1:T(2,128)(2,1)S(1)} %copy.28), channel_id=1, source_target_pairs={{0,4},{4,8},{8,12},{12,0},{1,5},{5,9},{9,13},{13,1},{2,6},{6,10},{... | collective-permute-start | bytes 98312 | tf_op jit(solution)/shard_map/ppermute | solution.py:13
  11.1 3.9 %collective-permute-done = bf16[2,2,2,8,256]{4,0,3,2,1:T(2,128)(2,1)S(1)} collective-permute-done((bf16[2,2,2,8,256]{4,0,3,2,1:T(2,128)(2,1)S(1)}, bf16[2,2,2,8,256]{4,0,3,2,1:T(2,128)(2,1)S(1)}, u32[]{:S(2)}, u32[]{:S(2)}) %collective-permute-start) | collective-permute-done | bytes 32800 | tf_op jit(solution)/shard_map/ppermute | solution.py:13
  15.1 0.1 broadcast_select_fusion
  15.2 0.1 fusion.5
  15.2 3.6 %collective-permute-start.1 = (bf16[2,4,1,8,256]{4,0,3,2,1:T(2,128)(2,1)S(1)}, bf16[2,4,1,8,256]{4,0,3,2,1:T(2,128)(2,1)S(1)}, u32[]{:S(2)}, u32[]{:S(2)}) collective-permute-start(bf16[2,4,1,8,256]{4,0,3,2,1:T(2,128)(2,1)S(1)} %get-tuple-element.11), channel_id=1, source_target_pairs={{0,2},{1,3},{4,6},{5,7},{8,10},{9,11},{12,14},{13,15},{16,18},{17,... | collective-permute-start | bytes 98312 | tf_op jit(solution)/shard_map/ppermute | solution.py:21
  18.9 1.3 collective-permute-start.2
  20.2 0.3 collective-permute-done.1
  20.4 4.2 %collective-permute-done.2 = bf16[2,4,1,8,256]{4,0,3,2,1:T(2,128)(2,1)S(1)} collective-permute-done((bf16[2,4,1,8,256]{4,0,3,2,1:T(2,128)(2,1)S(1)}, bf16[2,4,1,8,256]{4,0,3,2,1:T(2,128)(2,1)S(1)}, u32[]{:S(2)}, u32[]{:S(2)}) %collective-permute-start.2) | collective-permute-done | bytes 32800 | tf_op jit(solution)/shard_map/ppermute | solution.py:24
  24.7 0.2 pad_maximum_fusion
  24.9 2.0 %all_gather.9 = bf16[2,4,4,8,512]{4,0,3,2,1:T(2,128)(2,1)S(1)} all-gather(bf16[2,4,4,8,256]{4,0,3,2,1:T(2,128)(2,1)S(1)} %pad_maximum_fusion), channel_id=1, replica_groups=mesh['groups'=2,'tm'=4,'space'=2,'chan'=2] {'chan'}, dimensions={4}, use_global_device_ids=true | all-gather | bytes 393216 | tf_op jit(solution)/shard_map/all_gather | solution.py:45
  26.9 113.0 %all-gather.2.cloned.1.call-done = bf16[3,3,3,512,256]{4,3,2,1,0:T(8,128)(2,1)} async-done(((bf16[3,3,3,128,256]{4,3,2,1,0:T(8,128)(2,1)}), bf16[3,3,3,512,256]{4,3,2,1,0:T(8,128)(2,1)}) %all-gather.2.cloned.1.call-update) | async-done | bytes 7077904 | tf_op jit(solution)/shard_map/all_gather | solution.py:50
  139.9 5.1 %fusion.10 = f32[2,2,2,8,256]{4,0,3,2,1:T(2,128)S(1)} fusion(bf16[2,4,4,8,512]{4,0,3,2,1:T(2,128)(2,1)S(1)} %all_gather.9, bf16[3,3,3,512,256]{4,3,2,1,0:T(8,128)(2,1)} %all-gather.2.cloned.1.call-done), kind=kOutput, calls=%fused_computation.29 | convolution fusion | flops 415236096 | bytes 7405568 | tf_op jit(solution)/shard_map/conv_general_dilated | solution.py:48
  145.0 0.0 copy-done.1
  145.0 0.0 copy-start.4
  145.1 8.0 %all_to_all.4 = bf16[2,2,2,8,256]{4,0,2,1,3:T(2,128)(2,1)S(1)} all-to-all(bf16[2,2,2,8,256]{4,0,2,1,3:T(2,128)(2,1)S(1)} %copy.31), channel_id=1, replica_groups=mesh['groups'=2,'tm'=4,'space'=2,'chan'=2] {'tm'}, dimensions={3} | all-to-all | bytes 65536 | tf_op jit(solution)/shard_map/all_to_all | solution.py:95
  153.1 0.1 bitcast_reduce_fusion
  153.2 0.1 reduce_sum.24
  153.2 0.1 reduce_sum.36
  153.3 0.1 reduce_sum.25
  153.4 0.1 reduce_sum.37
  153.5 18.7 %all-reduce = (f32[2,16]{1,0:T(2,128)S(1)}, f32[2,16]{1,0:T(2,128)S(1)}) all-reduce(f32[2,16]{1,0:T(2,128)S(1)} %reduce_sum.37, f32[2,16]{1,0:T(2,128)S(1)} %reduce_sum.25), channel_id=1, replica_groups=mesh['groups'=2,'tm'=4,'space'=2,'chan'=2] {'tm','space'}, use_global_device_ids=true, to_apply=%region_5.6 | all-reduce | flops 64 | bytes 512 | tf_op jit(solution)/shard_map/psum | solution.py:67
  172.2 0.1 mul.34
  172.2 0.1 mul.35
  172.3 0.1 sub.28
  172.4 0.1 sub.29
  172.5 0.0 copy-done.2
  172.5 0.0 copy-done.3
  172.5 0.1 fusion.4
  172.7 1.3 collective-permute-start.3
  174.0 1.3 collective-permute-start.4
  175.3 0.3 collective-permute-done.3
  175.6 4.2 %collective-permute-done.4 = bf16[2,8,2,1,256]{4,3,2,1,0:T(2,128)(2,1)S(1)} collective-permute-done((bf16[2,8,2,1,256]{4,3,2,1,0:T(2,128)(2,1)S(1)}, bf16[2,8,2,1,256]{4,3,2,1,0:T(2,128)(2,1)S(1)}, u32[]{:S(2)}, u32[]{:S(2)}) %collective-permute-start.4) | collective-permute-done | bytes 16416 | tf_op jit(solution)/shard_map/ppermute | solution.py:24
  179.8 0.1 pad_maximum_fusion.2
  180.0 2.4 %collective-permute-start.5 = (bf16[2,8,1,4,256]{4,3,2,1,0:T(4,128)(2,1)S(1)}, bf16[2,8,1,4,256]{4,3,2,1,0:T(4,128)(2,1)S(1)}, u32[]{:S(2)}, u32[]{:S(2)}) collective-permute-start(bf16[2,8,1,4,256]{4,3,2,1,0:T(4,128)(2,1)S(1)} %get-tuple-element.9), channel_id=1, source_target_pairs={{0,2},{1,3},{4,6},{5,7},{8,10},{9,11},{12,14},{13,15},{16,18},{17,... | collective-permute-start | bytes 98312 | tf_op jit(solution)/shard_map/ppermute | solution.py:21
  182.3 1.3 collective-permute-start.6
  183.6 0.3 collective-permute-done.5
  183.9 4.2 %collective-permute-done.6 = bf16[2,8,1,4,256]{4,3,2,1,0:T(4,128)(2,1)S(1)} collective-permute-done((bf16[2,8,1,4,256]{4,3,2,1,0:T(4,128)(2,1)S(1)}, bf16[2,8,1,4,256]{4,3,2,1,0:T(4,128)(2,1)S(1)}, u32[]{:S(2)}, u32[]{:S(2)}) %collective-permute-start.6) | collective-permute-done | bytes 32800 | tf_op jit(solution)/shard_map/ppermute | solution.py:24
  188.2 0.1 pad_maximum_fusion.1
  188.3 2.0 %all_gather.11 = bf16[2,8,4,4,512]{4,3,2,1,0:T(4,128)(2,1)S(1)} all-gather(bf16[2,8,4,4,256]{4,3,2,1,0:T(4,128)(2,1)S(1)} %pad_maximum_fusion.1), channel_id=1, replica_groups=mesh['groups'=2,'tm'=4,'space'=2,'chan'=2] {'chan'}, dimensions={4}, use_global_device_ids=true | all-gather | bytes 393216 | tf_op jit(solution)/shard_map/all_gather | solution.py:99
  190.3 0.1 copy.33
  190.4 0.1 broadcast_in_dim.26
  190.5 0.1 broadcast_in_dim.27
  190.7 0.8 fusion.1
  191.4 0.7 copy.34
  (13 shorter events, 0.2 us)
Async XLA Ops:
  6.5 184.1 %copy-start = (bf16[3,3,512,256]{3,2,1,0:T(8,128)(2,1)S(1)}, bf16[3,3,512,256]{3,2,1,0:T(8,128)(2,1)}, u32[]{:S(2)}) copy-start(bf16[3,3,512,256]{3,2,1,0:T(8,128)(2,1)} %param.12) | copy-start | bytes 7077892
  6.5 133.3 %all-gather.2.cloned.1.call-start = ((), (), s32[]{:S(2)}) async-start(), calls=%async_computation.1 | async-start | bytes 8847360 | tf_op jit(solution)/shard_map/all_gather | solution.py:50
  8.1 7.0 %collective-permute-start = (bf16[2,2,2,8,256]{4,0,3,2,1:T(2,128)(2,1)S(1)}, bf16[2,2,2,8,256]{4,0,3,2,1:T(2,128)(2,1)S(1)}, u32[]{:S(2)}, u32[]{:S(2)}) collective-permute-start(bf16[2,2,2,8,256]{4,0,3,2,1:T(2,128)(2,1)S(1)} %copy.28), channel_id=1, source_target_pairs={{0,4},{4,8},{8,12},{12,0},{1,5},{5,9},{9,13},{13,1},{2,6},{6,10},{... | collective-permute-start | bytes 98312 | tf_op jit(solution)/shard_map/ppermute | solution.py:13
  15.2 5.2 %collective-permute-start.1 = (bf16[2,4,1,8,256]{4,0,3,2,1:T(2,128)(2,1)S(1)}, bf16[2,4,1,8,256]{4,0,3,2,1:T(2,128)(2,1)S(1)}, u32[]{:S(2)}, u32[]{:S(2)}) collective-permute-start(bf16[2,4,1,8,256]{4,0,3,2,1:T(2,128)(2,1)S(1)} %get-tuple-element.11), channel_id=1, source_target_pairs={{0,2},{1,3},{4,6},{5,7},{8,10},{9,11},{12,14},{13,15},{16,18},{17,... | collective-permute-start | bytes 98312 | tf_op jit(solution)/shard_map/ppermute | solution.py:21
  18.9 5.8 %collective-permute-start.2 = (bf16[2,4,1,8,256]{4,0,3,2,1:T(2,128)(2,1)S(1)}, bf16[2,4,1,8,256]{4,0,3,2,1:T(2,128)(2,1)S(1)}, u32[]{:S(2)}, u32[]{:S(2)}) collective-permute-start(bf16[2,4,1,8,256]{4,0,3,2,1:T(2,128)(2,1)S(1)} %get-tuple-element.12), channel_id=1, source_target_pairs={{2,0},{3,1},{6,4},{7,5},{10,8},{11,9},{14,12},{15,13},{18,16},{19,... | collective-permute-start | bytes 98312 | tf_op jit(solution)/shard_map/ppermute | solution.py:24
  26.9 118.1 %copy-start.1 = (f32[256]{0:T(256)S(1)}, f32[256]{0:T(256)}, u32[]{:S(2)}) copy-start(f32[256]{0:T(256)} %param.9) | copy-start | bytes 3076
  26.9 145.6 %copy-start.2 = (f32[256]{0:T(256)S(1)}, f32[256]{0:T(256)}, u32[]{:S(2)}) copy-start(f32[256]{0:T(256)} %param.11) | copy-start | bytes 3076
  26.9 145.6 %copy-start.3 = (f32[256]{0:T(256)S(1)}, f32[256]{0:T(256)}, u32[]{:S(2)}) copy-start(f32[256]{0:T(256)} %param.10) | copy-start | bytes 3076
  145.0 45.7 %copy-start.4 = (f32[256]{0:T(256)S(1)}, f32[256]{0:T(256)}, u32[]{:S(2)}) copy-start(f32[256]{0:T(256)} %param.13) | copy-start | bytes 3076
  172.7 2.9 %collective-permute-start.3 = (bf16[2,8,2,1,256]{4,3,2,1,0:T(2,128)(2,1)S(1)}, bf16[2,8,2,1,256]{4,3,2,1,0:T(2,128)(2,1)S(1)}, u32[]{:S(2)}, u32[]{:S(2)}) collective-permute-start(bf16[2,8,2,1,256]{4,3,2,1,0:T(2,128)(2,1)S(1)} %get-tuple-element.13), channel_id=1, source_target_pairs={{0,4},{4,8},{8,12},{1,5},{5,9},{9,13},{2,6},{6,10},{10,14},{3,7},{... | collective-permute-start | bytes 49160 | tf_op jit(solution)/shard_map/ppermute | solution.py:21
  174.0 5.8 %collective-permute-start.4 = (bf16[2,8,2,1,256]{4,3,2,1,0:T(2,128)(2,1)S(1)}, bf16[2,8,2,1,256]{4,3,2,1,0:T(2,128)(2,1)S(1)}, u32[]{:S(2)}, u32[]{:S(2)}) collective-permute-start(bf16[2,8,2,1,256]{4,3,2,1,0:T(2,128)(2,1)S(1)} %get-tuple-element.14), channel_id=1, source_target_pairs={{4,0},{8,4},{12,8},{5,1},{9,5},{13,9},{6,2},{10,6},{14,10},{7,3},{... | collective-permute-start | bytes 49160 | tf_op jit(solution)/shard_map/ppermute | solution.py:24
  180.0 4.0 %collective-permute-start.5 = (bf16[2,8,1,4,256]{4,3,2,1,0:T(4,128)(2,1)S(1)}, bf16[2,8,1,4,256]{4,3,2,1,0:T(4,128)(2,1)S(1)}, u32[]{:S(2)}, u32[]{:S(2)}) collective-permute-start(bf16[2,8,1,4,256]{4,3,2,1,0:T(4,128)(2,1)S(1)} %get-tuple-element.9), channel_id=1, source_target_pairs={{0,2},{1,3},{4,6},{5,7},{8,10},{9,11},{12,14},{13,15},{16,18},{17,... | collective-permute-start | bytes 98312 | tf_op jit(solution)/shard_map/ppermute | solution.py:21
  182.3 5.8 %collective-permute-start.6 = (bf16[2,8,1,4,256]{4,3,2,1,0:T(4,128)(2,1)S(1)}, bf16[2,8,1,4,256]{4,3,2,1,0:T(4,128)(2,1)S(1)}, u32[]{:S(2)}, u32[]{:S(2)}) collective-permute-start(bf16[2,8,1,4,256]{4,3,2,1,0:T(4,128)(2,1)S(1)} %get-tuple-element.10), channel_id=1, source_target_pairs={{2,0},{3,1},{6,4},{7,5},{10,8},{11,9},{14,12},{15,13},{18,16},{19,... | collective-permute-start | bytes 98312 | tf_op jit(solution)/shard_map/ppermute | solution.py:24
Sparse Core Ops, SparseCore 0:
  8.9 130.8 all-gather.1
where the time goes:
time: 199 us
  waiting for transfers between devices  131 us (66%)
  blocking collectives  30.7 us (15%)
  starting transfers between devices  14.2 us (7%)
  between operations  13.6 us (7%)
  matrix products  5.87 us (3%)
  local copies, waits for them, and re-layouts  2.47 us (1%)
    all_gather x1, waiting for transfers between devices, causal_conv(): lax.all_gather(conv_weight, 'tm', axis=3, tiled=True)  113 us
    psum x1, blocking collectives, moments(): lax.psum((group_sums, squared_sums), ('tm', 'space'))  18.7 us
    ppermute x3, waiting for transfers between devices, with_halo(): lax.ppermute(lax.slice_in_dim(block, 0, width, axis=dim), axis, backward)  12.7 us
    all_to_all x1, blocking collectives, relayout(): return lax.all_to_all(block, 'tm', split_axis=3, concat_axis=1, tiled=True)  8.01 us
    ppermute x3, starting transfers between devices, with_halo(): lax.ppermute(lax.slice_in_dim(block, block.shape[dim] - width, None, axis...  7.28 us
    conv_general_dilated x1, matrix products, causal_conv(): lax.conv_general_dilated(padded, lax.all_gather(conv_weight, 'tm', axis=3...  5.09 us
  transfers between devices with their start and end apart: 8, of which 8 were waited for; matrix products, arithmetic and copies ran while one was open for 1% of the time, Pallas kernels for 0%

commit v1 on v0

v1 whole, which is shorter than its diff:
```python
import jax
import jax.numpy as jnp
from jax import lax
from jax.sharding import PartitionSpec as P

C = 512
GROUPS = 32


def shifted(value, axis, step):
    count = lax.axis_size(axis)
    pairs = [(i, i + step) for i in range(count) if 0 <= i + step < count]
    return lax.ppermute(value, axis, pairs)


def rows_around(block, axis_rows, depth):
    low = shifted(lax.slice_in_dim(block, block.shape[axis_rows] - depth, None, axis=axis_rows), "space", 1)
    high = shifted(lax.slice_in_dim(block, 0, depth, axis=axis_rows), "space", -1)
    return jnp.concatenate([low, block, high], axis=axis_rows)


def input_slice(latents):
    clips, span, rows, cols, half = latents.shape
    spans, spaces, chans = lax.axis_size("tm"), lax.axis_size("space"), lax.axis_size("chan")
    me, row_block = lax.axis_index("tm"), lax.axis_index("space")
    depth = half * chans // spans
    per_half = half // depth
    if spaces == 2:
        whole = lax.all_gather(latents, ("tm", "space", "chan"))
        whole = whole.reshape(spans, spaces, chans, clips, span, rows, cols, per_half, depth)
        mine = lax.dynamic_index_in_dim(whole, me // per_half, axis=2, keepdims=False)
        mine = lax.dynamic_index_in_dim(mine, me % per_half, axis=7 - 1, keepdims=False)
        mine = mine.transpose(2, 0, 3, 1, 4, 5, 6).reshape(clips, spans * span, spaces * rows, cols, depth)
        mine = jnp.pad(mine, ((0, 0), (0, 0), (1, 1), (0, 0), (0, 0)))
        mine = lax.dynamic_slice_in_dim(mine, row_block * rows, rows + 2, axis=2)
    else:
        bordered = rows_around(latents, 2, 1)
        whole = lax.all_gather(bordered, ("tm", "chan"))
        whole = whole.reshape((spans, chans) + bordered.shape[:4] + (per_half, depth))
        mine = lax.dynamic_index_in_dim(whole, me // per_half, axis=1, keepdims=False)
        mine = lax.dynamic_index_in_dim(mine, me % per_half, axis=5, keepdims=False)
        mine = mine.transpose(1, 0, 2, 3, 4, 5).reshape(clips, spans * span, rows + 2, cols, depth)
    return jnp.stack([jnp.roll(mine[c], -c * span, axis=0) for c in range(clips)])


def on_device(latents, conv_weight, conv_bias, gn_gain, gn_shift, up_weight, up_bias):
    clips, span, rows, cols, half = latents.shape
    spans, spaces, chans = lax.axis_size("tm"), lax.axis_size("space"), lax.axis_size("chan")
    me, row_block = lax.axis_index("tm"), lax.axis_index("space")
    frames, width = span * spans, cols // spans
    group_width = C // GROUPS

    mine = input_slice(latents)
    padded = jnp.pad(mine, ((0, 0), (2, 0), (0, 0), (1, 1), (0, 0)))
    partial = lax.conv_general_dilated(
        padded,
        conv_weight,
        (1, 1, 1),
        "VALID",
        dimension_numbers=("NDHWC", "DHWIO", "NDHWC"),
        preferred_element_type=jnp.float32,
    )
    partial = jnp.stack([jnp.roll(partial[c], c * span, axis=0) for c in range(clips)])
    parts = partial.reshape(clips, frames, rows, spans, width, half)
    parts = parts.transpose(3, 0, 1, 2, 4, 5)
    parts = lax.all_to_all(parts, "tm", split_axis=0, concat_axis=0, tiled=True)
    conved = (jnp.sum(parts, axis=0) + conv_bias).astype(jnp.bfloat16)

    values = conved.astype(jnp.float32).reshape(-1, half)
    values = values.reshape(clips, frames * rows * width, half // group_width, group_width)
    if spaces == 2:
        every = lax.all_gather(conved, ("tm", "space", "chan"))
        every = every.reshape(spans, spaces, chans, clips, frames, rows, width, half)
        every = every.transpose(3, 4, 1, 5, 0, 6, 2, 7).reshape(clips, frames, spaces * rows, cols, C)
        gain = lax.all_gather(gn_gain, "chan", tiled=True)
        shift = lax.all_gather(gn_shift, "chan", tiled=True)
        values = every.astype(jnp.float32).reshape(clips, -1, GROUPS, group_width)
        sums = jnp.sum(values, axis=(1, 3))
        squares = jnp.sum(values * values, axis=(1, 3))
        count = float(values.shape[1] * group_width)
        mean = sums / count
        factor = lax.rsqrt(squares / count - mean * mean + 1e-06)
        edged = jnp.pad(every, ((0, 0), (0, 0), (1, 1), (1, 1), (0, 0)))
        tile = lax.dynamic_slice(
            edged, (0, 0, row_block * rows, me * width, 0), (clips, frames, rows + 2, width + 2, C)
        )
    else:
        sums = jnp.sum(values, axis=(1, 3))
        squares = jnp.sum(values * values, axis=(1, 3))
        sums, squares = lax.psum((sums, squares), ("tm", "space"))
        count = float(values.shape[1] * group_width * spans * spaces)
        mean = sums / count
        factor = lax.rsqrt(squares / count - mean * mean + 1e-06)
        bordered = rows_around(conved, 2, 1)
        left = shifted(bordered[:, :, :, -1:], "tm", 1)
        right = shifted(bordered[:, :, :, :1], "tm", -1)
        tile = jnp.concatenate([left, bordered, right], axis=3)
        tile = lax.all_gather(tile, "chan", axis=4, tiled=True)
        gain, shift, mean, factor = (
            lax.all_gather(v, "chan", axis=v.ndim - 1, tiled=True) for v in (gn_gain, gn_shift, mean, factor)
        )
    mean = jnp.repeat(mean, group_width, axis=1)[:, None, None, None]
    factor = jnp.repeat(factor, group_width, axis=1)[:, None, None, None]
    normed = (tile.astype(jnp.float32) - mean) * factor * gain + shift
    row_at = row_block * rows - 1 + jnp.arange(rows + 2)
    col_at = me * width - 1 + jnp.arange(width + 2)
    inside = ((row_at >= 0) & (row_at < rows * spaces))[:, None] & ((col_at >= 0) & (col_at < cols))[None]
    active = jnp.where(inside[None, None, :, :, None], jax.nn.silu(normed), 0.0).astype(jnp.bfloat16)
    wide = jnp.repeat(jnp.repeat(active, 2, axis=2), 2, axis=3)[:, :, 1:-1, 1:-1]
    flat = wide.reshape((clips * frames,) + wide.shape[2:])
    output = lax.conv_general_dilated(
        flat,
        up_weight,
        (1, 1),
        "VALID",
        dimension_numbers=("NHWC", "HWIO", "NHWC"),
        preferred_element_type=jnp.float32,
    )
    output = (output + up_bias).astype(jnp.bfloat16)
    return output.reshape(clips, frames, 2 * rows, 2 * width, half)


def solution(mesh):
    placed = (
        P("groups", "tm", "space", None, "chan"),
        P(None, None, None, "tm", "chan"),
        P("chan"),
        P("chan"),
        P("chan"),
        P(None, None, None, "chan"),
        P("chan"),
    )
    return jax.shard_map(
        on_device,
        mesh=mesh,
        in_specs=placed,
        out_specs=P("groups", None, "space", "tm", "chan"),
        check_vma=False,
    )
```

time: 199 us -> 66.3 us (0.33)
  waiting for transfers between devices: 131 us -> 5.94 us
  blocking collectives: 30.7 us -> 47.2 us
  between operations: 13.6 us -> 0.27 us
  starting transfers between devices: 14.2 us -> 3.4 us
  matrix products: 5.87 us -> 3.87 us
    all_gather x1 -> x0, waiting for transfers between devices: 113 us -> none  [causal_conv(): lax.all_gather(conv_weight, 'tm', axis=3, tiled=True)]
    all_gather x2 -> x4, blocking collectives: 3.99 us -> 47.2 us  [the longest x1 24.9 us: input_slice(): whole = lax.all_gather(latents, ('tm', 'space', 'chan'))]
    psum x1 -> x0, blocking collectives: 18.7 us -> none  [moments(): lax.psum((group_sums, squared_sums), ('tm', 'space'))]
    ppermute x7 -> x0, waiting for transfers between devices: 17.4 us -> none  [the longest x3 12.7 us: with_halo(): lax.ppermute(lax.slice_in_dim(block, 0, width, axis=dim), axis, backward)]
    ppermute x7 -> x0, starting transfers between devices: 14.2 us -> none  [the longest x3 7.28 us: with_halo(): lax.ppermute(lax.slice_in_dim(block, block.shape[dim] - width, None, axis...]
    all_to_all x1 -> x0, blocking collectives: 8.01 us -> none  [relayout(): return lax.all_to_all(block, 'tm', split_axis=3, concat_axis=1, tiled=True)]
    all_to_all x0 -> x1, waiting for transfers between devices: none -> 5.94 us  [on_device(): parts = lax.all_to_all(parts, 'tm', split_axis=0, concat_axis=0, tiled=True)]
    all_to_all x0 -> x1, starting transfers between devices: none -> 3.4 us  [on_device(): parts = lax.all_to_all(parts, 'tm', split_axis=0, concat_axis=0, tiled=True)]
  transfers between devices with their start and end apart: 8 -> 1, of which waited for: 8 -> 1; matrix products, arithmetic and copies ran while one was open for 1% -> 0% of each run, Pallas kernels for 0% -> 0%
where the time goes in v1:
time: 66.3 us; the launch traced here: 66.1 us
  blocking collectives  47.2 us (71%)
  waiting for transfers between devices  5.94 us (9%)
  matrix products  3.87 us (6%)
  starting transfers between devices  3.4 us (5%)
  local copies, waits for them, and re-layouts  3.29 us (5%)
  other arithmetic  2.1 us (3%)
    all_gather x1, blocking collectives, input_slice(): whole = lax.all_gather(latents, ('tm', 'space', 'chan'))  24.9 us
    all_gather x1, blocking collectives, on_device(): every = lax.all_gather(conved, ('tm', 'space', 'chan'))  18.7 us
    all_to_all x1, waiting for transfers between devices, on_device(): parts = lax.all_to_all(parts, 'tm', split_axis=0, concat_axis=0, tiled=True)  5.94 us
    all_to_all x1, starting transfers between devices, on_device(): parts = lax.all_to_all(parts, 'tm', split_axis=0, concat_axis=0, tiled=True)  3.4 us
    conv_general_dilated x1, matrix products, on_device(): lax.conv_general_dilated(padded, conv_weight, (1, 1, 1), 'VALID', dimensi...  3.09 us
    all_gather x1, blocking collectives, on_device(): gain = lax.all_gather(gn_gain, 'chan', tiled=True)  1.81 us
    all_gather x1, blocking collectives, on_device(): shift = lax.all_gather(gn_shift, 'chan', tiled=True)  1.77 us
  transfers between devices with their start and end apart: 1, of which 1 were waited for; matrix products, arithmetic and copies ran while one was open for 0% of the time, Pallas kernels for 0%

profile of v1, /device:TPU:0, one launch (start us, length us, event | category | flops | bytes accessed | tf_op | source)
XLA Modules:
  0.0 66.1 jit_solution(5894749130049558942)
XLA Ops:
  0.0 0.0 copy-start
  0.0 24.9 %all-gather = bf16[32,2,2,8,256]{4,3,2,1,0:T(8,128)(2,1)S(1)} all-gather(bf16[2,2,2,8,256]{4,3,2,1,0:T(8,128)(2,1)} %param.7), channel_id=2, replica_groups=mesh['groups'=2,'tm'=4,'space'=2,'chan'=2] {'tm','space','chan'}, dimensions={0}, use_global_device_ids=true | all-gather | bytes 557056 | tf_op jit(solution)/shard_map/all_gather | solution.py:29
  24.9 0.1 copy.31
  25.1 0.1 pad_dynamic-slice_fusion.2
  25.2 0.1 pad_dynamic-slice_fusion.3
  25.3 0.2 pad_dynamic-slice_fusion.1
  25.5 0.1 copy.32
  25.6 0.0 copy-start.2
  25.6 0.0 copy-start.3
  25.6 3.1 %fusion.3 = f32[2,8,2,8,256]{4,0,3,2,1:T(2,128)S(1)} fusion(bf16[3,3,3,128,256]{4,3,2,1,0:T(8,128)(2,1)} %param.8, bf16[1,8,4,8,128]{4,0,3,2,1:T(2,128)(2,1)S(1)} %copy.32, bf16[1,8,4,8,128]{4,0,3,2,1:T(2,128)(2,1)S(1)} %pad_dynamic-slice_fusion.2), kind=kOutput, calls=%fused_computation.12 | convolution fusion | flops 363593728 | bytes 2162688 | tf_op jit(solution)/shard_map/conv_general_dilated | solution.py:55
  28.7 0.0 copy-start.1
  28.8 0.1 slice.50
  28.9 0.1 slice.48
  29.0 0.9 %copy_bitcast_fusion = f32[4,2,8,2,2,256]{5,1,4,3,2,0:T(2,128)} fusion(f32[1,6,2,4,2,256]{5,0,4,3,2,1:T(1,128)S(1)} %bitcast.48, f32[1,2,2,4,2,256]{5,0,4,3,2,1:T(1,128)S(1)} %bitcast.50, f32[1,8,2,4,2,256]{5,0,4,3,2,1:T(1,128)S(1)} %bitcast.47), kind=kLoop, calls=%fused_computation.11 | loop fusion | flops 131072 | bytes 524288 | tf_op jit(solution)/shard_map/transpose | solution.py:65
  29.9 3.4 %all-to-all-start = ((f32[4,2,8,2,2,256]{5,1,4,3,2,0:T(2,128)}), f32[4,2,8,2,2,256]{5,1,4,3,2,0:T(2,128)S(1)}, u32[]{:S(2)}, u32[]{:S(2)}) async-start(f32[4,2,8,2,2,256]{5,1,4,3,2,0:T(2,128)} %copy_bitcast_fusion), calls=%async_computation | async-start | bytes 524288 | tf_op jit(solution)/shard_map/all_to_all | solution.py:66
  33.3 0.0 copy-done.2
  33.3 1.8 %all-gather.1 = f32[2,1,256]{2,1,0:T(1,128)S(1)} all-gather(f32[1,1,256]{2,1,0:T(1,128)S(1)} %bitcast.54), channel_id=1, replica_groups=mesh['groups'=2,'tm'=4,'space'=2,'chan'=2] {'chan'}, dimensions={0}, use_global_device_ids=true | all-gather | bytes 3072 | tf_op jit(solution)/shard_map/all_gather | solution.py:75
  35.2 0.0 copy-done.3
  35.2 1.8 %all-gather.2 = f32[2,1,256]{2,1,0:T(1,128)S(1)} all-gather(f32[1,1,256]{2,1,0:T(1,128)S(1)} %bitcast.55), channel_id=1, replica_groups=mesh['groups'=2,'tm'=4,'space'=2,'chan'=2] {'chan'}, dimensions={0}, use_global_device_ids=true | all-gather | bytes 3072 | tf_op jit(solution)/shard_map/all_gather | solution.py:76
  36.9 0.1 broadcast_and_fusion
  37.0 5.9 %all-to-all-done = f32[4,2,8,2,2,256]{5,1,4,3,2,0:T(2,128)S(1)} async-done(((f32[4,2,8,2,2,256]{5,1,4,3,2,0:T(2,128)}), f32[4,2,8,2,2,256]{5,1,4,3,2,0:T(2,128)S(1)}, u32[]{:S(2)}, u32[]{:S(2)}) %all-to-all-start) | async-done | bytes 262176 | tf_op jit(solution)/shard_map/all_to_all | solution.py:66
  43.0 0.1 reduce_sum.32
  43.1 0.0 copy-done.1
  43.1 18.7 %all_gather.18 = bf16[16,2,8,2,2,256]{5,2,4,3,1,0:T(8,128)(2,1)S(1)} all-gather(bf16[1,2,8,2,2,256]{5,2,4,3,1,0:T(8,128)(2,1)S(1)} %fusion.7), channel_id=1, replica_groups=mesh['groups'=2,'tm'=4,'space'=2,'chan'=2] {'tm','space','chan'}, dimensions={0}, use_global_device_ids=true | all-gather | bytes 557056 | tf_op jit(solution)/shard_map/all_gather | solution.py:72
  61.8 0.2 convert_reduce_fusion
  62.0 0.5 copy.38
  62.5 0.3 reshape.106
  62.9 0.1 reduce_sum.49
  63.0 0.1 reduce_sum.50
  63.1 0.1 reduce_sum.46
  63.2 0.1 reduce_sum.47
  63.3 0.1 broadcast_in_dim.32
  63.3 0.1 sub.26
  63.4 0.1 broadcast_in_dim.33
  63.5 0.1 mul.42
  63.6 0.0 copy-start.4
  63.6 0.6 select_convert_fusion
  64.2 0.1 copy.41
  64.4 0.1 broadcast_in_dim.35
  64.4 0.1 broadcast_in_dim.36
  64.6 0.0 copy-done
  64.6 0.0 copy-done.4
  64.6 0.8 %fusion.1 = bf16[2,8,4,4,256]{4,1,0,3,2:T(8,128)(2,1)S(1)} fusion(bf16[3,3,512,256]{3,2,1,0:T(8,128)(2,1)S(1)} %copy-done, bf16[2,8,8,8,512]{4,1,0,3,2:T(8,128)(2,1)S(1)} %bitcast.45, f32[256]{0:T(256)S(1)} %copy-done.4), kind=kOutput, calls=%fused_computation.5 | convolution fusion | flops 604110848 | bytes 3081216 | tf_op jit(solution)/shard_map/conv_general_dilated | solution.py:111
  65.4 0.7 %copy.42 = bf16[2,8,4,4,256]{4,3,2,1,0:T(4,128)(2,1)} copy(bf16[2,8,4,4,256]{4,1,0,3,2:T(8,128)(2,1)S(1)} %fusion.1) | data formatting | bytes 262144 | tf_op jit(solution)/shard_map/reshape | solution.py:120
  (10 shorter events, 0.1 us)
Async XLA Ops:
  0.0 64.6 %copy-start = (bf16[3,3,512,256]{3,2,1,0:T(8,128)(2,1)S(1)}, bf16[3,3,512,256]{3,2,1,0:T(8,128)(2,1)}, u32[]{:S(2)}) copy-start(bf16[3,3,512,256]{3,2,1,0:T(8,128)(2,1)} %param.12) | copy-start | bytes 7077892
  25.6 7.7 %copy-start.2 = (f32[256]{0:T(256)S(1)}, f32[256]{0:T(256)}, u32[]{:S(2)}) copy-start(f32[256]{0:T(256)} %param.10) | copy-start | bytes 3076
  25.6 9.6 %copy-start.3 = (f32[256]{0:T(256)S(1)}, f32[256]{0:T(256)}, u32[]{:S(2)}) copy-start(f32[256]{0:T(256)} %param.11) | copy-start | bytes 3076
  28.7 14.4 %copy-start.1 = (f32[256]{0:T(256)S(1)}, f32[256]{0:T(256)}, u32[]{:S(2)}) copy-start(f32[256]{0:T(256)} %param.9) | copy-start | bytes 3076
  29.9 13.0 %all-to-all-start = ((f32[4,2,8,2,2,256]{5,1,4,3,2,0:T(2,128)}), f32[4,2,8,2,2,256]{5,1,4,3,2,0:T(2,128)S(1)}, u32[]{:S(2)}, u32[]{:S(2)}) async-start(f32[4,2,8,2,2,256]{5,1,4,3,2,0:T(2,128)} %copy_bitcast_fusion), calls=%async_computation | async-start | bytes 524288 | tf_op jit(solution)/shard_map/all_to_all | solution.py:66
  63.6 1.0 %copy-start.4 = (f32[256]{0:T(256)S(1)}, f32[256]{0:T(256)}, u32[]{:S(2)}) copy-start(f32[256]{0:T(256)} %param.13) | copy-start | bytes 3076

commit v2 on v1

--- a/solution.py
+++ b/solution.py
@@ -1,6 +1,9 @@
 import jax
 import jax.numpy as jnp
 from jax import lax
+from jax.experimental import pallas as pl
+from jax.experimental.pallas import tpu as pltpu
+from jax.sharding import Mesh
 from jax.sharding import PartitionSpec as P
 
 C = 512
@@ -43,7 +46,7 @@
     return jnp.stack([jnp.roll(mine[c], -c * span, axis=0) for c in range(clips)])
 
 
-def on_device(latents, conv_weight, conv_bias, gn_gain, gn_shift, up_weight, up_bias):
+def general_plan(latents, conv_weight, conv_bias, gn_gain, gn_shift, up_weight, up_bias):
     clips, span, rows, cols, half = latents.shape
     spans, spaces, chans = lax.axis_size("tm"), lax.axis_size("space"), lax.axis_size("chan")
     me, row_block = lax.axis_index("tm"), lax.axis_index("space")
@@ -120,10 +123,203 @@
     return output.reshape(clips, frames, 2 * rows, 2 * width, half)
 
 
+def conv_kernel(side_ref, latents_ref, weight_ref, sums_ref, taps):
+    spaces, his, los, clips, span, rows, cols, depth = latents_ref.shape
+    spans = his * los
+    frames = spans * span
+    side = side_ref[0]
+    block = rows * cols
+    lead = 2 * block
+    column = lax.broadcasted_iota(jnp.int32, (1, 1, cols, depth), 2)
+    for clip in range(clips):
+        taps[clip, :lead] = jnp.zeros((lead, taps.shape[2]), taps.dtype)
+        order = [(j + clip) % spans for j in range(spans)]
+
+        def taken(at, row):
+            parts = [latents_ref[at, j // los, j % los, clip, :, row] for j in order]
+            return jnp.concatenate(parts, axis=0).astype(jnp.float32)
+
+        above = jnp.where(side > 0, taken(1 - side, rows - 1), 0.0)
+        below = jnp.where(side > 0, 0.0, taken(1 - side, 0))
+        own = [taken(side, row) for row in range(rows)]
+        tall = jnp.stack([above] + own + [below], axis=1)
+        shifts = (
+            jnp.where(column > 0, pltpu.roll(tall, 1, 2), 0.0),
+            tall,
+            jnp.where(column < cols - 1, pltpu.roll(tall, cols - 1, 2), 0.0),
+        )
+        for e in range(3):
+            for b in range(3):
+                piece = shifts[e][:, b : b + rows].reshape(frames * block, depth)
+                at = (b * 3 + e) * depth
+                taps[clip, lead:, at : at + depth] = piece.astype(taps.dtype)
+    total = None
+    for a in range(3):
+        left = jnp.concatenate(
+            [taps[clip, a * block : a * block + frames * block] for clip in range(clips)], axis=0
+        )
+        right = weight_ref[a].reshape(9 * depth, weight_ref.shape[4])
+        part = jnp.dot(left, right, preferred_element_type=jnp.float32)
+        total = part if total is None else total + part
+    count = frames * block
+    width = sums_ref.shape[3]
+    for x in range(los):
+        for clip in range(clips):
+            piece = total[clip * count : (clip + 1) * count, x * width : (x + 1) * width]
+            sums_ref[x, clip] = piece.astype(sums_ref.dtype)
+
+
+def norm_kernel(side_ref, conv_ref, gain_ref, shift_ref, tiles_ref):
+    spaces, frames, rows, cols, depth = conv_ref.shape
+    owners, reach = tiles_ref.shape[0], tiles_ref.shape[1]
+    side = side_ref[0]
+    group = C // GROUPS
+    values = conv_ref[...].astype(jnp.float32)
+    flat = values.reshape(spaces * frames * rows * cols, depth)
+    sums = jnp.sum(flat, axis=0, keepdims=True)
+    squares = jnp.sum(flat * flat, axis=0, keepdims=True)
+    lane = lax.broadcasted_iota(jnp.int32, (depth, depth), 0) // group
+    other = lax.broadcasted_iota(jnp.int32, (depth, depth), 1) // group
+    same = (lane == other).astype(jnp.float32)
+    both = jnp.concatenate([sums, squares, jnp.zeros((6, depth), jnp.float32)], axis=0)
+    both = jnp.dot(both, same, precision=lax.Precision.HIGHEST, preferred_element_type=jnp.float32)
+    both = both / float(flat.shape[0] * group)
+    mean, square = both[0:1], both[1:2]
+    factor = lax.rsqrt(square - mean * mean + 1e-06)
+    normed = (flat - mean) * factor * gain_ref[...] + shift_ref[...]
+    active = (normed / (1.0 + jnp.exp(-normed))).reshape(values.shape)
+    cells = {}
+    for at in range(spaces):
+        for row in range(rows):
+            cells[at * rows + row] = jnp.swapaxes(active[at, :, row], 0, 1)
+    width = cols // owners
+    empty = jnp.zeros((frames, depth), jnp.float32)
+    for i in range(reach):
+        lower, upper = cells[i], cells[i + spaces * rows - reach]
+        chosen = jnp.where(side > 0, upper, lower)
+        for owner in range(owners):
+            picked = []
+            for j in range(owner * width - 1, (owner + 1) * width + 1):
+                picked.append(chosen[j] if 0 <= j < cols else empty)
+            tiles_ref[owner, i] = jnp.concatenate(picked, axis=0).astype(tiles_ref.dtype)
+
+
+def up_kernel(side_ref, tiles_ref, weight_ref, bias_ref, out_ref, cells):
+    chans, clips, los, reach, tall, depth = tiles_ref.shape
+    frames = out_ref.shape[1]
+    out_rows, out_cols = out_ref.shape[2], out_ref.shape[3]
+    wide = tall // frames
+    side = side_ref[0]
+    edge = jnp.where(side > 0, reach, 0)
+    cells[edge] = jnp.zeros(cells.shape[1:], cells.dtype)
+    for i in range(reach):
+        for j in range(wide):
+            parts = []
+            for chan in range(chans):
+                for x in range(los):
+                    stack = [
+                        tiles_ref[chan, clip, x, i, j * frames : (j + 1) * frames].astype(jnp.float32)
+                        for clip in range(clips)
+                    ]
+                    parts.append(jnp.concatenate(stack, axis=0))
+            cells[i + 1 - side, j] = jnp.concatenate(parts, axis=1).astype(cells.dtype)
+    total = None
+    for b in range(3):
+        for e in range(3):
+            left = jnp.concatenate(
+                [
+                    cells[(r - 1 + b) // 2 + 1, (q - 1 + e) // 2 + 1]
+                    for r in range(out_rows)
+                    for q in range(out_cols)
+                ],
+                axis=0,
+            )
+            part = jnp.dot(left, weight_ref[b, e], preferred_element_type=jnp.float32)
+            total = part if total is None else total + part
+    total = total + bias_ref[...]
+    total = total.reshape(out_rows * out_cols, clips, frames, total.shape[1])
+    span = frames // (clips * los)
+    for clip in range(clips):
+        turned = jnp.swapaxes(total[:, clip], 0, 1).astype(out_ref.dtype)
+        for k in range(frames):
+            slot = (k + clip * span) % frames
+            for r in range(out_rows):
+                out_ref[clip, slot, r] = turned[k, r * out_cols : (r + 1) * out_cols]
+
+
+def whole_vmem():
+    return pl.BlockSpec(memory_space=pltpu.VMEM)
+
+
+def in_smem():
+    return pl.BlockSpec(memory_space=pltpu.SMEM)
+
+
+def swap(value, axis):
+    return lax.all_to_all(value, axis, split_axis=0, concat_axis=0, tiled=True)
+
+
+def small_plan(latents, conv_weight, conv_bias, gn_gain, gn_shift, up_weight, up_bias):
+    clips, span, rows, cols, half = latents.shape
+    his, los = lax.axis_size("tm_hi"), lax.axis_size("tm_lo")
+    spaces, chans = lax.axis_size("space"), lax.axis_size("chan")
+    spans = his * los
+    frames, width, depth = span * spans, cols // spans, half // los
+    side = lax.axis_index("space").astype(jnp.int32).reshape(1)
+    x = lax.axis_index("tm_lo")
+
+    split = latents.reshape(clips, span, rows, cols, los, depth).transpose(4, 0, 1, 2, 3, 5)
+    both = lax.all_gather(split[None], "chan", axis=0, tiled=True)
+    both = swap(both, "tm_hi")
+    both = swap(both.swapaxes(0, 1), "tm_lo").swapaxes(0, 1)
+    every = lax.all_gather(both, "space")
+    sums = pl.pallas_call(
+        conv_kernel,
+        out_shape=jax.ShapeDtypeStruct((los, clips, frames * rows * cols, depth), jnp.float32),
+        in_specs=[in_smem(), whole_vmem(), whole_vmem()],
+        out_specs=whole_vmem(),
+        scratch_shapes=[pltpu.VMEM((clips, (frames + 2) * rows * cols, 9 * depth), jnp.bfloat16)],
+        compiler_params=pltpu.CompilerParams(vmem_limit_bytes=16 << 20),
+    )(side, every, conv_weight)
+    sums = jnp.sum(swap(sums, "tm_lo"), axis=0)
+    sums = jnp.sum(swap(sums, "tm_hi"), axis=0)
+
+    def block_of(vector):
+        return lax.dynamic_slice_in_dim(vector, x * depth, depth)[None]
+
+    conved = (sums + block_of(conv_bias)).astype(jnp.bfloat16)
+    conved = lax.all_gather(conved, "space").reshape(spaces, frames, rows, cols, depth)
+    tiles = pl.pallas_call(
+        norm_kernel,
+        out_shape=jax.ShapeDtypeStruct((spans, rows + 1, (width + 2) * frames, depth), jnp.bfloat16),
+        in_specs=[in_smem(), whole_vmem(), whole_vmem(), whole_vmem()],
+        out_specs=whole_vmem(),
+        compiler_params=pltpu.CompilerParams(vmem_limit_bytes=16 << 20),
+    )(side, conved, block_of(gn_gain), block_of(gn_shift))
+    tiles = tiles.reshape((his, los) + tiles.shape[1:])
+    tiles = swap(tiles, "tm_hi")
+    tiles = swap(tiles.swapaxes(0, 1), "tm_lo").swapaxes(0, 1)
+    tiles = lax.all_gather(tiles, "chan")
+    return pl.pallas_call(
+        up_kernel,
+        out_shape=jax.ShapeDtypeStruct((clips, frames, 2 * rows, 2 * width, half), jnp.bfloat16),
+        in_specs=[in_smem(), whole_vmem(), whole_vmem(), whole_vmem()],
+        out_specs=whole_vmem(),
+        scratch_shapes=[pltpu.VMEM((rows + 2, width + 2, clips * frames, C), jnp.bfloat16)],
+        compiler_params=pltpu.CompilerParams(vmem_limit_bytes=16 << 20),
+    )(side, tiles, up_weight, up_bias[None])
+
+
 def solution(mesh):
+    sizes = dict(mesh.shape)
+    small = sizes["tm"] == 4 and sizes["space"] == 2 and sizes["chan"] == 2
+    if small:
+        shape = (sizes["groups"], 2, 2, sizes["space"], sizes["chan"])
+        mesh = Mesh(mesh.devices.reshape(shape), ("groups", "tm_hi", "tm_lo", "space", "chan"))
+    tm = ("tm_hi", "tm_lo") if small else "tm"
     placed = (
-        P("groups", "tm", "space", None, "chan"),
-        P(None, None, None, "tm", "chan"),
+        P("groups", tm, "space", None, "chan"),
+        P(None, None, None, tm, "chan"),
         P("chan"),
         P("chan"),
         P("chan"),
@@ -131,9 +327,9 @@
         P("chan"),
     )
     return jax.shard_map(
-        on_device,
+        small_plan if small else general_plan,
         mesh=mesh,
         in_specs=placed,
-        out_specs=P("groups", None, "space", "tm", "chan"),
+        out_specs=P("groups", None, "space", tm, "chan"),
         check_vma=False,
     )

time: 66.3 us -> 68.3 us (1.030)
  matrix products: 3.87 us -> 0 us
  waiting for transfers between devices: 5.94 us -> 9.44 us
  starting transfers between devices: 3.4 us -> 6.68 us
  Pallas kernels: 0 us -> 2.43 us
  other arithmetic: 2.1 us -> 0.69 us
  blocking collectives: 47.2 us -> 46.2 us
  local copies, waits for them, and re-layouts: 3.29 us -> 2.31 us
    all_gather x4, blocking collectives: 47.2 us -> 14 us  [the longest x1 4.93 us: small_plan(): every = lax.all_gather(both, 'space')]
    all_to_all x0 -> x4, blocking collectives: none -> 32.2 us  [swap(): return lax.all_to_all(value, axis, split_axis=0, concat_axis=0, tiled=True)]
    conv_general_dilated x2 -> x0, matrix products: 3.87 us -> none  [the longest x1 3.09 us: on_device(): lax.conv_general_dilated(padded, conv_weight, (1, 1, 1), 'VALID', dimensi...]
    all_to_all x1 -> x2, waiting for transfers between devices: 5.94 us -> 9.44 us  [swap(): return lax.all_to_all(value, axis, split_axis=0, concat_axis=0, tiled=True)]
    all_to_all x1 -> x2, starting transfers between devices: 3.4 us -> 6.68 us  [swap(): return lax.all_to_all(value, axis, split_axis=0, concat_axis=0, tiled=True)]
    pallas_call x0 -> x3, Pallas kernels: none -> 2.43 us  [the longest x1 1.46 us: small_plan(): pl.pallas_call(up_kernel, out_shape=jax.ShapeDtypeStruct((clips, frames,...]
    unnamed x12, local copies, waits for them, and re-layouts: 0.04 us -> 1.49 us
    reshape x2 -> x0, local copies, waits for them, and re-layouts: 1.06 us -> none  [the longest x1 0.72 us: on_device(): return output.reshape(clips, frames, 2 * rows, 2 * width, half)]
  transfers between devices with their start and end apart: 1 -> 2, of which waited for: 1 -> 2; matrix products, arithmetic and copies ran while one was open for 0% -> 0% of each run, Pallas kernels for 0% -> 0%
where the time goes in v2:
time: 68.3 us; the launch traced here: 67.8 us
  blocking collectives  46.2 us (68%)
  waiting for transfers between devices  9.44 us (14%)
  starting transfers between devices  6.68 us (10%)
  Pallas kernels  2.43 us (4%)
  local copies, waits for them, and re-layouts  2.31 us (3%)
  other arithmetic  0.69 us (1%)
    all_to_all x4, blocking collectives, swap(): return lax.all_to_all(value, axis, split_axis=0, concat_axis=0, tiled=True)  32.2 us
    all_to_all x2, waiting for transfers between devices, swap(): return lax.all_to_all(value, axis, split_axis=0, concat_axis=0, tiled=True)  9.44 us
    all_to_all x2, starting transfers between devices, swap(): return lax.all_to_all(value, axis, split_axis=0, concat_axis=0, tiled=True)  6.68 us
    all_gather x1, blocking collectives, small_plan(): every = lax.all_gather(both, 'space')  4.93 us
    all_gather x1, blocking collectives, small_plan(): lax.all_gather(conved, 'space').reshape(spaces, frames, rows, cols, depth)  4.59 us
    all_gather x1, blocking collectives, small_plan(): both = lax.all_gather(split[None], 'chan', axis=0, tiled=True)  2.53 us
    all_gather x1, blocking collectives, small_plan(): tiles = lax.all_gather(tiles, 'chan')  1.95 us
    unnamed x12, local copies, waits for them, and re-layouts  1.49 us
  transfers between devices with their start and end apart: 2, of which 2 were waited for; matrix products, arithmetic and copies ran while one was open for 0% of the time, Pallas kernels for 0%

profile of v2, /device:TPU:0, one launch (start us, length us, event | category | flops | bytes accessed | tf_op | source)
XLA Modules:
  0.0 67.8 jit_solution(6771648120310450191)
XLA Ops:
  0.0 0.0 copy-start.5
  0.0 0.0 copy-start.3
  0.0 0.0 copy-start.4
  0.0 2.5 %all-gather = bf16[4,2,2,2,8,128]{5,4,0,3,2,1:T(8,128)(2,1)S(1)} all-gather(bf16[2,2,2,2,8,128]{5,4,0,3,2,1:T(8,128)(2,1)} %bitcast.32), channel_id=2, replica_groups=mesh['groups'=2,'tm_hi'=2,'tm_lo'=2,'space'=2,'chan'=2] {'chan'}, dimensions={0}, use_global_device_ids=true | all-gather | bytes 98304 | tf_op jit(solution)/shard_map/all_gather | solution.py:272
  2.5 10.3 %all_to_all.30 = bf16[2,2,2,2,2,8,128]{6,5,4,3,2,1,0:T(8,128)(2,1)S(1)} all-to-all(bf16[2,2,2,2,2,8,128]{6,5,4,3,2,1,0:T(8,128)(2,1)S(1)} %bitcast.30), channel_id=1, replica_groups=mesh['groups'=2,'tm_hi'=2,'tm_lo'=2,'space'=2,'chan'=2] {'tm_hi'}, dimensions={0} | all-to-all | bytes 131072 | tf_op jit(solution)/shard_map/all_to_all | solution.py:259
  12.8 0.6 copy.27
  13.5 3.3 %all-to-all-start.1 = ((bf16[2,2,2,2,2,8,128]{6,5,4,3,2,1,0:T(8,128)(2,1)}), bf16[2,2,2,2,2,8,128]{6,5,4,3,2,1,0:T(8,128)(2,1)S(1)}, u32[]{:S(2)}, u32[]{:S(2)}) async-start(bf16[2,2,2,2,2,8,128]{6,5,4,3,2,1,0:T(8,128)(2,1)} %copy.27), calls=%async_computation.1 | async-start | bytes 131072 | tf_op jit(solution)/shard_map/all_to_all | solution.py:259
  16.8 4.1 %all-to-all-done.1 = bf16[2,2,2,2,2,8,128]{6,5,4,3,2,1,0:T(8,128)(2,1)S(1)} async-done(((bf16[2,2,2,2,2,8,128]{6,5,4,3,2,1,0:T(8,128)(2,1)}), bf16[2,2,2,2,2,8,128]{6,5,4,3,2,1,0:T(8,128)(2,1)S(1)}, u32[]{:S(2)}, u32[]{:S(2)}) %all-to-all-start.1) | async-done | bytes 65568 | tf_op jit(solution)/shard_map/all_to_all | solution.py:259
  20.9 4.9 %all-gather.1 = bf16[4,2,2,2,2,8,128]{6,5,4,3,2,1,0:T(8,128)(2,1)S(1)} all-gather(bf16[2,2,2,2,2,8,128]{6,5,4,3,2,1,0:T(8,128)(2,1)S(1)} %copy.28), channel_id=3, replica_groups=mesh['groups'=2,'tm_hi'=2,'tm_lo'=2,'space'=2,'chan'=2] {'space'}, dimensions={0}, use_global_device_ids=true | all-gather | bytes 196608 | tf_op jit(solution)/shard_map/all_gather | solution.py:275
  25.8 0.0 copy-start.1
  25.8 1.5 %copy-done.1 = bf16[3,3,3,128,256]{4,3,2,1,0:T(8,128)(2,1)S(1)} copy-done((bf16[3,3,3,128,256]{4,3,2,1,0:T(8,128)(2,1)S(1)}, bf16[3,3,3,128,256]{4,3,2,1,0:T(8,128)(2,1)}, u32[]{:S(2)}) %copy-start.1) | copy-done | bytes 1769496
  27.3 0.0 copy-start
  27.3 0.0 copy-start.2
  27.3 0.7 %shard_map.73 = f32[2,2,128,128]{3,2,1,0:T(8,128)S(1)} custom-call(s32[1]{0:T(128)} %bitcast.side_ref, bf16[2,2,2,2,2,2,8,128]{7,6,5,4,3,2,1,0:T(8,128)(2,1)S(1)} %bitcast.23, bf16[3,3,3,128,256]{4,3,2,1,0:T(8,128)(2,1)S(1)} %copy-done.1), custom_call_target="tpu_custom_call" | custom-call | tf_op jit(solution)/shard_map/pallas_call | solution.py:276
  28.0 7.7 %all_to_all.31 = f32[2,2,128,128]{3,2,1,0:T(8,128)S(1)} all-to-all(f32[2,2,128,128]{3,2,1,0:T(8,128)S(1)} %shard_map.73), channel_id=1, replica_groups=mesh['groups'=2,'tm_hi'=2,'tm_lo'=2,'space'=2,'chan'=2] {'tm_lo'}, dimensions={0} | all-to-all | bytes 524288 | tf_op jit(solution)/shard_map/all_to_all | solution.py:259
  35.7 0.7 reduce_sum.20
  36.4 3.4 %all-to-all-start.3 = ((f32[2,128,128]{2,1,0:T(8,128)}), f32[2,128,128]{2,1,0:T(8,128)S(1)}, u32[]{:S(2)}, u32[]{:S(2)}) async-start(f32[2,128,128]{2,1,0:T(8,128)} %reduce_sum.20), calls=%async_computation.3 | async-start | bytes 262144 | tf_op jit(solution)/shard_map/all_to_all | solution.py:259
  39.8 0.0 copy-done.5
  39.8 0.1 dynamic_slice.9
  39.8 0.0 copy-done.3
  39.8 0.0 copy-done.4
  39.8 0.1 dynamic-slice_bitcast_fusion
  39.9 5.3 %all-to-all-done.3 = f32[2,128,128]{2,1,0:T(8,128)S(1)} async-done(((f32[2,128,128]{2,1,0:T(8,128)}), f32[2,128,128]{2,1,0:T(8,128)S(1)}, u32[]{:S(2)}, u32[]{:S(2)}) %all-to-all-start.3) | async-done | bytes 131104 | tf_op jit(solution)/shard_map/all_to_all | solution.py:259
  45.3 4.6 %all_gather.22 = bf16[2,128,128]{2,1,0:T(8,128)(2,1)S(1)} all-gather(bf16[1,128,128]{2,1,0:T(8,128)(2,1)S(1)} %fusion), channel_id=1, replica_groups=mesh['groups'=2,'tm_hi'=2,'tm_lo'=2,'space'=2,'chan'=2] {'space'}, dimensions={0}, use_global_device_ids=true | all-gather | bytes 98304 | tf_op jit(solution)/shard_map/all_gather | solution.py:291
  49.9 0.3 shard_map.74
  50.2 7.6 %all_to_all.32 = bf16[2,2,3,32,128]{4,3,2,1,0:T(8,128)(2,1)S(1)} all-to-all(bf16[2,2,3,32,128]{4,3,2,1,0:T(8,128)(2,1)S(1)} %bitcast.24), channel_id=1, replica_groups=mesh['groups'=2,'tm_hi'=2,'tm_lo'=2,'space'=2,'chan'=2] {'tm_hi'}, dimensions={0} | all-to-all | bytes 196608 | tf_op jit(solution)/shard_map/all_to_all | solution.py:259
  57.7 6.7 %all_to_all.33 = bf16[2,2,3,32,128]{4,3,2,1,0:T(8,128)(2,1)S(1)} all-to-all(bf16[2,2,3,32,128]{4,3,2,1,0:T(8,128)(2,1)S(1)} %copy.29), channel_id=1, replica_groups=mesh['groups'=2,'tm_hi'=2,'tm_lo'=2,'space'=2,'chan'=2] {'tm_lo'}, dimensions={0} | all-to-all | bytes 196608 | tf_op jit(solution)/shard_map/all_to_all | solution.py:259
  64.4 1.9 %all-gather.2 = bf16[4,2,3,32,128]{4,3,2,1,0:T(8,128)(2,1)S(1)} all-gather(bf16[2,2,3,32,128]{4,3,2,1,0:T(8,128)(2,1)S(1)} %copy.30), channel_id=4, replica_groups=mesh['groups'=2,'tm_hi'=2,'tm_lo'=2,'space'=2,'chan'=2] {'chan'}, dimensions={0}, use_global_device_ids=true | all-gather | bytes 294912 | tf_op jit(solution)/shard_map/all_gather | solution.py:302
  66.4 0.0 copy-done
  66.4 0.0 copy-done.2
  66.4 1.5 %shard_map.75 = bf16[2,8,4,4,256]{4,3,2,1,0:T(4,128)(2,1)} custom-call(s32[1]{0:T(128)} %bitcast.side_ref, bf16[2,2,2,3,32,128]{5,4,3,2,1,0:T(8,128)(2,1)S(1)} %bitcast.22, bf16[3,3,512,256]{3,2,1,0:T(8,128)(2,1)S(1)} %copy-done, f32[1,256]{1,0:T(1,128)S(1)} %bitcast.26), custom_call_target="tpu_custom_call" | custom-call | tf_op jit(solution)/shard_map/pallas_call | solution.py:303
  (6 shorter events, 0.1 us)
Async XLA Ops:
  0.0 39.8 %copy-start.5 = (f32[256]{0:T(256)S(1)}, f32[256]{0:T(256)}, u32[]{:S(2)}) copy-start(f32[256]{0:T(256)} %param.9) | copy-start | bytes 3076
  0.0 39.8 %copy-start.3 = (f32[256]{0:T(256)S(1)}, f32[256]{0:T(256)}, u32[]{:S(2)}) copy-start(f32[256]{0:T(256)} %param.11) | copy-start | bytes 3076
  0.0 39.8 %copy-start.4 = (f32[256]{0:T(256)S(1)}, f32[256]{0:T(256)}, u32[]{:S(2)}) copy-start(f32[256]{0:T(256)} %param.10) | copy-start | bytes 3076
  13.5 7.4 %all-to-all-start.1 = ((bf16[2,2,2,2,2,8,128]{6,5,4,3,2,1,0:T(8,128)(2,1)}), bf16[2,2,2,2,2,8,128]{6,5,4,3,2,1,0:T(8,128)(2,1)S(1)}, u32[]{:S(2)}, u32[]{:S(2)}) async-start(bf16[2,2,2,2,2,8,128]{6,5,4,3,2,1,0:T(8,128)(2,1)} %copy.27), calls=%async_computation.1 | async-start | bytes 131072 | tf_op jit(solution)/shard_map/all_to_all | solution.py:259
  25.8 1.5 %copy-start.1 = (bf16[3,3,3,128,256]{4,3,2,1,0:T(8,128)(2,1)S(1)}, bf16[3,3,3,128,256]{4,3,2,1,0:T(8,128)(2,1)}, u32[]{:S(2)}) copy-start(bf16[3,3,3,128,256]{4,3,2,1,0:T(8,128)(2,1)} %weight_ref.2) | copy-start | bytes 5308420
  27.3 39.1 %copy-start = (bf16[3,3,512,256]{3,2,1,0:T(8,128)(2,1)S(1)}, bf16[3,3,512,256]{3,2,1,0:T(8,128)(2,1)}, u32[]{:S(2)}) copy-start(bf16[3,3,512,256]{3,2,1,0:T(8,128)(2,1)} %weight_ref.3) | copy-start | bytes 7077892
  27.3 39.1 %copy-start.2 = (f32[256]{0:T(256)S(1)}, f32[256]{0:T(256)}, u32[]{:S(2)}) copy-start(f32[256]{0:T(256)} %param.13) | copy-start | bytes 3076
  36.4 8.9 %all-to-all-start.3 = ((f32[2,128,128]{2,1,0:T(8,128)}), f32[2,128,128]{2,1,0:T(8,128)S(1)}, u32[]{:S(2)}, u32[]{:S(2)}) async-start(f32[2,128,128]{2,1,0:T(8,128)} %reduce_sum.20), calls=%async_computation.3 | async-start | bytes 262144 | tf_op jit(solution)/shard_map/all_to_all | solution.py:259

commit v3 on v1

--- a/solution.py
+++ b/solution.py
@@ -1,6 +1,8 @@
 import jax
 import jax.numpy as jnp
 from jax import lax
+from jax.experimental import pallas as pl
+from jax.experimental.pallas import tpu as pltpu
 from jax.sharding import PartitionSpec as P
 
 C = 512
@@ -43,7 +45,7 @@
     return jnp.stack([jnp.roll(mine[c], -c * span, axis=0) for c in range(clips)])
 
 
-def on_device(latents, conv_weight, conv_bias, gn_gain, gn_shift, up_weight, up_bias):
+def general_plan(latents, conv_weight, conv_bias, gn_gain, gn_shift, up_weight, up_bias):
     clips, span, rows, cols, half = latents.shape
     spans, spaces, chans = lax.axis_size("tm"), lax.axis_size("space"), lax.axis_size("chan")
     me, row_block = lax.axis_index("tm"), lax.axis_index("space")
@@ -120,7 +122,260 @@
     return output.reshape(clips, frames, 2 * rows, 2 * width, half)
 
 
+def pack_kernel(place_ref, own_ref, other_ref, first_ref, second_ref):
+    tm, side = place_ref[0], place_ref[1]
+    depth = first_ref.shape[5]
+    upper = (tm // 2) > 0
+    for ref, at in ((own_ref, side), (other_ref, 1 - side)):
+        low, high = ref[..., :depth], ref[..., depth:]
+        first_ref[at] = jnp.where(upper, high, low)
+        second_ref[at] = jnp.where(upper, low, high)
+
+
+def conv_kernel(place_ref, *refs):
+    got, (weight_ref, keep_ref), sent = refs[:4], refs[4:6], refs[6:9]
+    latents, taps, tiles = refs[9:]
+    spans, spaces, clips, span, rows, cols, depth = latents.shape
+    frames, tall = spans * span, spaces * rows
+    tm, chan = place_ref[0], place_ref[2]
+    turn = 2 * (tm % 2) + chan
+    for m in range(spans):
+        latents[m ^ turn] = got[m][...].astype(jnp.float32)
+    block = tall * cols
+    lead = 2 * block
+    column = lax.broadcasted_iota(jnp.int32, (1, 1, cols, depth), 2)
+    empty = jnp.zeros((frames, cols, depth), jnp.float32)
+    for clip in range(clips):
+        taps[clip, :lead] = jnp.zeros((lead, taps.shape[2]), taps.dtype)
+        lines = [empty]
+        for at in range(spaces):
+            for row in range(rows):
+                parts = [latents[(j + clip) % spans, at, clip, :, row] for j in range(spans)]
+                lines.append(jnp.concatenate(parts, axis=0))
+        padded = jnp.stack(lines + [empty], axis=1)
+        shifts = (
+            jnp.where(column > 0, pltpu.roll(padded, 1, 2), 0.0),
+            padded,
+            jnp.where(column < cols - 1, pltpu.roll(padded, cols - 1, 2), 0.0),
+        )
+        for e in range(3):
+            for b in range(3):
+                piece = shifts[e][:, b : b + tall].reshape(frames * block, depth)
+                at = (b * 3 + e) * depth
+                taps[clip, lead:, at : at + depth] = piece.astype(taps.dtype)
+    count = frames * block
+    total = None
+    for a in range(3):
+        left = jnp.concatenate([taps[clip, a * block : a * block + count] for clip in range(clips)], axis=0)
+        right = weight_ref[a].reshape(9 * depth, weight_ref.shape[4])
+        part = jnp.dot(left, right, preferred_element_type=jnp.float32)
+        total = part if total is None else total + part
+    width = tiles.shape[2]
+    los = spans // clips
+    for clip in range(clips):
+        for x in range(los):
+            tiles[clip * los + x] = total[clip * count : (clip + 1) * count, x * width : (x + 1) * width]
+    keep_ref[...] = tiles[tm]
+    for m in range(1, spans):
+        sent[m - 1][...] = tiles[tm ^ m].astype(sent[m - 1].dtype)
+
+
+def norm_kernel(place_ref, *refs):
+    partial, (bias_ref, gain_ref, shift_ref), sent = refs[:4], refs[4:7], refs[7:11]
+    tiles = refs[11]
+    tm, side = place_ref[0], place_ref[1]
+    owners, reach, strip, depth = tiles.shape
+    cols = 8
+    frames = strip // (cols // owners + 2)
+    tall = partial[0].shape[0] // (frames * cols)
+    group = C // GROUPS
+    block = pl.ds(tm % bias_ref.shape[0], 1)
+    total = partial[0][...]
+    for ref in partial[1:]:
+        total = total + ref[...].astype(jnp.float32)
+    flat = (total + bias_ref[block, :]).astype(jnp.bfloat16).astype(jnp.float32)
+    sums = jnp.sum(flat, axis=0, keepdims=True)
+    squares = jnp.sum(flat * flat, axis=0, keepdims=True)
+    lane = lax.broadcasted_iota(jnp.int32, (depth, depth), 0) // group
+    other = lax.broadcasted_iota(jnp.int32, (depth, depth), 1) // group
+    same = (lane == other).astype(jnp.float32)
+    both = jnp.concatenate([sums, squares, jnp.zeros((6, depth), jnp.float32)], axis=0)
+    both = jnp.dot(both, same, precision=lax.Precision.HIGHEST, preferred_element_type=jnp.float32)
+    both = both / float(flat.shape[0] * group)
+    mean, square = both[0:1], both[1:2]
+    factor = lax.rsqrt(square - mean * mean + 1e-06)
+    normed = (flat - mean) * factor * gain_ref[block, :] + shift_ref[block, :]
+    active = (normed / (1.0 + jnp.exp(-normed))).reshape(frames, tall, cols, depth)
+    cells = [jnp.swapaxes(active[:, row], 0, 1) for row in range(tall)]
+    width = cols // owners
+    empty = jnp.zeros((frames, depth), jnp.float32)
+    for i in range(reach):
+        chosen = jnp.where(side > 0, cells[i + tall - reach], cells[i])
+        for owner in range(owners):
+            picked = []
+            for j in range(owner * width - 1, (owner + 1) * width + 1):
+                picked.append(chosen[j] if 0 <= j < cols else empty)
+            tiles[owner, i] = jnp.concatenate(picked, axis=0).astype(tiles.dtype)
+    for m in range(owners):
+        sent[m][...] = tiles[tm ^ m]
+
+
+def cells_kernel(place_ref, *refs):
+    got, cells_ref, tiles = refs[:4], refs[4], refs[5]
+    tm = place_ref[0]
+    for m in range(len(got)):
+        tiles[tm ^ m] = got[m][...].astype(jnp.float32)
+    reach, wide, tall, half = cells_ref.shape
+    depth = tiles.shape[3]
+    los = half // depth
+    clips = tiles.shape[0] // los
+    frames = tall // clips
+    for i in range(reach):
+        for j in range(wide):
+            for x in range(los):
+                stack = [tiles[clip * los + x, i, j * frames : (j + 1) * frames] for clip in range(clips)]
+                piece = jnp.concatenate(stack, axis=0).astype(cells_ref.dtype)
+                cells_ref[i, j, :, x * depth : (x + 1) * depth] = piece
+
+
+def taps_of(side, half, cells_ref, weight_ref, cells, out_rows, out_cols):
+    reach, width = cells_ref.shape[0], cells_ref.shape[3]
+    cells[jnp.where(side > 0, reach, 0)] = jnp.zeros(cells.shape[1:], cells.dtype)
+    for i in range(reach):
+        cells[i + 1 - side] = cells_ref[i]
+    rows = pl.ds(pl.multiple_of(half * width, width), width)
+    total = None
+    for b in range(3):
+        for e in range(3):
+            left = jnp.concatenate(
+                [
+                    cells[(r - 1 + b) // 2 + 1, (q - 1 + e) // 2 + 1]
+                    for r in range(out_rows)
+                    for q in range(out_cols)
+                ],
+                axis=0,
+            )
+            part = jnp.dot(left, weight_ref[b, e, rows, :], preferred_element_type=jnp.float32)
+            total = part if total is None else total + part
+    return total
+
+
+def near_kernel(place_ref, cells_ref, weight_ref, bias_ref, total_ref, cells):
+    tall = cells_ref.shape[2]
+    out_rows, out_cols = 2 * (cells_ref.shape[0] - 1), 2 * (cells_ref.shape[1] - 2)
+    total = taps_of(place_ref[1], place_ref[2], cells_ref, weight_ref, cells, out_rows, out_cols)
+    total_ref[...] = total + bias_ref[...]
+
+
+def far_kernel(place_ref, cells_ref, weight_ref, total_ref, out_ref, cells):
+    clips, frames, out_rows, out_cols, width = out_ref.shape
+    total = taps_of(place_ref[1], 1 - place_ref[2], cells_ref, weight_ref, cells, out_rows, out_cols)
+    total = (total + total_ref[...]).reshape(out_rows * out_cols, clips, frames, width)
+    span = frames // 4
+    for clip in range(clips):
+        turned = jnp.swapaxes(total[:, clip], 0, 1).astype(out_ref.dtype)
+        for k in range(frames):
+            slot = (k + clip * span) % frames
+            for r in range(out_rows):
+                out_ref[clip, slot, r] = turned[k, r * out_cols : (r + 1) * out_cols]
+
+
+def run(kernel, shapes, scratch, place, *operands, flops=0, moved=0):
+    several = isinstance(shapes, (list, tuple))
+    vmem = pl.BlockSpec(memory_space=pltpu.VMEM)
+    return pl.pallas_call(
+        kernel,
+        out_shape=shapes,
+        in_specs=[pl.BlockSpec(memory_space=pltpu.SMEM)] + [vmem] * len(operands),
+        out_specs=[vmem] * len(shapes) if several else vmem,
+        scratch_shapes=scratch,
+        compiler_params=pltpu.CompilerParams(vmem_limit_bytes=16 << 20),
+        cost_estimate=pl.CostEstimate(flops=flops, bytes_accessed=moved, transcendentals=0),
+    )(place, *operands)
+
+
+def small_plan(latents, conv_weight, conv_bias, gn_gain, gn_shift, up_weight, up_bias):
+    clips, span, rows, cols, half = latents.shape
+    spans, spaces, chans = lax.axis_size("tm"), lax.axis_size("space"), lax.axis_size("chan")
+    los = spans // clips
+    frames, tall, width, depth = span * spans, rows * spaces, cols // spans, half // los
+    place = jnp.stack([lax.axis_index(axis) for axis in ("tm", "space", "chan")]).astype(jnp.int32)
+    low, full = jnp.bfloat16, jnp.float32
+    shape = jax.ShapeDtypeStruct
+    flip = ((0, 1), (1, 0))
+
+    other = lax.ppermute(latents, "space", flip)
+    packed = shape((spaces,) + latents.shape[:4] + (depth,), low)
+    pair = run(pack_kernel, [packed, packed], [], place, latents, other, moved=1 << 17)
+    got = []
+    for m in range(spans):
+        pairs = []
+        for source in range(spans):
+            for chan in range(chans):
+                turned = source ^ m
+                target = 2 * chan + turned // 2
+                pairs.append((source * chans + chan, target * chans + turned % 2))
+        got.append(lax.ppermute(pair[m // 2], ("tm", "chan"), pairs))
+
+    count = frames * tall * cols
+    part = shape((count, depth), low)
+    partial = run(
+        conv_kernel,
+        [shape((count, depth), full)] + [part] * (spans - 1),
+        [
+            pltpu.VMEM((spans,) + packed.shape, full),
+            pltpu.VMEM((clips, count + 2 * tall * cols, 9 * depth), low),
+            pltpu.VMEM((spans, count, depth), full),
+        ],
+        place,
+        *got,
+        conv_weight,
+        flops=2 * clips * count * 27 * depth * half,
+        moved=3 << 20,
+    )
+    partial = [partial[0]] + [
+        lax.ppermute(partial[m], "tm", [(i, i ^ m) for i in range(spans)]) for m in range(1, spans)
+    ]
+
+    tile = shape((rows + 1, (width + 2) * frames, depth), low)
+    tiles = run(
+        norm_kernel,
+        [tile] * spans,
+        [pltpu.VMEM((spans,) + tile.shape, low)],
+        place,
+        *partial,
+        *(vector.reshape(los, depth) for vector in (conv_bias, gn_gain, gn_shift)),
+        moved=1 << 19,
+    )
+    tiles = [tiles[0]] + [
+        lax.ppermute(tiles[m], "tm", [(i, i ^ m) for i in range(spans)]) for m in range(1, spans)
+    ]
+
+    near = run(
+        cells_kernel,
+        shape((rows + 1, width + 2, clips * frames, half), low),
+        [pltpu.VMEM((spans,) + tile.shape, full)],
+        place,
+        *tiles,
+        moved=1 << 18,
+    )
+    far = lax.ppermute(near, "chan", flip)
+    cells = pltpu.VMEM((rows + 2,) + near.shape[1:], low)
+    outputs = clips * frames * 4 * rows * width
+    flops = 2 * outputs * 9 * half * half
+    total = run(
+        near_kernel, shape((outputs, half), full), [cells], place, near, up_weight, up_bias[None],
+        flops=flops, moved=2 << 20,
+    )
+    return run(
+        far_kernel, shape((clips, frames, 2 * rows, 2 * width, half), low), [cells], place, far, up_weight, total,
+        flops=flops, moved=2 << 20,
+    )
+
+
 def solution(mesh):
+    sizes = dict(mesh.shape)
+    small = sizes["tm"] == 4 and sizes["space"] == 2 and sizes["chan"] == 2
     placed = (
         P("groups", "tm", "space", None, "chan"),
         P(None, None, None, "tm", "chan"),
@@ -131,7 +386,7 @@
         P("chan"),
     )
     return jax.shard_map(
-        on_device,
+        small_plan if small else general_plan,
         mesh=mesh,
         in_specs=placed,
         out_specs=P("groups", None, "space", "tm", "chan"),

time: 66.3 us -> 43.6 us (0.66)
  blocking collectives: 47.2 us -> 0 us
  starting transfers between devices: 3.4 us -> 19.2 us
  waiting for transfers between devices: 5.94 us -> 15.1 us
  Pallas kernels: 0 us -> 6.52 us
  matrix products: 3.87 us -> 0 us
  other arithmetic: 2.1 us -> 0.08 us
  local copies, waits for them, and re-layouts: 3.29 us -> 2.25 us
    all_gather x4 -> x0, blocking collectives: 47.2 us -> none  [the longest x1 24.9 us: input_slice(): whole = lax.all_gather(latents, ('tm', 'space', 'chan'))]
    ppermute x0 -> x12, starting transfers between devices: none -> 19.2 us  [the longest x4 7.33 us: small_plan(): got.append(lax.ppermute(pair[m // 2], ('tm', 'chan'), pairs))]
    ppermute x0 -> x12, waiting for transfers between devices: none -> 15.1 us  [the longest x3 4.96 us: small_plan(): lax.ppermute(partial[m], 'tm', [(i, i ^ m) for i in range(spans)])]
    pallas_call x0 -> x6, Pallas kernels: none -> 6.52 us  [run(): pl.pallas_call(kernel, out_shape=shapes, in_specs=[pl.BlockSpec(memory_sp...]
    all_to_all x1 -> x0, waiting for transfers between devices: 5.94 us -> none  [on_device(): parts = lax.all_to_all(parts, 'tm', split_axis=0, concat_axis=0, tiled=True)]
    conv_general_dilated x2 -> x0, matrix products: 3.87 us -> none  [the longest x1 3.09 us: on_device(): lax.conv_general_dilated(padded, conv_weight, (1, 1, 1), 'VALID', dimensi...]
    all_to_all x1 -> x0, starting transfers between devices: 3.4 us -> none  [on_device(): parts = lax.all_to_all(parts, 'tm', split_axis=0, concat_axis=0, tiled=True)]
    unnamed x12 -> x14, local copies, waits for them, and re-layouts: 0.04 us -> 2.25 us
  transfers between devices with their start and end apart: 1 -> 12, of which waited for: 1 -> 9; matrix products, arithmetic and copies ran while one was open for 0% -> 0% of each run, Pallas kernels for 0% -> 2%
where the time goes in v3:
time: 43.6 us; the launch traced here: 43.4 us
  starting transfers between devices  19.2 us (44%)
  waiting for transfers between devices  15.1 us (35%)
  Pallas kernels  6.52 us (15%)
  local copies, waits for them, and re-layouts  2.25 us (5%)
    ppermute x4, starting transfers between devices, small_plan(): got.append(lax.ppermute(pair[m // 2], ('tm', 'chan'), pairs))  7.33 us
    pallas_call x6, Pallas kernels, run(): pl.pallas_call(kernel, out_shape=shapes, in_specs=[pl.BlockSpec(memory_sp...  6.52 us
    ppermute x3, waiting for transfers between devices, small_plan(): lax.ppermute(partial[m], 'tm', [(i, i ^ m) for i in range(spans)])  4.96 us
    ppermute x4, waiting for transfers between devices, small_plan(): got.append(lax.ppermute(pair[m // 2], ('tm', 'chan'), pairs))  4.85 us
    ppermute x3, starting transfers between devices, small_plan(): lax.ppermute(tiles[m], 'tm', [(i, i ^ m) for i in range(spans)])  4.45 us
    ppermute x3, starting transfers between devices, small_plan(): lax.ppermute(partial[m], 'tm', [(i, i ^ m) for i in range(spans)])  4.44 us
    ppermute x3, waiting for transfers between devices, small_plan(): lax.ppermute(tiles[m], 'tm', [(i, i ^ m) for i in range(spans)])  3.05 us
    ppermute x1, starting transfers between devices, small_plan(): other = lax.ppermute(latents, 'space', flip)  2.94 us
  transfers between devices with their start and end apart: 12, of which 9 were waited for; matrix products, arithmetic and copies ran while one was open for 0% of the time, Pallas kernels for 2%

profile of v3, /device:TPU:0, one launch (start us, length us, event | category | flops | bytes accessed | tf_op | source)
XLA Modules:
  0.0 43.4 jit_solution(16252734640260175590)
XLA Ops:
  0.0 0.0 copy-start
  0.0 2.9 %collective-permute-start = (bf16[2,2,2,8,256]{4,3,2,1,0:T(8,128)(2,1)}, bf16[2,2,2,8,256]{4,3,2,1,0:T(8,128)(2,1)S(1)}, u32[]{:S(2)}, u32[]{:S(2)}) collective-permute-start(bf16[2,2,2,8,256]{4,3,2,1,0:T(8,128)(2,1)} %own_ref.1), channel_id=1, source_target_pairs={{0,2},{2,0},{1,3},{3,1},{4,6},{6,4},{5,7},{7,5},{8,10},{10,8},{9,1... | collective-permute-start | bytes 98312 | tf_op jit(solution)/shard_map/ppermute | solution.py:307
  2.9 0.1 pad_add_fusion.place_ref
  3.0 2.0 %collective-permute-done.other_ref = bf16[2,2,2,8,256]{4,3,2,1,0:T(8,128)(2,1)S(1)} collective-permute-done((bf16[2,2,2,8,256]{4,3,2,1,0:T(8,128)(2,1)}, bf16[2,2,2,8,256]{4,3,2,1,0:T(8,128)(2,1)S(1)}, u32[]{:S(2)}, u32[]{:S(2)}) %collective-permute-start) | collective-permute-done | bytes 32800 | tf_op jit(solution)/shard_map/ppermute | solution.py:307
  5.0 0.0 copy-start.1
  5.0 0.8 %copy-done.1 = bf16[2,2,2,8,256]{4,3,2,1,0:T(8,128)(2,1)S(1)} copy-done((bf16[2,2,2,8,256]{4,3,2,1,0:T(8,128)(2,1)S(1)}, bf16[2,2,2,8,256]{4,3,2,1,0:T(8,128)(2,1)}, u32[]{:S(2)}) %copy-start.1) | copy-done | bytes 32792
  5.8 0.0 copy-start.3
  5.8 0.0 copy-start.4
  5.8 0.0 copy-start.5
  5.8 0.0 copy-start.2
  5.8 0.6 %shard_map.73 = (bf16[2,2,2,2,8,128]{5,4,3,2,1,0:T(8,128)(2,1)S(1)}, bf16[2,2,2,2,8,128]{5,4,3,2,1,0:T(8,128)(2,1)S(1)}) custom-call(s32[3]{0:T(128)S(1)} %pad_add_fusion.place_ref, bf16[2,2,2,8,256]{4,3,2,1,0:T(8,128)(2,1)S(1)} %copy-done.1, bf16[2,2,2,8,256]{4,3,2,1,0:T(8,128)(2,1)S(1)} %collective-permute-done.other_ref), custom_call_target="tpu_custom_call" | custom-call | bytes 131072 | tf_op jit(solution)/shard_map/pallas_call | solution.py:286
  6.4 0.1 collective-permute-start.2
  6.5 0.7 %collective-permute-start.1 = (bf16[2,2,2,2,8,128]{5,4,3,2,1,0:T(8,128)(2,1)S(1)}, bf16[2,2,2,2,8,128]{5,4,3,2,1,0:T(8,128)(2,1)S(1)}, u32[]{:S(2)}, u32[]{:S(2)}) collective-permute-start(bf16[2,2,2,2,8,128]{5,4,3,2,1,0:T(8,128)(2,1)S(1)} %get-tuple-element.15), channel_id=1, source_target_pairs={{0,0},{1,8},{4,1},{5,9},{8,4},{9,12},{12,5},{13,13},{2,2},{3,10},{... | collective-permute-start | bytes 98312 | tf_op jit(solution)/shard_map/ppermute | solution.py:318
  7.1 6.5 %collective-permute-start.4 = (bf16[2,2,2,2,8,128]{5,4,3,2,1,0:T(8,128)(2,1)S(1)}, bf16[2,2,2,2,8,128]{5,4,3,2,1,0:T(8,128)(2,1)S(1)}, u32[]{:S(2)}, u32[]{:S(2)}) collective-permute-start(bf16[2,2,2,2,8,128]{5,4,3,2,1,0:T(8,128)(2,1)S(1)} %get-tuple-element.16), channel_id=1, source_target_pairs={{0,5},{1,13},{4,4},{5,12},{8,1},{9,9},{12,0},{13,8},{2,7},{3,15},{... | collective-permute-start | bytes 98312 | tf_op jit(solution)/shard_map/ppermute | solution.py:318
  13.7 0.1 collective-permute-start.3
  13.8 0.0 collective-permute-done.2.refs_1_
  13.8 0.0 collective-permute-done.1.refs_0_
  13.8 4.2 %collective-permute-done.4.refs_3_ = bf16[2,2,2,2,8,128]{5,4,3,2,1,0:T(8,128)(2,1)S(1)} collective-permute-done((bf16[2,2,2,2,8,128]{5,4,3,2,1,0:T(8,128)(2,1)S(1)}, bf16[2,2,2,2,8,128]{5,4,3,2,1,0:T(8,128)(2,1)S(1)}, u32[]{:S(2)}, u32[]{:S(2)}) %collective-permute-start.4) | collective-permute-done | bytes 32800 | tf_op jit(solution)/shard_map/ppermute | solution.py:318
  17.9 0.7 %collective-permute-done.3.refs_2_ = bf16[2,2,2,2,8,128]{5,4,3,2,1,0:T(8,128)(2,1)S(1)} collective-permute-done((bf16[2,2,2,2,8,128]{5,4,3,2,1,0:T(8,128)(2,1)S(1)}, bf16[2,2,2,2,8,128]{5,4,3,2,1,0:T(8,128)(2,1)S(1)}, u32[]{:S(2)}, u32[]{:S(2)}) %collective-permute-start.3) | collective-permute-done | bytes 32800 | tf_op jit(solution)/shard_map/ppermute | solution.py:318
  18.6 0.0 copy-start.6
  18.6 1.5 %copy-done.6 = bf16[3,3,3,128,256]{4,3,2,1,0:T(8,128)(2,1)S(1)} copy-done((bf16[3,3,3,128,256]{4,3,2,1,0:T(8,128)(2,1)S(1)}, bf16[3,3,3,128,256]{4,3,2,1,0:T(8,128)(2,1)}, u32[]{:S(2)}) %copy-start.6) | copy-done | bytes 1769496
  20.1 1.8 %shard_map.74 = (f32[256,128]{1,0:T(8,128)S(1)}, bf16[256,128]{1,0:T(8,128)(2,1)S(1)}, bf16[256,128]{1,0:T(8,128)(2,1)S(1)}, bf16[256,128]{1,0:T(8,128)(2,1)S(1)}) custom-call(s32[3]{0:T(128)S(1)} %pad_add_fusion.place_ref, bf16[2,2,2,2,8,128]{5,4,3,2,1,0:T(8,128)(2,1)S(1)} %collective-permute-done.1.refs_0_, ...), custom_call_target="tpu_custom_call" | custom-call | flops 905969664 | bytes 3145728 | tf_op jit(solution)/shard_map/pallas_call | solution.py:286
  21.9 0.1 collective-permute-start.5
  22.0 3.2 %collective-permute-start.6 = (bf16[256,128]{1,0:T(8,128)(2,1)S(1)}, bf16[256,128]{1,0:T(8,128)(2,1)S(1)}, u32[]{:S(2)}, u32[]{:S(2)}) collective-permute-start(bf16[256,128]{1,0:T(8,128)(2,1)S(1)} %get-tuple-element.19), channel_id=1, source_target_pairs={{0,8},{4,12},{8,0},{12,4},{1,9},{5,13},{9,1},{13,5},{2,10},{6,14},... | collective-permute-start | bytes 196616 | tf_op jit(solution)/shard_map/ppermute | solution.py:337
  25.1 1.2 %collective-permute-start.7 = (bf16[256,128]{1,0:T(8,128)(2,1)S(1)}, bf16[256,128]{1,0:T(8,128)(2,1)S(1)}, u32[]{:S(2)}, u32[]{:S(2)}) collective-permute-start(bf16[256,128]{1,0:T(8,128)(2,1)S(1)} %get-tuple-element.20), channel_id=1, source_target_pairs={{0,12},{4,8},{8,4},{12,0},{1,13},{5,9},{9,5},{13,1},{2,14},{6,10},... | collective-permute-start | bytes 196616 | tf_op jit(solution)/shard_map/ppermute | solution.py:337
  26.3 0.7 %collective-permute-done.5.refs_1_ = bf16[256,128]{1,0:T(8,128)(2,1)S(1)} collective-permute-done((bf16[256,128]{1,0:T(8,128)(2,1)S(1)}, bf16[256,128]{1,0:T(8,128)(2,1)S(1)}, u32[]{:S(2)}, u32[]{:S(2)}) %collective-permute-start.5) | collective-permute-done | bytes 65568 | tf_op jit(solution)/shard_map/ppermute | solution.py:337
  27.0 2.9 %collective-permute-done.6.refs_2_ = bf16[256,128]{1,0:T(8,128)(2,1)S(1)} collective-permute-done((bf16[256,128]{1,0:T(8,128)(2,1)S(1)}, bf16[256,128]{1,0:T(8,128)(2,1)S(1)}, u32[]{:S(2)}, u32[]{:S(2)}) %collective-permute-start.6) | collective-permute-done | bytes 65568 | tf_op jit(solution)/shard_map/ppermute | solution.py:337
  29.9 1.4 %collective-permute-done.7.refs_3_ = bf16[256,128]{1,0:T(8,128)(2,1)S(1)} collective-permute-done((bf16[256,128]{1,0:T(8,128)(2,1)S(1)}, bf16[256,128]{1,0:T(8,128)(2,1)S(1)}, u32[]{:S(2)}, u32[]{:S(2)}) %collective-permute-start.7) | collective-permute-done | bytes 65568 | tf_op jit(solution)/shard_map/ppermute | solution.py:337
  31.3 0.0 copy-done.3
  31.3 0.0 copy-done.4
  31.3 0.0 copy-done.5
  31.3 0.9 %shard_map.75 = (bf16[3,32,128]{2,1,0:T(8,128)(2,1)S(1)}, bf16[3,32,128]{2,1,0:T(8,128)(2,1)S(1)}, bf16[3,32,128]{2,1,0:T(8,128)(2,1)S(1)}, bf16[3,32,128]{2,1,0:T(8,128)(2,1)S(1)}) custom-call(s32[3]{0:T(128)S(1)} %pad_add_fusion.place_ref, f32[256,128]{1,0:T(8,128)S(1)} %get-tuple-element.17.refs_0_, bf16[256,128]{1,0:T(8,128)(2,1)S(1)} %collective-permute-done.5.refs_1_, ...), custom_call_target="tpu_custom_call" | custom-call | bytes 524288 | tf_op jit(solution)/shard_map/pallas_call | solution.py:286
  32.2 0.6 %collective-permute-start.8 = (bf16[3,32,128]{2,1,0:T(8,128)(2,1)S(1)}, bf16[3,32,128]{2,1,0:T(8,128)(2,1)S(1)}, u32[]{:S(2)}, u32[]{:S(2)}) collective-permute-start(bf16[3,32,128]{2,1,0:T(8,128)(2,1)S(1)} %get-tuple-element.22), channel_id=1, source_target_pairs={{0,4},{4,0},{8,12},{12,8},{1,5},{5,1},{9,13},{13,9},{2,6},{6,2},{1... | collective-permute-start | bytes 73736 | tf_op jit(solution)/shard_map/ppermute | solution.py:351
  32.8 1.3 %collective-permute-start.9 = (bf16[3,32,128]{2,1,0:T(8,128)(2,1)S(1)}, bf16[3,32,128]{2,1,0:T(8,128)(2,1)S(1)}, u32[]{:S(2)}, u32[]{:S(2)}) collective-permute-start(bf16[3,32,128]{2,1,0:T(8,128)(2,1)S(1)} %get-tuple-element.23), channel_id=1, source_target_pairs={{0,8},{4,12},{8,0},{12,4},{1,9},{5,13},{9,1},{13,5},{2,10},{6,14},... | collective-permute-start | bytes 73736 | tf_op jit(solution)/shard_map/ppermute | solution.py:351
  34.1 2.6 %collective-permute-start.10 = (bf16[3,32,128]{2,1,0:T(8,128)(2,1)S(1)}, bf16[3,32,128]{2,1,0:T(8,128)(2,1)S(1)}, u32[]{:S(2)}, u32[]{:S(2)}) collective-permute-start(bf16[3,32,128]{2,1,0:T(8,128)(2,1)S(1)} %get-tuple-element.24), channel_id=1, source_target_pairs={{0,12},{4,8},{8,4},{12,0},{1,13},{5,9},{9,5},{13,1},{2,14},{6,10},... | collective-permute-start | bytes 73736 | tf_op jit(solution)/shard_map/ppermute | solution.py:351
  36.7 0.0 collective-permute-done.8.refs_1_
  36.7 0.9 %collective-permute-done.9.refs_2_ = bf16[3,32,128]{2,1,0:T(8,128)(2,1)S(1)} collective-permute-done((bf16[3,32,128]{2,1,0:T(8,128)(2,1)S(1)}, bf16[3,32,128]{2,1,0:T(8,128)(2,1)S(1)}, u32[]{:S(2)}, u32[]{:S(2)}) %collective-permute-start.9) | collective-permute-done | bytes 24608 | tf_op jit(solution)/shard_map/ppermute | solution.py:351
  37.5 2.2 %collective-permute-done.10.refs_3_ = bf16[3,32,128]{2,1,0:T(8,128)(2,1)S(1)} collective-permute-done((bf16[3,32,128]{2,1,0:T(8,128)(2,1)S(1)}, bf16[3,32,128]{2,1,0:T(8,128)(2,1)S(1)}, u32[]{:S(2)}, u32[]{:S(2)}) %collective-permute-start.10) | collective-permute-done | bytes 24608 | tf_op jit(solution)/shard_map/ppermute | solution.py:351
  39.7 0.6 %shard_map.76.cells_ref = bf16[3,4,16,256]{3,2,1,0:T(8,128)(2,1)S(1)} custom-call(s32[3]{0:T(128)S(1)} %pad_add_fusion.place_ref, bf16[3,32,128]{2,1,0:T(8,128)(2,1)S(1)} %get-tuple-element.21.refs_0_, bf16[3,32,128]{2,1,0:T(8,128)(2,1)S(1)} %collective-permute-done.8.refs_1_, bf16[3,32,128]{2,1,0:T(8,128)(2,1)S(1)} %collective-permute-done.9.refs_2_, ...), custom_call_target="tpu_custom_call" | custom-call | bytes 262144 | tf_op jit(solution)/shard_map/pallas_call | solution.py:286
  40.3 0.1 collective-permute-start.11
  40.4 0.0 copy-done
  40.4 0.0 copy-done.2
  40.4 1.0 %shard_map.77.total_ref = f32[256,256]{1,0:T(8,128)S(1)} custom-call(s32[3]{0:T(128)S(1)} %pad_add_fusion.place_ref, bf16[3,4,16,256]{3,2,1,0:T(8,128)(2,1)S(1)} %shard_map.76.cells_ref, bf16[3,3,512,256]{3,2,1,0:T(8,128)(2,1)S(1)} %copy-done, f32[1,256]{1,0:T(1,128)S(1)} %bitcast.7), custom_call_target="tpu_custom_call" | custom-call | flops 301989888 | bytes 2097152 | tf_op jit(solution)/shard_map/pallas_call | solution.py:286
  41.4 0.2 collective-permute-done.11.cells_ref
  41.6 1.7 %shard_map.78 = bf16[2,8,4,4,256]{4,3,2,1,0:T(4,128)(2,1)} custom-call(s32[3]{0:T(128)S(1)} %pad_add_fusion.place_ref, bf16[3,4,16,256]{3,2,1,0:T(8,128)(2,1)S(1)} %collective-permute-done.11.cells_ref, bf16[3,3,512,256]{3,2,1,0:T(8,128)(2,1)S(1)} %copy-done, f32[256,256]{1,0:T(8,128)S(1)} %shard_map.77.total_ref), custom_call_target="tpu_custom_call" | custom-call | flops 301989888 | bytes 2097152 | tf_op jit(solution)/shard_map/pallas_call | solution.py:286
Async XLA Ops:
  0.0 40.4 %copy-start = (bf16[3,3,512,256]{3,2,1,0:T(8,128)(2,1)S(1)}, bf16[3,3,512,256]{3,2,1,0:T(8,128)(2,1)}, u32[]{:S(2)}) copy-start(bf16[3,3,512,256]{3,2,1,0:T(8,128)(2,1)} %weight_ref.3) | copy-start | bytes 7077892
  0.0 5.0 %collective-permute-start = (bf16[2,2,2,8,256]{4,3,2,1,0:T(8,128)(2,1)}, bf16[2,2,2,8,256]{4,3,2,1,0:T(8,128)(2,1)S(1)}, u32[]{:S(2)}, u32[]{:S(2)}) collective-permute-start(bf16[2,2,2,8,256]{4,3,2,1,0:T(8,128)(2,1)} %own_ref.1), channel_id=1, source_target_pairs={{0,2},{2,0},{1,3},{3,1},{4,6},{6,4},{5,7},{7,5},{8,10},{10,8},{9,1... | collective-permute-start | bytes 98312 | tf_op jit(solution)/shard_map/ppermute | solution.py:307
  5.0 0.8 %copy-start.1 = (bf16[2,2,2,8,256]{4,3,2,1,0:T(8,128)(2,1)S(1)}, bf16[2,2,2,8,256]{4,3,2,1,0:T(8,128)(2,1)}, u32[]{:S(2)}) copy-start(bf16[2,2,2,8,256]{4,3,2,1,0:T(8,128)(2,1)} %own_ref.1) | copy-start | bytes 98308
  5.8 25.5 %copy-start.3 = (f32[256]{0:T(256)S(1)}, f32[256]{0:T(256)}, u32[]{:S(2)}) copy-start(f32[256]{0:T(256)} %param.9) | copy-start | bytes 3076
  5.8 25.5 %copy-start.4 = (f32[256]{0:T(256)S(1)}, f32[256]{0:T(256)}, u32[]{:S(2)}) copy-start(f32[256]{0:T(256)} %param.10) | copy-start | bytes 3076
  5.8 25.5 %copy-start.5 = (f32[256]{0:T(256)S(1)}, f32[256]{0:T(256)}, u32[]{:S(2)}) copy-start(f32[256]{0:T(256)} %param.11) | copy-start | bytes 3076
  5.8 34.6 %copy-start.2 = (f32[256]{0:T(256)S(1)}, f32[256]{0:T(256)}, u32[]{:S(2)}) copy-start(f32[256]{0:T(256)} %param.13) | copy-start | bytes 3076
  6.4 7.4 %collective-permute-start.2 = (bf16[2,2,2,2,8,128]{5,4,3,2,1,0:T(8,128)(2,1)S(1)}, bf16[2,2,2,2,8,128]{5,4,3,2,1,0:T(8,128)(2,1)S(1)}, u32[]{:S(2)}, u32[]{:S(2)}) collective-permute-start(bf16[2,2,2,2,8,128]{5,4,3,2,1,0:T(8,128)(2,1)S(1)} %get-tuple-element.15), channel_id=1, source_target_pairs={{0,1},{1,9},{4,0},{5,8},{8,5},{9,13},{12,4},{13,12},{2,3},{3,11},{... | collective-permute-start | bytes 98312 | tf_op jit(solution)/shard_map/ppermute | solution.py:318
  6.5 7.3 %collective-permute-start.1 = (bf16[2,2,2,2,8,128]{5,4,3,2,1,0:T(8,128)(2,1)S(1)}, bf16[2,2,2,2,8,128]{5,4,3,2,1,0:T(8,128)(2,1)S(1)}, u32[]{:S(2)}, u32[]{:S(2)}) collective-permute-start(bf16[2,2,2,2,8,128]{5,4,3,2,1,0:T(8,128)(2,1)S(1)} %get-tuple-element.15), channel_id=1, source_target_pairs={{0,0},{1,8},{4,1},{5,9},{8,4},{9,12},{12,5},{13,13},{2,2},{3,10},{... | collective-permute-start | bytes 98312 | tf_op jit(solution)/shard_map/ppermute | solution.py:318
  7.1 10.8 %collective-permute-start.4 = (bf16[2,2,2,2,8,128]{5,4,3,2,1,0:T(8,128)(2,1)S(1)}, bf16[2,2,2,2,8,128]{5,4,3,2,1,0:T(8,128)(2,1)S(1)}, u32[]{:S(2)}, u32[]{:S(2)}) collective-permute-start(bf16[2,2,2,2,8,128]{5,4,3,2,1,0:T(8,128)(2,1)S(1)} %get-tuple-element.16), channel_id=1, source_target_pairs={{0,5},{1,13},{4,4},{5,12},{8,1},{9,9},{12,0},{13,8},{2,7},{3,15},{... | collective-permute-start | bytes 98312 | tf_op jit(solution)/shard_map/ppermute | solution.py:318
  13.7 4.9 %collective-permute-start.3 = (bf16[2,2,2,2,8,128]{5,4,3,2,1,0:T(8,128)(2,1)S(1)}, bf16[2,2,2,2,8,128]{5,4,3,2,1,0:T(8,128)(2,1)S(1)}, u32[]{:S(2)}, u32[]{:S(2)}) collective-permute-start(bf16[2,2,2,2,8,128]{5,4,3,2,1,0:T(8,128)(2,1)S(1)} %get-tuple-element.16), channel_id=1, source_target_pairs={{0,4},{1,12},{4,5},{5,13},{8,0},{9,8},{12,1},{13,9},{2,6},{3,14},{... | collective-permute-start | bytes 98312 | tf_op jit(solution)/shard_map/ppermute | solution.py:318
  18.6 1.5 %copy-start.6 = (bf16[3,3,3,128,256]{4,3,2,1,0:T(8,128)(2,1)S(1)}, bf16[3,3,3,128,256]{4,3,2,1,0:T(8,128)(2,1)}, u32[]{:S(2)}) copy-start(bf16[3,3,3,128,256]{4,3,2,1,0:T(8,128)(2,1)} %refs_4_.1) | copy-start | bytes 5308420
  21.9 5.1 %collective-permute-start.5 = (bf16[256,128]{1,0:T(8,128)(2,1)S(1)}, bf16[256,128]{1,0:T(8,128)(2,1)S(1)}, u32[]{:S(2)}, u32[]{:S(2)}) collective-permute-start(bf16[256,128]{1,0:T(8,128)(2,1)S(1)} %get-tuple-element.18), channel_id=1, source_target_pairs={{0,4},{4,0},{8,12},{12,8},{1,5},{5,1},{9,13},{13,9},{2,6},{6,2},{1... | collective-permute-start | bytes 196616 | tf_op jit(solution)/shard_map/ppermute | solution.py:337
  22.0 7.9 %collective-permute-start.6 = (bf16[256,128]{1,0:T(8,128)(2,1)S(1)}, bf16[256,128]{1,0:T(8,128)(2,1)S(1)}, u32[]{:S(2)}, u32[]{:S(2)}) collective-permute-start(bf16[256,128]{1,0:T(8,128)(2,1)S(1)} %get-tuple-element.19), channel_id=1, source_target_pairs={{0,8},{4,12},{8,0},{12,4},{1,9},{5,13},{9,1},{13,5},{2,10},{6,14},... | collective-permute-start | bytes 196616 | tf_op jit(solution)/shard_map/ppermute | solution.py:337
  25.1 6.2 %collective-permute-start.7 = (bf16[256,128]{1,0:T(8,128)(2,1)S(1)}, bf16[256,128]{1,0:T(8,128)(2,1)S(1)}, u32[]{:S(2)}, u32[]{:S(2)}) collective-permute-start(bf16[256,128]{1,0:T(8,128)(2,1)S(1)} %get-tuple-element.20), channel_id=1, source_target_pairs={{0,12},{4,8},{8,4},{12,0},{1,13},{5,9},{9,5},{13,1},{2,14},{6,10},... | collective-permute-start | bytes 196616 | tf_op jit(solution)/shard_map/ppermute | solution.py:337
  32.2 4.5 %collective-permute-start.8 = (bf16[3,32,128]{2,1,0:T(8,128)(2,1)S(1)}, bf16[3,32,128]{2,1,0:T(8,128)(2,1)S(1)}, u32[]{:S(2)}, u32[]{:S(2)}) collective-permute-start(bf16[3,32,128]{2,1,0:T(8,128)(2,1)S(1)} %get-tuple-element.22), channel_id=1, source_target_pairs={{0,4},{4,0},{8,12},{12,8},{1,5},{5,1},{9,13},{13,9},{2,6},{6,2},{1... | collective-permute-start | bytes 73736 | tf_op jit(solution)/shard_map/ppermute | solution.py:351
  32.8 4.7 %collective-permute-start.9 = (bf16[3,32,128]{2,1,0:T(8,128)(2,1)S(1)}, bf16[3,32,128]{2,1,0:T(8,128)(2,1)S(1)}, u32[]{:S(2)}, u32[]{:S(2)}) collective-permute-start(bf16[3,32,128]{2,1,0:T(8,128)(2,1)S(1)} %get-tuple-element.23), channel_id=1, source_target_pairs={{0,8},{4,12},{8,0},{12,4},{1,9},{5,13},{9,1},{13,5},{2,10},{6,14},... | collective-permute-start | bytes 73736 | tf_op jit(solution)/shard_map/ppermute | solution.py:351
  34.1 5.6 %collective-permute-start.10 = (bf16[3,32,128]{2,1,0:T(8,128)(2,1)S(1)}, bf16[3,32,128]{2,1,0:T(8,128)(2,1)S(1)}, u32[]{:S(2)}, u32[]{:S(2)}) collective-permute-start(bf16[3,32,128]{2,1,0:T(8,128)(2,1)S(1)} %get-tuple-element.24), channel_id=1, source_target_pairs={{0,12},{4,8},{8,4},{12,0},{1,13},{5,9},{9,5},{13,1},{2,14},{6,10},... | collective-permute-start | bytes 73736 | tf_op jit(solution)/shard_map/ppermute | solution.py:351
  40.3 1.4 %collective-permute-start.11 = (bf16[3,4,16,256]{3,2,1,0:T(8,128)(2,1)S(1)}, bf16[3,4,16,256]{3,2,1,0:T(8,128)(2,1)S(1)}, u32[]{:S(2)}, u32[]{:S(2)}) collective-permute-start(bf16[3,4,16,256]{3,2,1,0:T(8,128)(2,1)S(1)} %shard_map.76.cells_ref), channel_id=1, source_target_pairs={{0,1},{1,0},{2,3},{3,2},{4,5},{5,4},{6,7},{7,6},{8,9},{9,8},{10,11... | collective-permute-start | bytes 294920 | tf_op jit(solution)/shard_map/ppermute | solution.py:362

commit v4 on v3

--- a/solution.py
+++ b/solution.py
@@ -122,68 +122,78 @@
     return output.reshape(clips, frames, 2 * rows, 2 * width, half)
 
 
-def pack_kernel(place_ref, own_ref, other_ref, first_ref, second_ref):
-    tm, side = place_ref[0], place_ref[1]
-    depth = first_ref.shape[5]
-    upper = (tm // 2) > 0
+def placed_at():
+    return lax.axis_index("tm"), lax.axis_index("space"), lax.axis_index("chan")
+
+
+def fetch_kernel(latents_ref, weight_ref, token_ref):
+    depth = token_ref.shape[1]
+    token_ref[...] = latents_ref[:16, :depth] + weight_ref[0, 0, 0, :16, :depth]
+
+
+def pack_kernel(own_ref, other_ref, token_ref, first_ref, second_ref):
+    del token_ref
+    tm, side, chan = placed_at()
+    depth = first_ref.shape[2]
+    home = (chan == tm // 2).astype(jnp.int32)
+    upper = ((tm % 2) ^ home) > 0
     for ref, at in ((own_ref, side), (other_ref, 1 - side)):
-        low, high = ref[..., :depth], ref[..., depth:]
+        low, high = ref[:, :depth], ref[:, depth:]
         first_ref[at] = jnp.where(upper, high, low)
         second_ref[at] = jnp.where(upper, low, high)
 
 
-def conv_kernel(place_ref, *refs):
-    got, (weight_ref, keep_ref), sent = refs[:4], refs[4:6], refs[6:9]
-    latents, taps, tiles = refs[9:]
+def conv_kernel(own_ref, other_ref, weight_ref, keep_ref, *refs):
+    sent, (latents, taps, tiles) = refs[:3], refs[3:]
     spans, spaces, clips, span, rows, cols, depth = latents.shape
     frames, tall = spans * span, spaces * rows
-    tm, chan = place_ref[0], place_ref[2]
-    turn = 2 * (tm % 2) + chan
-    for m in range(spans):
-        latents[m ^ turn] = got[m][...].astype(jnp.float32)
-    block = tall * cols
-    lead = 2 * block
-    column = lax.broadcasted_iota(jnp.int32, (1, 1, cols, depth), 2)
-    empty = jnp.zeros((frames, cols, depth), jnp.float32)
-    for clip in range(clips):
-        taps[clip, :lead] = jnp.zeros((lead, taps.shape[2]), taps.dtype)
-        lines = [empty]
-        for at in range(spaces):
-            for row in range(rows):
+    tm, _, chan = placed_at()
+    home = chan == tm // 2
+    near, far = jnp.where(home, 0, 2), jnp.where(home, 2, 0)
+    for ref, turn in ((own_ref, near), (other_ref, far)):
+        first = jnp.where(turn > 0, tm ^ 2, tm ^ 1)
+        second = jnp.where(turn > 0, tm ^ 3, tm)
+        latents[first] = ref[0].astype(jnp.float32).reshape(latents.shape[1:])
+        latents[second] = ref[1].astype(jnp.float32).reshape(latents.shape[1:])
+    column = lax.broadcasted_iota(jnp.int32, (1, cols, depth), 1)
+    taps[0] = jnp.zeros(taps.shape[1:], taps.dtype)
+    taps[tall + 1] = jnp.zeros(taps.shape[1:], taps.dtype)
+    for at in range(spaces):
+        for row in range(rows):
+            line = at * rows + row + 1
+            taps[line, :2] = jnp.zeros((2,) + taps.shape[2:], taps.dtype)
+            shifts = [[], [], []]
+            for clip in range(clips):
                 parts = [latents[(j + clip) % spans, at, clip, :, row] for j in range(spans)]
-                lines.append(jnp.concatenate(parts, axis=0))
-        padded = jnp.stack(lines + [empty], axis=1)
-        shifts = (
-            jnp.where(column > 0, pltpu.roll(padded, 1, 2), 0.0),
-            padded,
-            jnp.where(column < cols - 1, pltpu.roll(padded, cols - 1, 2), 0.0),
-        )
-        for e in range(3):
-            for b in range(3):
-                piece = shifts[e][:, b : b + tall].reshape(frames * block, depth)
-                at = (b * 3 + e) * depth
-                taps[clip, lead:, at : at + depth] = piece.astype(taps.dtype)
-    count = frames * block
+                value = jnp.concatenate(parts, axis=0)
+                shifts[0].append(jnp.where(column > 0, pltpu.roll(value, 1, 1), 0.0))
+                shifts[1].append(value)
+                shifts[2].append(jnp.where(column < cols - 1, pltpu.roll(value, cols - 1, 1), 0.0))
+            for e in range(3):
+                piece = jnp.concatenate(shifts[e], axis=1).astype(taps.dtype)
+                taps[line, 2:, :, e * depth : (e + 1) * depth] = piece
+    count = frames * tall * cols
     total = None
     for a in range(3):
-        left = jnp.concatenate([taps[clip, a * block : a * block + count] for clip in range(clips)], axis=0)
+        lines = [taps[b : b + tall, a : a + frames].reshape(clips * count, 3 * depth) for b in range(3)]
         right = weight_ref[a].reshape(9 * depth, weight_ref.shape[4])
-        part = jnp.dot(left, right, preferred_element_type=jnp.float32)
+        part = jnp.dot(jnp.concatenate(lines, axis=1), right, preferred_element_type=jnp.float32)
         total = part if total is None else total + part
     width = tiles.shape[2]
     los = spans // clips
+    total = total.reshape(tall * frames, clips, cols, total.shape[1])
     for clip in range(clips):
         for x in range(los):
-            tiles[clip * los + x] = total[clip * count : (clip + 1) * count, x * width : (x + 1) * width]
+            tiles[clip * los + x] = total[:, clip, :, x * width : (x + 1) * width].reshape(count, width)
     keep_ref[...] = tiles[tm]
     for m in range(1, spans):
         sent[m - 1][...] = tiles[tm ^ m].astype(sent[m - 1].dtype)
 
 
-def norm_kernel(place_ref, *refs):
+def norm_kernel(*refs):
     partial, (bias_ref, gain_ref, shift_ref), sent = refs[:4], refs[4:7], refs[7:11]
     tiles = refs[11]
-    tm, side = place_ref[0], place_ref[1]
+    tm, side, _ = placed_at()
     owners, reach, strip, depth = tiles.shape
     cols = 8
     frames = strip // (cols // owners + 2)
@@ -205,8 +215,8 @@
     mean, square = both[0:1], both[1:2]
     factor = lax.rsqrt(square - mean * mean + 1e-06)
     normed = (flat - mean) * factor * gain_ref[block, :] + shift_ref[block, :]
-    active = (normed / (1.0 + jnp.exp(-normed))).reshape(frames, tall, cols, depth)
-    cells = [jnp.swapaxes(active[:, row], 0, 1) for row in range(tall)]
+    active = (normed / (1.0 + jnp.exp(-normed))).reshape(tall, frames, cols, depth)
+    cells = [jnp.swapaxes(active[row], 0, 1) for row in range(tall)]
     width = cols // owners
     empty = jnp.zeros((frames, depth), jnp.float32)
     for i in range(reach):
@@ -220,9 +230,9 @@
         sent[m][...] = tiles[tm ^ m]
 
 
-def cells_kernel(place_ref, *refs):
+def cells_kernel(*refs):
     got, cells_ref, tiles = refs[:4], refs[4], refs[5]
-    tm = place_ref[0]
+    tm, _, _ = placed_at()
     for m in range(len(got)):
         tiles[tm ^ m] = got[m][...].astype(jnp.float32)
     reach, wide, tall, half = cells_ref.shape
@@ -246,30 +256,31 @@
     rows = pl.ds(pl.multiple_of(half * width, width), width)
     total = None
     for b in range(3):
+        lines = []
         for e in range(3):
-            left = jnp.concatenate(
-                [
-                    cells[(r - 1 + b) // 2 + 1, (q - 1 + e) // 2 + 1]
-                    for r in range(out_rows)
-                    for q in range(out_cols)
-                ],
-                axis=0,
-            )
-            part = jnp.dot(left, weight_ref[b, e, rows, :], preferred_element_type=jnp.float32)
-            total = part if total is None else total + part
+            pieces = [
+                cells[(r - 1 + b) // 2 + 1, (q - 1 + e) // 2 + 1]
+                for r in range(out_rows)
+                for q in range(out_cols)
+            ]
+            lines.append(jnp.concatenate(pieces, axis=0))
+        right = jnp.concatenate([weight_ref[b, e, rows, :] for e in range(3)], axis=0)
+        part = jnp.dot(jnp.concatenate(lines, axis=1), right, preferred_element_type=jnp.float32)
+        total = part if total is None else total + part
     return total
 
 
-def near_kernel(place_ref, cells_ref, weight_ref, bias_ref, total_ref, cells):
-    tall = cells_ref.shape[2]
+def near_kernel(cells_ref, weight_ref, bias_ref, total_ref, cells):
+    _, side, chan = placed_at()
     out_rows, out_cols = 2 * (cells_ref.shape[0] - 1), 2 * (cells_ref.shape[1] - 2)
-    total = taps_of(place_ref[1], place_ref[2], cells_ref, weight_ref, cells, out_rows, out_cols)
+    total = taps_of(side, chan, cells_ref, weight_ref, cells, out_rows, out_cols)
     total_ref[...] = total + bias_ref[...]
 
 
-def far_kernel(place_ref, cells_ref, weight_ref, total_ref, out_ref, cells):
+def far_kernel(cells_ref, weight_ref, total_ref, out_ref, cells):
+    _, side, chan = placed_at()
     clips, frames, out_rows, out_cols, width = out_ref.shape
-    total = taps_of(place_ref[1], 1 - place_ref[2], cells_ref, weight_ref, cells, out_rows, out_cols)
+    total = taps_of(side, 1 - chan, cells_ref, weight_ref, cells, out_rows, out_cols)
     total = (total + total_ref[...]).reshape(out_rows * out_cols, clips, frames, width)
     span = frames // 4
     for clip in range(clips):
@@ -280,18 +291,18 @@
                 out_ref[clip, slot, r] = turned[k, r * out_cols : (r + 1) * out_cols]
 
 
-def run(kernel, shapes, scratch, place, *operands, flops=0, moved=0):
+def run(kernel, shapes, scratch, *operands, flops=0, moved=0):
     several = isinstance(shapes, (list, tuple))
     vmem = pl.BlockSpec(memory_space=pltpu.VMEM)
     return pl.pallas_call(
         kernel,
         out_shape=shapes,
-        in_specs=[pl.BlockSpec(memory_space=pltpu.SMEM)] + [vmem] * len(operands),
+        in_specs=[vmem] * len(operands),
         out_specs=[vmem] * len(shapes) if several else vmem,
         scratch_shapes=scratch,
         compiler_params=pltpu.CompilerParams(vmem_limit_bytes=16 << 20),
         cost_estimate=pl.CostEstimate(flops=flops, bytes_accessed=moved, transcendentals=0),
-    )(place, *operands)
+    )(*operands)
 
 
 def small_plan(latents, conv_weight, conv_bias, gn_gain, gn_shift, up_weight, up_bias):
@@ -299,23 +310,34 @@
     spans, spaces, chans = lax.axis_size("tm"), lax.axis_size("space"), lax.axis_size("chan")
     los = spans // clips
     frames, tall, width, depth = span * spans, rows * spaces, cols // spans, half // los
-    place = jnp.stack([lax.axis_index(axis) for axis in ("tm", "space", "chan")]).astype(jnp.int32)
     low, full = jnp.bfloat16, jnp.float32
     shape = jax.ShapeDtypeStruct
     flip = ((0, 1), (1, 0))
 
-    other = lax.ppermute(latents, "space", flip)
-    packed = shape((spaces,) + latents.shape[:4] + (depth,), low)
-    pair = run(pack_kernel, [packed, packed], [], place, latents, other, moved=1 << 17)
+    cells_in = latents.reshape(clips * span * rows * cols, half)
+    other = lax.ppermute(cells_in, "space", flip)
+    token = run(
+        fetch_kernel,
+        shape((16, depth), low),
+        [],
+        cells_in,
+        conv_weight,
+        moved=4 << 20,
+    )
+    packed = shape((spaces, cells_in.shape[0], depth), low)
+    pair = run(pack_kernel, [packed, packed], [], cells_in, other, token, moved=1 << 17)
+    turns = ((1, 2), (0, 3))
     got = []
-    for m in range(spans):
+    for block, (at_home, across) in zip(pair, turns):
         pairs = []
         for source in range(spans):
             for chan in range(chans):
-                turned = source ^ m
-                target = 2 * chan + turned // 2
-                pairs.append((source * chans + chan, target * chans + turned % 2))
-        got.append(lax.ppermute(pair[m // 2], ("tm", "chan"), pairs))
+                home = chan == source // 2
+                target = (source ^ at_home, chan) if home else (source ^ across, 1 - chan)
+                pairs.append((source * chans + chan, target[0] * chans + target[1]))
+        got.append(lax.ppermute(block, ("tm", "chan"), pairs))
+    got = jnp.stack(got)
+    core = lax.ppermute(got, "chan", flip)
 
     count = frames * tall * cols
     part = shape((count, depth), low)
@@ -323,12 +345,12 @@
         conv_kernel,
         [shape((count, depth), full)] + [part] * (spans - 1),
         [
-            pltpu.VMEM((spans,) + packed.shape, full),
-            pltpu.VMEM((clips, count + 2 * tall * cols, 9 * depth), low),
+            pltpu.VMEM((spans, spaces, clips, span, rows, cols, depth), full),
+            pltpu.VMEM((tall + 2, frames + 2, clips * cols, 3 * depth), low),
             pltpu.VMEM((spans, count, depth), full),
         ],
-        place,
-        *got,
+        got,
+        core,
         conv_weight,
         flops=2 * clips * count * 27 * depth * half,
         moved=3 << 20,
@@ -342,7 +364,6 @@
         norm_kernel,
         [tile] * spans,
         [pltpu.VMEM((spans,) + tile.shape, low)],
-        place,
         *partial,
         *(vector.reshape(los, depth) for vector in (conv_bias, gn_gain, gn_shift)),
         moved=1 << 19,
@@ -355,7 +376,6 @@
         cells_kernel,
         shape((rows + 1, width + 2, clips * frames, half), low),
         [pltpu.VMEM((spans,) + tile.shape, full)],
-        place,
         *tiles,
         moved=1 << 18,
     )
@@ -364,11 +384,11 @@
     outputs = clips * frames * 4 * rows * width
     flops = 2 * outputs * 9 * half * half
     total = run(
-        near_kernel, shape((outputs, half), full), [cells], place, near, up_weight, up_bias[None],
+        near_kernel, shape((outputs, half), full), [cells], near, up_weight, up_bias[None],
         flops=flops, moved=2 << 20,
     )
     return run(
-        far_kernel, shape((clips, frames, 2 * rows, 2 * width, half), low), [cells], place, far, up_weight, total,
+        far_kernel, shape((clips, frames, 2 * rows, 2 * width, half), low), [cells], far, up_weight, total,
         flops=flops, moved=2 << 20,
     )
 

time: 43.6 us -> 39.1 us (0.90)
  waiting for transfers between devices: 15.1 us -> 10.9 us
  Pallas kernels: 6.52 us -> 3.29 us
  starting transfers between devices: 19.2 us -> 20.7 us
  local copies, waits for them, and re-layouts: 2.25 us -> 3.73 us
    ppermute x5 -> x4, waiting for transfers between devices: 6.88 us -> 2.25 us  [the longest x2 1.35 us: small_plan(): got.append(lax.ppermute(block, ('tm', 'chan'), pairs))]
    pallas_call x6 -> x7, Pallas kernels: 6.52 us -> 3.29 us  [run(): pl.pallas_call(kernel, out_shape=shapes, in_specs=[vmem] * len(operands),...]
    ppermute x5 -> x4, starting transfers between devices: 10.3 us -> 11.8 us  [the longest x1 6.2 us: small_plan(): core = lax.ppermute(got, 'chan', flip)]
    unnamed x14 -> x16, local copies, waits for them, and re-layouts: 2.25 us -> 3.73 us
    ppermute x3, waiting for transfers between devices: 4.96 us -> 4.31 us  [small_plan(): lax.ppermute(partial[m], 'tm', [(i, i ^ m) for i in range(spans)])]
    ppermute x3, waiting for transfers between devices: 3.05 us -> 3.6 us  [small_plan(): lax.ppermute(tiles[m], 'tm', [(i, i ^ m) for i in range(spans)])]
    ppermute x1, waiting for transfers between devices: 0.24 us -> 0.78 us  [small_plan(): far = lax.ppermute(near, 'chan', flip)]
  transfers between devices with their start and end apart: 12 -> 11, of which waited for: 9 -> 7; matrix products, arithmetic and copies ran while one was open for 0% -> 0% of each run, Pallas kernels for 2% -> 1%
where the time goes in v4:
time: 39.1 us; the launch traced here: 38.9 us
  starting transfers between devices  20.7 us (53%)
  waiting for transfers between devices  10.9 us (28%)
  local copies, waits for them, and re-layouts  3.73 us (10%)
  Pallas kernels  3.29 us (8%)
    ppermute x1, starting transfers between devices, small_plan(): core = lax.ppermute(got, 'chan', flip)  6.2 us
    ppermute x3, starting transfers between devices, small_plan(): lax.ppermute(partial[m], 'tm', [(i, i ^ m) for i in range(spans)])  4.46 us
    ppermute x3, starting transfers between devices, small_plan(): lax.ppermute(tiles[m], 'tm', [(i, i ^ m) for i in range(spans)])  4.45 us
    ppermute x3, waiting for transfers between devices, small_plan(): lax.ppermute(partial[m], 'tm', [(i, i ^ m) for i in range(spans)])  4.31 us
    unnamed x16, local copies, waits for them, and re-layouts  3.73 us
    ppermute x3, waiting for transfers between devices, small_plan(): lax.ppermute(tiles[m], 'tm', [(i, i ^ m) for i in range(spans)])  3.6 us
    pallas_call x7, Pallas kernels, run(): pl.pallas_call(kernel, out_shape=shapes, in_specs=[vmem] * len(operands),...  3.29 us
    ppermute x1, starting transfers between devices, small_plan(): other = lax.ppermute(cells_in, 'space', flip)  2.94 us
  transfers between devices with their start and end apart: 11, of which 7 were waited for; matrix products, arithmetic and copies ran while one was open for 0% of the time, Pallas kernels for 1%

profile of v4, /device:TPU:0, one launch (start us, length us, event | category | flops | bytes accessed | tf_op | source)
XLA Modules:
  0.0 38.9 jit_solution(11924614595227558872)
XLA Ops:
  0.0 2.9 %collective-permute-start = (bf16[64,256]{1,0:T(8,128)(2,1)}, bf16[64,256]{1,0:T(8,128)(2,1)S(1)}, u32[]{:S(2)}, u32[]{:S(2)}) collective-permute-start(bf16[64,256]{1,0:T(8,128)(2,1)} %bitcast.7), channel_id=1, source_target_pairs={{0,2},{2,0},{1,3},{3,1},{4,6},{6,4},{5,7},{7,5},{8,10},{10,8},{9,1... | collective-permute-start | bytes 98312 | tf_op jit(solution)/shard_map/ppermute | solution.py:318
  2.9 0.0 copy-start.1
  2.9 1.5 %copy-done.1 = bf16[3,3,3,128,256]{4,3,2,1,0:T(8,128)(2,1)S(1)} copy-done((bf16[3,3,3,128,256]{4,3,2,1,0:T(8,128)(2,1)S(1)}, bf16[3,3,3,128,256]{4,3,2,1,0:T(8,128)(2,1)}, u32[]{:S(2)}) %copy-start.1) | copy-done | bytes 1769496
  4.4 0.0 copy-start.3
  4.4 0.8 %copy-done.3 = bf16[2,2,2,8,256]{4,3,2,1,0:T(8,128)(2,1)S(1)} copy-done((bf16[2,2,2,8,256]{4,3,2,1,0:T(8,128)(2,1)S(1)}, bf16[2,2,2,8,256]{4,3,2,1,0:T(8,128)(2,1)}, u32[]{:S(2)}) %copy-start.3) | copy-done | bytes 32792
  5.2 0.0 copy-start.5
  5.2 0.0 copy-start.6
  5.2 0.0 copy-start.7
  5.2 0.0 copy-start.4
  5.2 0.0 copy-start
  5.2 0.0 collective-permute-done.other_ref
  5.3 2.0 %collective-permute-start.1 = (bf16[2,64,128]{2,1,0:T(8,128)(2,1)S(1)}, bf16[2,64,128]{2,1,0:T(8,128)(2,1)S(1)}, u32[]{:S(2)}, u32[]{:S(2)}) collective-permute-start(bf16[2,64,128]{2,1,0:T(8,128)(2,1)S(1)} %get-tuple-element.15), channel_id=1, source_target_pairs={{0,4},{1,8},{4,0},{5,12},{8,1},{9,13},{12,5},{13,9},{2,6},{3,10},{... | collective-permute-start | bytes 98312 | tf_op jit(solution)/shard_map/ppermute | solution.py:338
  7.2 0.7 %collective-permute-start.2 = (bf16[2,64,128]{2,1,0:T(8,128)(2,1)S(1)}, bf16[2,64,128]{2,1,0:T(8,128)(2,1)S(1)}, u32[]{:S(2)}, u32[]{:S(2)}) collective-permute-start(bf16[2,64,128]{2,1,0:T(8,128)(2,1)S(1)} %get-tuple-element.16), channel_id=1, source_target_pairs={{0,0},{1,12},{4,4},{5,8},{8,5},{9,9},{12,1},{13,13},{2,2},{3,14},{... | collective-permute-start | bytes 98312 | tf_op jit(solution)/shard_map/ppermute | solution.py:338
  7.9 1.3 %collective-permute-done.1 = bf16[2,64,128]{2,1,0:T(8,128)(2,1)S(1)} collective-permute-done((bf16[2,64,128]{2,1,0:T(8,128)(2,1)S(1)}, bf16[2,64,128]{2,1,0:T(8,128)(2,1)S(1)}, u32[]{:S(2)}, u32[]{:S(2)}) %collective-permute-start.1) | collective-permute-done | bytes 32800 | tf_op jit(solution)/shard_map/ppermute | solution.py:338
  9.2 0.0 collective-permute-done.2
  9.3 6.2 %collective-permute-start.3 = (bf16[2,2,64,128]{3,2,1,0:T(8,128)(2,1)S(1)}, bf16[2,2,64,128]{3,2,1,0:T(8,128)(2,1)S(1)}, u32[]{:S(2)}, u32[]{:S(2)}) collective-permute-start(bf16[2,2,64,128]{3,2,1,0:T(8,128)(2,1)S(1)} %pad_maximum_fusion.own_ref), channel_id=1, source_target_pairs={{0,1},{1,0},{2,3},{3,2},{4,5},{5,4},{6,7},{7,6},{8,9},{9,8},{10,11... | collective-permute-start | bytes 196616 | tf_op jit(solution)/shard_map/ppermute | solution.py:340
  15.5 0.9 %collective-permute-done.3.other_ref = bf16[2,2,64,128]{3,2,1,0:T(8,128)(2,1)S(1)} collective-permute-done((bf16[2,2,64,128]{3,2,1,0:T(8,128)(2,1)S(1)}, bf16[2,2,64,128]{3,2,1,0:T(8,128)(2,1)S(1)}, u32[]{:S(2)}, u32[]{:S(2)}) %collective-permute-start.3) | collective-permute-done | bytes 65568 | tf_op jit(solution)/shard_map/ppermute | solution.py:340
  16.4 0.0 copy-start.2
  16.4 1.5 %copy-done.2 = bf16[3,3,3,128,256]{4,3,2,1,0:T(8,128)(2,1)S(1)} copy-done((bf16[3,3,3,128,256]{4,3,2,1,0:T(8,128)(2,1)S(1)}, bf16[3,3,3,128,256]{4,3,2,1,0:T(8,128)(2,1)}, u32[]{:S(2)}) %copy-start.2) | copy-done | bytes 1769496
  17.8 1.2 %shard_map.75 = (f32[256,128]{1,0:T(8,128)S(1)}, bf16[256,128]{1,0:T(8,128)(2,1)S(1)}, bf16[256,128]{1,0:T(8,128)(2,1)S(1)}, bf16[256,128]{1,0:T(8,128)(2,1)S(1)}) custom-call(bf16[2,2,64,128]{3,2,1,0:T(8,128)(2,1)S(1)} %pad_maximum_fusion.own_ref, bf16[2,2,64,128]{3,2,1,0:T(8,128)(2,1)S(1)} %collective-permute-done.3.other_ref, ...), custom_call_target="tpu_custom_call" | custom-call | flops 905969664 | bytes 3145728 | tf_op jit(solution)/shard_map/pallas_call | solution.py:297
  19.1 0.1 collective-permute-start.4
  19.2 2.0 %collective-permute-start.5 = (bf16[256,128]{1,0:T(8,128)(2,1)S(1)}, bf16[256,128]{1,0:T(8,128)(2,1)S(1)}, u32[]{:S(2)}, u32[]{:S(2)}) collective-permute-start(bf16[256,128]{1,0:T(8,128)(2,1)S(1)} %get-tuple-element.19), channel_id=1, source_target_pairs={{0,8},{4,12},{8,0},{12,4},{1,9},{5,13},{9,1},{13,5},{2,10},{6,14},... | collective-permute-start | bytes 196616 | tf_op jit(solution)/shard_map/ppermute | solution.py:359
  21.2 2.4 %collective-permute-start.6 = (bf16[256,128]{1,0:T(8,128)(2,1)S(1)}, bf16[256,128]{1,0:T(8,128)(2,1)S(1)}, u32[]{:S(2)}, u32[]{:S(2)}) collective-permute-start(bf16[256,128]{1,0:T(8,128)(2,1)S(1)} %get-tuple-element.20), channel_id=1, source_target_pairs={{0,12},{4,8},{8,4},{12,0},{1,13},{5,9},{9,5},{13,1},{2,14},{6,10},... | collective-permute-start | bytes 196616 | tf_op jit(solution)/shard_map/ppermute | solution.py:359
  23.5 1.0 %collective-permute-done.4.refs_1_ = bf16[256,128]{1,0:T(8,128)(2,1)S(1)} collective-permute-done((bf16[256,128]{1,0:T(8,128)(2,1)S(1)}, bf16[256,128]{1,0:T(8,128)(2,1)S(1)}, u32[]{:S(2)}, u32[]{:S(2)}) %collective-permute-start.4) | collective-permute-done | bytes 65568 | tf_op jit(solution)/shard_map/ppermute | solution.py:359
  24.5 3.3 %collective-permute-done.5.refs_2_ = bf16[256,128]{1,0:T(8,128)(2,1)S(1)} collective-permute-done((bf16[256,128]{1,0:T(8,128)(2,1)S(1)}, bf16[256,128]{1,0:T(8,128)(2,1)S(1)}, u32[]{:S(2)}, u32[]{:S(2)}) %collective-permute-start.5) | collective-permute-done | bytes 65568 | tf_op jit(solution)/shard_map/ppermute | solution.py:359
  27.9 0.0 collective-permute-done.6.refs_3_
  27.9 0.0 copy-done.5
  27.9 0.0 copy-done.6
  27.9 0.0 copy-done.7
  27.9 0.3 shard_map.76
  28.2 1.5 %collective-permute-start.7 = (bf16[3,32,128]{2,1,0:T(8,128)(2,1)S(1)}, bf16[3,32,128]{2,1,0:T(8,128)(2,1)S(1)}, u32[]{:S(2)}, u32[]{:S(2)}) collective-permute-start(bf16[3,32,128]{2,1,0:T(8,128)(2,1)S(1)} %get-tuple-element.22), channel_id=1, source_target_pairs={{0,4},{4,0},{8,12},{12,8},{1,5},{5,1},{9,13},{13,9},{2,6},{6,2},{1... | collective-permute-start | bytes 73736 | tf_op jit(solution)/shard_map/ppermute | solution.py:372
  29.7 1.0 %collective-permute-start.8 = (bf16[3,32,128]{2,1,0:T(8,128)(2,1)S(1)}, bf16[3,32,128]{2,1,0:T(8,128)(2,1)S(1)}, u32[]{:S(2)}, u32[]{:S(2)}) collective-permute-start(bf16[3,32,128]{2,1,0:T(8,128)(2,1)S(1)} %get-tuple-element.23), channel_id=1, source_target_pairs={{0,8},{4,12},{8,0},{12,4},{1,9},{5,13},{9,1},{13,5},{2,10},{6,14},... | collective-permute-start | bytes 73736 | tf_op jit(solution)/shard_map/ppermute | solution.py:372
  30.7 2.0 %collective-permute-start.9 = (bf16[3,32,128]{2,1,0:T(8,128)(2,1)S(1)}, bf16[3,32,128]{2,1,0:T(8,128)(2,1)S(1)}, u32[]{:S(2)}, u32[]{:S(2)}) collective-permute-start(bf16[3,32,128]{2,1,0:T(8,128)(2,1)S(1)} %get-tuple-element.24), channel_id=1, source_target_pairs={{0,12},{4,8},{8,4},{12,0},{1,13},{5,9},{9,5},{13,1},{2,14},{6,10},... | collective-permute-start | bytes 73736 | tf_op jit(solution)/shard_map/ppermute | solution.py:372
  32.7 0.0 collective-permute-done.7.refs_1_
  32.7 2.0 %collective-permute-done.8.refs_2_ = bf16[3,32,128]{2,1,0:T(8,128)(2,1)S(1)} collective-permute-done((bf16[3,32,128]{2,1,0:T(8,128)(2,1)S(1)}, bf16[3,32,128]{2,1,0:T(8,128)(2,1)S(1)}, u32[]{:S(2)}, u32[]{:S(2)}) %collective-permute-start.8) | collective-permute-done | bytes 24608 | tf_op jit(solution)/shard_map/ppermute | solution.py:372
  34.7 1.6 %collective-permute-done.9.refs_3_ = bf16[3,32,128]{2,1,0:T(8,128)(2,1)S(1)} collective-permute-done((bf16[3,32,128]{2,1,0:T(8,128)(2,1)S(1)}, bf16[3,32,128]{2,1,0:T(8,128)(2,1)S(1)}, u32[]{:S(2)}, u32[]{:S(2)}) %collective-permute-start.9) | collective-permute-done | bytes 24608 | tf_op jit(solution)/shard_map/ppermute | solution.py:372
  36.3 0.1 collective-permute-start.10
  36.4 0.0 copy-done.4
  36.4 0.0 copy-done
  36.4 0.5 %shard_map.78.total_ref = f32[256,256]{1,0:T(8,128)S(1)} custom-call(bf16[3,4,16,256]{3,2,1,0:T(8,128)(2,1)S(1)} %shard_map.77.cells_ref, bf16[3,3,512,256]{3,2,1,0:T(8,128)(2,1)S(1)} %copy-done, f32[1,256]{1,0:T(1,128)S(1)} %bitcast.10), custom_call_target="tpu_custom_call" | custom-call | flops 301989888 | bytes 2097152 | tf_op jit(solution)/shard_map/pallas_call | solution.py:297
  36.9 0.8 %collective-permute-done.10.cells_ref = bf16[3,4,16,256]{3,2,1,0:T(8,128)(2,1)S(1)} collective-permute-done((bf16[3,4,16,256]{3,2,1,0:T(8,128)(2,1)S(1)}, bf16[3,4,16,256]{3,2,1,0:T(8,128)(2,1)S(1)}, u32[]{:S(2)}, u32[]{:S(2)}) %collective-permute-start.10) | collective-permute-done | bytes 98336 | tf_op jit(solution)/shard_map/ppermute | solution.py:382
  37.7 1.2 %shard_map.79 = bf16[2,8,4,4,256]{4,3,2,1,0:T(4,128)(2,1)} custom-call(bf16[3,4,16,256]{3,2,1,0:T(8,128)(2,1)S(1)} %collective-permute-done.10.cells_ref, bf16[3,3,512,256]{3,2,1,0:T(8,128)(2,1)S(1)} %copy-done, f32[256,256]{1,0:T(8,128)S(1)} %shard_map.78.total_ref), custom_call_target="tpu_custom_call" | custom-call | flops 301989888 | bytes 2097152 | tf_op jit(solution)/shard_map/pallas_call | solution.py:297
  (4 shorter events, 0.1 us)
Async XLA Ops:
  0.0 5.2 %collective-permute-start = (bf16[64,256]{1,0:T(8,128)(2,1)}, bf16[64,256]{1,0:T(8,128)(2,1)S(1)}, u32[]{:S(2)}, u32[]{:S(2)}) collective-permute-start(bf16[64,256]{1,0:T(8,128)(2,1)} %bitcast.7), channel_id=1, source_target_pairs={{0,2},{2,0},{1,3},{3,1},{4,6},{6,4},{5,7},{7,5},{8,10},{10,8},{9,1... | collective-permute-start | bytes 98312 | tf_op jit(solution)/shard_map/ppermute | solution.py:318
  2.9 1.5 %copy-start.1 = (bf16[3,3,3,128,256]{4,3,2,1,0:T(8,128)(2,1)S(1)}, bf16[3,3,3,128,256]{4,3,2,1,0:T(8,128)(2,1)}, u32[]{:S(2)}) copy-start(bf16[3,3,3,128,256]{4,3,2,1,0:T(8,128)(2,1)} %weight_ref.5) | copy-start | bytes 5308420
  4.4 0.8 %copy-start.3 = (bf16[2,2,2,8,256]{4,3,2,1,0:T(8,128)(2,1)S(1)}, bf16[2,2,2,8,256]{4,3,2,1,0:T(8,128)(2,1)}, u32[]{:S(2)}) copy-start(bf16[2,2,2,8,256]{4,3,2,1,0:T(8,128)(2,1)} %param.7) | copy-start | bytes 98308
  5.2 22.7 %copy-start.5 = (f32[256]{0:T(256)S(1)}, f32[256]{0:T(256)}, u32[]{:S(2)}) copy-start(f32[256]{0:T(256)} %param.9) | copy-start | bytes 3076
  5.2 22.7 %copy-start.6 = (f32[256]{0:T(256)S(1)}, f32[256]{0:T(256)}, u32[]{:S(2)}) copy-start(f32[256]{0:T(256)} %param.10) | copy-start | bytes 3076
  5.2 22.7 %copy-start.7 = (f32[256]{0:T(256)S(1)}, f32[256]{0:T(256)}, u32[]{:S(2)}) copy-start(f32[256]{0:T(256)} %param.11) | copy-start | bytes 3076
  5.2 31.2 %copy-start.4 = (f32[256]{0:T(256)S(1)}, f32[256]{0:T(256)}, u32[]{:S(2)}) copy-start(f32[256]{0:T(256)} %param.13) | copy-start | bytes 3076
  5.2 31.2 %copy-start = (bf16[3,3,512,256]{3,2,1,0:T(8,128)(2,1)S(1)}, bf16[3,3,512,256]{3,2,1,0:T(8,128)(2,1)}, u32[]{:S(2)}) copy-start(bf16[3,3,512,256]{3,2,1,0:T(8,128)(2,1)} %weight_ref.7) | copy-start | bytes 7077892
  5.3 4.0 %collective-permute-start.1 = (bf16[2,64,128]{2,1,0:T(8,128)(2,1)S(1)}, bf16[2,64,128]{2,1,0:T(8,128)(2,1)S(1)}, u32[]{:S(2)}, u32[]{:S(2)}) collective-permute-start(bf16[2,64,128]{2,1,0:T(8,128)(2,1)S(1)} %get-tuple-element.15), channel_id=1, source_target_pairs={{0,4},{1,8},{4,0},{5,12},{8,1},{9,13},{12,5},{13,9},{2,6},{3,10},{... | collective-permute-start | bytes 98312 | tf_op jit(solution)/shard_map/ppermute | solution.py:338
  7.2 2.0 %collective-permute-start.2 = (bf16[2,64,128]{2,1,0:T(8,128)(2,1)S(1)}, bf16[2,64,128]{2,1,0:T(8,128)(2,1)S(1)}, u32[]{:S(2)}, u32[]{:S(2)}) collective-permute-start(bf16[2,64,128]{2,1,0:T(8,128)(2,1)S(1)} %get-tuple-element.16), channel_id=1, source_target_pairs={{0,0},{1,12},{4,4},{5,8},{8,5},{9,9},{12,1},{13,13},{2,2},{3,14},{... | collective-permute-start | bytes 98312 | tf_op jit(solution)/shard_map/ppermute | solution.py:338
  9.3 7.1 %collective-permute-start.3 = (bf16[2,2,64,128]{3,2,1,0:T(8,128)(2,1)S(1)}, bf16[2,2,64,128]{3,2,1,0:T(8,128)(2,1)S(1)}, u32[]{:S(2)}, u32[]{:S(2)}) collective-permute-start(bf16[2,2,64,128]{3,2,1,0:T(8,128)(2,1)S(1)} %pad_maximum_fusion.own_ref), channel_id=1, source_target_pairs={{0,1},{1,0},{2,3},{3,2},{4,5},{5,4},{6,7},{7,6},{8,9},{9,8},{10,11... | collective-permute-start | bytes 196616 | tf_op jit(solution)/shard_map/ppermute | solution.py:340
  16.4 1.5 %copy-start.2 = (bf16[3,3,3,128,256]{4,3,2,1,0:T(8,128)(2,1)S(1)}, bf16[3,3,3,128,256]{4,3,2,1,0:T(8,128)(2,1)}, u32[]{:S(2)}) copy-start(bf16[3,3,3,128,256]{4,3,2,1,0:T(8,128)(2,1)} %weight_ref.5) | copy-start | bytes 5308420
  19.1 5.4 %collective-permute-start.4 = (bf16[256,128]{1,0:T(8,128)(2,1)S(1)}, bf16[256,128]{1,0:T(8,128)(2,1)S(1)}, u32[]{:S(2)}, u32[]{:S(2)}) collective-permute-start(bf16[256,128]{1,0:T(8,128)(2,1)S(1)} %get-tuple-element.18), channel_id=1, source_target_pairs={{0,4},{4,0},{8,12},{12,8},{1,5},{5,1},{9,13},{13,9},{2,6},{6,2},{1... | collective-permute-start | bytes 196616 | tf_op jit(solution)/shard_map/ppermute | solution.py:359
  19.2 8.7 %collective-permute-start.5 = (bf16[256,128]{1,0:T(8,128)(2,1)S(1)}, bf16[256,128]{1,0:T(8,128)(2,1)S(1)}, u32[]{:S(2)}, u32[]{:S(2)}) collective-permute-start(bf16[256,128]{1,0:T(8,128)(2,1)S(1)} %get-tuple-element.19), channel_id=1, source_target_pairs={{0,8},{4,12},{8,0},{12,4},{1,9},{5,13},{9,1},{13,5},{2,10},{6,14},... | collective-permute-start | bytes 196616 | tf_op jit(solution)/shard_map/ppermute | solution.py:359
  21.2 6.7 %collective-permute-start.6 = (bf16[256,128]{1,0:T(8,128)(2,1)S(1)}, bf16[256,128]{1,0:T(8,128)(2,1)S(1)}, u32[]{:S(2)}, u32[]{:S(2)}) collective-permute-start(bf16[256,128]{1,0:T(8,128)(2,1)S(1)} %get-tuple-element.20), channel_id=1, source_target_pairs={{0,12},{4,8},{8,4},{12,0},{1,13},{5,9},{9,5},{13,1},{2,14},{6,10},... | collective-permute-start | bytes 196616 | tf_op jit(solution)/shard_map/ppermute | solution.py:359
  28.2 4.5 %collective-permute-start.7 = (bf16[3,32,128]{2,1,0:T(8,128)(2,1)S(1)}, bf16[3,32,128]{2,1,0:T(8,128)(2,1)S(1)}, u32[]{:S(2)}, u32[]{:S(2)}) collective-permute-start(bf16[3,32,128]{2,1,0:T(8,128)(2,1)S(1)} %get-tuple-element.22), channel_id=1, source_target_pairs={{0,4},{4,0},{8,12},{12,8},{1,5},{5,1},{9,13},{13,9},{2,6},{6,2},{1... | collective-permute-start | bytes 73736 | tf_op jit(solution)/shard_map/ppermute | solution.py:372
  29.7 5.0 %collective-permute-start.8 = (bf16[3,32,128]{2,1,0:T(8,128)(2,1)S(1)}, bf16[3,32,128]{2,1,0:T(8,128)(2,1)S(1)}, u32[]{:S(2)}, u32[]{:S(2)}) collective-permute-start(bf16[3,32,128]{2,1,0:T(8,128)(2,1)S(1)} %get-tuple-element.23), channel_id=1, source_target_pairs={{0,8},{4,12},{8,0},{12,4},{1,9},{5,13},{9,1},{13,5},{2,10},{6,14},... | collective-permute-start | bytes 73736 | tf_op jit(solution)/shard_map/ppermute | solution.py:372
  30.7 5.6 %collective-permute-start.9 = (bf16[3,32,128]{2,1,0:T(8,128)(2,1)S(1)}, bf16[3,32,128]{2,1,0:T(8,128)(2,1)S(1)}, u32[]{:S(2)}, u32[]{:S(2)}) collective-permute-start(bf16[3,32,128]{2,1,0:T(8,128)(2,1)S(1)} %get-tuple-element.24), channel_id=1, source_target_pairs={{0,12},{4,8},{8,4},{12,0},{1,13},{5,9},{9,5},{13,1},{2,14},{6,10},... | collective-permute-start | bytes 73736 | tf_op jit(solution)/shard_map/ppermute | solution.py:372
  36.3 1.4 %collective-permute-start.10 = (bf16[3,4,16,256]{3,2,1,0:T(8,128)(2,1)S(1)}, bf16[3,4,16,256]{3,2,1,0:T(8,128)(2,1)S(1)}, u32[]{:S(2)}, u32[]{:S(2)}) collective-permute-start(bf16[3,4,16,256]{3,2,1,0:T(8,128)(2,1)S(1)} %shard_map.77.cells_ref), channel_id=1, source_target_pairs={{0,1},{1,0},{2,3},{3,2},{4,5},{5,4},{6,7},{7,6},{8,9},{9,8},{10,11... | collective-permute-start | bytes 294920 | tf_op jit(solution)/shard_map/ppermute | solution.py:382

commit v5 on v4

--- a/solution.py
+++ b/solution.py
@@ -126,68 +126,75 @@
     return lax.axis_index("tm"), lax.axis_index("space"), lax.axis_index("chan")
 
 
-def fetch_kernel(latents_ref, weight_ref, token_ref):
-    depth = token_ref.shape[1]
-    token_ref[...] = latents_ref[:16, :depth] + weight_ref[0, 0, 0, :16, :depth]
-
-
-def pack_kernel(own_ref, other_ref, token_ref, first_ref, second_ref):
-    del token_ref
+def fetch_kernel(weight_ref, weight_out, sem):
+    copy = pltpu.make_async_copy(weight_ref, weight_out, sem)
+    copy.start()
+    copy.wait()
+
+
+def select_kernel(first_ref, second_ref, after_ref, out_ref):
+    del after_ref
+    tm, _, _ = placed_at()
+    depth = out_ref.shape[2]
+    upper = tm % 2 > 0
+    for i, ref in enumerate((first_ref, second_ref)):
+        out_ref[i] = jnp.where(upper, ref[:, depth:], ref[:, :depth])
+
+
+def conv_of_clip(clip, got, weight_ref, latents, taps):
+    spans, spaces, span, rows, cols, depth = latents.shape
+    frames, tall = spans * span, spaces * rows
     tm, side, chan = placed_at()
-    depth = first_ref.shape[2]
-    home = (chan == tm // 2).astype(jnp.int32)
-    upper = ((tm % 2) ^ home) > 0
-    for ref, at in ((own_ref, side), (other_ref, 1 - side)):
-        low, high = ref[:, :depth], ref[:, depth:]
-        first_ref[at] = jnp.where(upper, high, low)
-        second_ref[at] = jnp.where(upper, low, high)
-
-
-def conv_kernel(own_ref, other_ref, weight_ref, keep_ref, *refs):
-    sent, (latents, taps, tiles) = refs[:3], refs[3:]
-    spans, spaces, clips, span, rows, cols, depth = latents.shape
-    frames, tall = spans * span, spaces * rows
-    tm, _, chan = placed_at()
-    home = chan == tm // 2
-    near, far = jnp.where(home, 0, 2), jnp.where(home, 2, 0)
-    for ref, turn in ((own_ref, near), (other_ref, far)):
-        first = jnp.where(turn > 0, tm ^ 2, tm ^ 1)
-        second = jnp.where(turn > 0, tm ^ 3, tm)
-        latents[first] = ref[0].astype(jnp.float32).reshape(latents.shape[1:])
-        latents[second] = ref[1].astype(jnp.float32).reshape(latents.shape[1:])
+    size = span * rows * cols
+    part = pl.ds(pl.multiple_of(clip * size, size), size)
+    for i, ref in enumerate(got):
+        at = side if i < 2 else 1 - side
+        home = (chan if i % 2 == 0 else 1 - chan) == tm // 2
+        for j, source in enumerate((jnp.where(home, tm ^ 1, tm ^ 2), jnp.where(home, tm, tm ^ 3))):
+            latents[source, at] = ref[j, part, :].astype(jnp.float32).reshape(latents.shape[2:])
     column = lax.broadcasted_iota(jnp.int32, (1, cols, depth), 1)
-    taps[0] = jnp.zeros(taps.shape[1:], taps.dtype)
-    taps[tall + 1] = jnp.zeros(taps.shape[1:], taps.dtype)
+    empty = jnp.zeros((frames, cols, depth), jnp.float32)
+    lines = [[empty] * 3]
     for at in range(spaces):
         for row in range(rows):
-            line = at * rows + row + 1
-            taps[line, :2] = jnp.zeros((2,) + taps.shape[2:], taps.dtype)
-            shifts = [[], [], []]
-            for clip in range(clips):
-                parts = [latents[(j + clip) % spans, at, clip, :, row] for j in range(spans)]
-                value = jnp.concatenate(parts, axis=0)
-                shifts[0].append(jnp.where(column > 0, pltpu.roll(value, 1, 1), 0.0))
-                shifts[1].append(value)
-                shifts[2].append(jnp.where(column < cols - 1, pltpu.roll(value, cols - 1, 1), 0.0))
-            for e in range(3):
-                piece = jnp.concatenate(shifts[e], axis=1).astype(taps.dtype)
-                taps[line, 2:, :, e * depth : (e + 1) * depth] = piece
-    count = frames * tall * cols
+            parts = [latents[(j + clip) % spans, at, :, row] for j in range(spans)]
+            value = jnp.concatenate(parts, axis=0)
+            lower = jnp.where(column > 0, pltpu.roll(value, 1, 1), 0.0)
+            upper = jnp.where(column < cols - 1, pltpu.roll(value, cols - 1, 1), 0.0)
+            lines.append([lower, value, upper])
+    lines.append([empty] * 3)
+    short = tall // 2
+    for line in range(short + 2):
+        taps[line, :2] = jnp.zeros((2,) + taps.shape[2:], taps.dtype)
+        for e in range(3):
+            piece = jnp.concatenate([lines[line][e], lines[line + short][e]], axis=1)
+            taps[line, 2:, :, e * depth : (e + 1) * depth] = piece.astype(taps.dtype)
     total = None
     for a in range(3):
-        lines = [taps[b : b + tall, a : a + frames].reshape(clips * count, 3 * depth) for b in range(3)]
+        wide = [taps[b : b + short, a : a + frames].reshape(frames * tall * cols, 3 * depth) for b in range(3)]
         right = weight_ref[a].reshape(9 * depth, weight_ref.shape[4])
-        part = jnp.dot(jnp.concatenate(lines, axis=1), right, preferred_element_type=jnp.float32)
-        total = part if total is None else total + part
-    width = tiles.shape[2]
-    los = spans // clips
-    total = total.reshape(tall * frames, clips, cols, total.shape[1])
-    for clip in range(clips):
-        for x in range(los):
-            tiles[clip * los + x] = total[:, clip, :, x * width : (x + 1) * width].reshape(count, width)
-    keep_ref[...] = tiles[tm]
-    for m in range(1, spans):
-        sent[m - 1][...] = tiles[tm ^ m].astype(sent[m - 1].dtype)
+        product = jnp.dot(jnp.concatenate(wide, axis=1), right, preferred_element_type=jnp.float32)
+        total = product if total is None else total + product
+    width = total.shape[1] // 2
+    swapped = tm % 2 > 0
+    lower, upper = total[:, :width], total[:, width:]
+    return jnp.where(swapped, upper, lower), jnp.where(swapped, lower, upper)
+
+
+def conv_far_kernel(own_ref, core_ref, row_ref, both_ref, weight_ref, same_ref, other_ref, latents, taps):
+    tm, _, _ = placed_at()
+    got = (own_ref, core_ref, row_ref, both_ref)
+    same, other = conv_of_clip(1 - tm // 2, got, weight_ref, latents, taps)
+    same_ref[...] = same.astype(same_ref.dtype)
+    other_ref[...] = other.astype(other_ref.dtype)
+
+
+def conv_near_kernel(own_ref, core_ref, row_ref, both_ref, weight_ref, keep_ref, other_ref, latents, taps):
+    tm, _, _ = placed_at()
+    got = (own_ref, core_ref, row_ref, both_ref)
+    keep, other = conv_of_clip(tm // 2, got, weight_ref, latents, taps)
+    keep_ref[...] = keep
+    other_ref[...] = other.astype(other_ref.dtype)
 
 
 def norm_kernel(*refs):
@@ -215,8 +222,9 @@
     mean, square = both[0:1], both[1:2]
     factor = lax.rsqrt(square - mean * mean + 1e-06)
     normed = (flat - mean) * factor * gain_ref[block, :] + shift_ref[block, :]
-    active = (normed / (1.0 + jnp.exp(-normed))).reshape(tall, frames, cols, depth)
-    cells = [jnp.swapaxes(active[row], 0, 1) for row in range(tall)]
+    active = (normed / (1.0 + jnp.exp(-normed))).reshape(tall // 2, frames, 2, cols, depth)
+    short = tall // 2
+    cells = [jnp.swapaxes(active[row % short, :, row // short], 0, 1) for row in range(tall)]
     width = cols // owners
     empty = jnp.zeros((frames, depth), jnp.float32)
     for i in range(reach):
@@ -315,49 +323,39 @@
     flip = ((0, 1), (1, 0))
 
     cells_in = latents.reshape(clips * span * rows * cols, half)
-    other = lax.ppermute(cells_in, "space", flip)
-    token = run(
-        fetch_kernel,
-        shape((16, depth), low),
-        [],
-        cells_in,
-        conv_weight,
-        moved=4 << 20,
-    )
-    packed = shape((spaces, cells_in.shape[0], depth), low)
-    pair = run(pack_kernel, [packed, packed], [], cells_in, other, token, moved=1 << 17)
     turns = ((1, 2), (0, 3))
     got = []
-    for block, (at_home, across) in zip(pair, turns):
+    for at_home, across in turns:
         pairs = []
         for source in range(spans):
             for chan in range(chans):
                 home = chan == source // 2
                 target = (source ^ at_home, chan) if home else (source ^ across, 1 - chan)
                 pairs.append((source * chans + chan, target[0] * chans + target[1]))
-        got.append(lax.ppermute(block, ("tm", "chan"), pairs))
-    got = jnp.stack(got)
-    core = lax.ppermute(got, "chan", flip)
+        got.append(lax.ppermute(cells_in, ("tm", "chan"), pairs))
+    weight = run(fetch_kernel, shape(conv_weight.shape, low), [pltpu.SemaphoreType.DMA], conv_weight, moved=4 << 20)
+    own = run(select_kernel, shape((2, cells_in.shape[0], depth), low), [], *got, weight, moved=1 << 17)
+    every = [own] + [
+        lax.ppermute(own, ("space", "chan"), [(i, i ^ m) for i in range(spaces * chans)]) for m in range(1, spaces * chans)
+    ]
 
     count = frames * tall * cols
     part = shape((count, depth), low)
-    partial = run(
-        conv_kernel,
-        [shape((count, depth), full)] + [part] * (spans - 1),
-        [
-            pltpu.VMEM((spans, spaces, clips, span, rows, cols, depth), full),
-            pltpu.VMEM((tall + 2, frames + 2, clips * cols, 3 * depth), low),
-            pltpu.VMEM((spans, count, depth), full),
-        ],
-        got,
-        core,
-        conv_weight,
-        flops=2 * clips * count * 27 * depth * half,
-        moved=3 << 20,
-    )
-    partial = [partial[0]] + [
-        lax.ppermute(partial[m], "tm", [(i, i ^ m) for i in range(spans)]) for m in range(1, spans)
+    scratch = [
+        pltpu.VMEM((spans, spaces, span, rows, cols, depth), full),
+        pltpu.VMEM((tall // 2 + 2, frames + 2, 2 * cols, 3 * depth), low),
     ]
+    flops = 2 * count * 27 * depth * half
+    far_same, far_other = run(
+        conv_far_kernel, [part, part], scratch, *every, weight, flops=flops, moved=3 << 20
+    )
+    partial = [
+        lax.ppermute(value, "tm", [(i, i ^ m) for i in range(spans)]) for m, value in ((2, far_same), (3, far_other))
+    ]
+    keep, near_other = run(
+        conv_near_kernel, [shape(part.shape, full), part], scratch, *every, weight, flops=flops, moved=3 << 20
+    )
+    partial = [keep] + partial + [lax.ppermute(near_other, "tm", [(i, i ^ 1) for i in range(spans)])]
 
     tile = shape((rows + 1, (width + 2) * frames, depth), low)
     tiles = run(

time: 39.1 us -> 35.5 us (0.908)
  local copies, waits for them, and re-layouts: 3.73 us -> 1.51 us
  starting transfers between devices: 20.7 us -> 19.2 us
  Pallas kernels: 3.29 us -> 3.79 us
    unnamed x16 -> x12, local copies, waits for them, and re-layouts: 3.73 us -> 1.51 us
    ppermute x3, waiting for transfers between devices: 3.6 us -> 1.93 us  [small_plan(): lax.ppermute(tiles[m], 'tm', [(i, i ^ m) for i in range(spans)])]
    ppermute x7 -> x8, starting transfers between devices: 16.2 us -> 14.7 us  [the longest x3 6.63 us: small_plan(): lax.ppermute(own, ('space', 'chan'), [(i, i ^ m) for i in range(spaces *...]
    ppermute x7 -> x8, waiting for transfers between devices: 6.56 us -> 7.91 us  [the longest x3 3.66 us: small_plan(): lax.ppermute(own, ('space', 'chan'), [(i, i ^ m) for i in range(spaces *...]
    pallas_call x7 -> x8, Pallas kernels: 3.29 us -> 3.79 us  [run(): pl.pallas_call(kernel, out_shape=shapes, in_specs=[vmem] * len(operands),...]
  transfers between devices with their start and end apart: 11 -> 12, of which waited for: 7 -> 7; matrix products, arithmetic and copies ran while one was open for 0% -> 0% of each run, Pallas kernels for 1% -> 4%
where the time goes in v5:
time: 35.5 us; the launch traced here: 35.3 us
  starting transfers between devices  19.2 us (54%)
  waiting for transfers between devices  10.6 us (30%)
  Pallas kernels  3.79 us (11%)
  local copies, waits for them, and re-layouts  1.51 us (4%)
    ppermute x3, starting transfers between devices, small_plan(): lax.ppermute(own, ('space', 'chan'), [(i, i ^ m) for i in range(spaces *...  6.63 us
    ppermute x3, starting transfers between devices, small_plan(): lax.ppermute(tiles[m], 'tm', [(i, i ^ m) for i in range(spans)])  4.45 us
    ppermute x2, starting transfers between devices, small_plan(): got.append(lax.ppermute(cells_in, ('tm', 'chan'), pairs))  4.43 us
    pallas_call x8, Pallas kernels, run(): pl.pallas_call(kernel, out_shape=shapes, in_specs=[vmem] * len(operands),...  3.79 us
    ppermute x3, waiting for transfers between devices, small_plan(): lax.ppermute(own, ('space', 'chan'), [(i, i ^ m) for i in range(spaces *...  3.66 us
    ppermute x2, waiting for transfers between devices, small_plan(): lax.ppermute(value, 'tm', [(i, i ^ m) for i in range(spans)])  3.08 us
    ppermute x2, starting transfers between devices, small_plan(): lax.ppermute(value, 'tm', [(i, i ^ m) for i in range(spans)])  2.2 us
    ppermute x3, waiting for transfers between devices, small_plan(): lax.ppermute(tiles[m], 'tm', [(i, i ^ m) for i in range(spans)])  1.93 us
  transfers between devices with their start and end apart: 12, of which 7 were waited for; matrix products, arithmetic and copies ran while one was open for 0% of the time, Pallas kernels for 4%

profile of v5, /device:TPU:0, one launch (start us, length us, event | category | flops | bytes accessed | tf_op | source)
XLA Modules:
  0.0 35.3 jit_solution(10047564280808129653)
XLA Ops:
  0.0 3.0 %collective-permute-start = (bf16[64,256]{1,0:T(8,128)(2,1)}, bf16[64,256]{1,0:T(8,128)(2,1)S(1)}, u32[]{:S(2)}, u32[]{:S(2)}) collective-permute-start(bf16[64,256]{1,0:T(8,128)(2,1)} %bitcast.9), channel_id=1, source_target_pairs={{0,4},{1,8},{4,0},{5,12},{8,1},{9,13},{12,5},{13,9},{2,6},{3,10},{... | collective-permute-start | bytes 98312 | tf_op jit(solution)/shard_map/ppermute | solution.py:335
  3.0 1.4 %collective-permute-start.1 = (bf16[64,256]{1,0:T(8,128)(2,1)}, bf16[64,256]{1,0:T(8,128)(2,1)S(1)}, u32[]{:S(2)}, u32[]{:S(2)}) collective-permute-start(bf16[64,256]{1,0:T(8,128)(2,1)} %bitcast.10), channel_id=1, source_target_pairs={{0,0},{1,12},{4,4},{5,8},{8,5},{9,9},{12,1},{13,13},{2,2},{3,14},{... | collective-permute-start | bytes 98312 | tf_op jit(solution)/shard_map/ppermute | solution.py:335
  4.4 0.0 copy-start.1
  4.4 1.5 %copy-done.1 = bf16[3,3,3,128,256]{4,3,2,1,0:T(8,128)(2,1)S(1)} copy-done((bf16[3,3,3,128,256]{4,3,2,1,0:T(8,128)(2,1)S(1)}, bf16[3,3,3,128,256]{4,3,2,1,0:T(8,128)(2,1)}, u32[]{:S(2)}) %copy-start.1) | copy-done | bytes 1769496
  5.9 0.4 %shard_map.73.after_ref.weight_ref = bf16[3,3,3,128,256]{4,3,2,1,0:T(8,128)(2,1)S(1)} custom-call(bf16[3,3,3,128,256]{4,3,2,1,0:T(8,128)(2,1)S(1)} %copy-done.1), custom_call_target="tpu_custom_call" | custom-call | bytes 4194304 | tf_op jit(solution)/shard_map/pallas_call | solution.py:305
  6.3 0.0 collective-permute-done.first_ref
  6.3 0.0 collective-permute-done.1.second_ref
  6.3 0.0 copy-start.3
  6.3 0.0 copy-start.4
  6.4 0.0 copy-start.5
  6.4 0.0 copy-start
  6.4 0.0 copy-start.2
  6.4 5.1 %collective-permute-start.2 = (bf16[2,64,128]{2,1,0:T(8,128)(2,1)S(1)}, bf16[2,64,128]{2,1,0:T(8,128)(2,1)S(1)}, u32[]{:S(2)}, u32[]{:S(2)}) collective-permute-start(bf16[2,64,128]{2,1,0:T(8,128)(2,1)S(1)} %shard_map.74.own_ref), channel_id=1, source_target_pairs={{0,1},{1,0},{2,3},{3,2},{4,5},{5,4},{6,7},{7,6},{8,9},{9,8},{10,11... | collective-permute-start | bytes 98312 | tf_op jit(solution)/shard_map/ppermute | solution.py:339
  11.5 1.5 %collective-permute-start.3 = (bf16[2,64,128]{2,1,0:T(8,128)(2,1)S(1)}, bf16[2,64,128]{2,1,0:T(8,128)(2,1)S(1)}, u32[]{:S(2)}, u32[]{:S(2)}) collective-permute-start(bf16[2,64,128]{2,1,0:T(8,128)(2,1)S(1)} %shard_map.74.own_ref), channel_id=1, source_target_pairs={{0,2},{1,3},{2,0},{3,1},{4,6},{5,7},{6,4},{7,5},{8,10},{9,11},{10,... | collective-permute-start | bytes 98312 | tf_op jit(solution)/shard_map/ppermute | solution.py:339
  13.0 0.0 collective-permute-start.4
  13.0 0.0 collective-permute-done.2.core_ref
  13.0 2.4 %collective-permute-done.3.row_ref = bf16[2,64,128]{2,1,0:T(8,128)(2,1)S(1)} collective-permute-done((bf16[2,64,128]{2,1,0:T(8,128)(2,1)S(1)}, bf16[2,64,128]{2,1,0:T(8,128)(2,1)S(1)}, u32[]{:S(2)}, u32[]{:S(2)}) %collective-permute-start.3) | collective-permute-done | bytes 32800 | tf_op jit(solution)/shard_map/ppermute | solution.py:339
  15.4 1.2 %collective-permute-done.4.both_ref = bf16[2,64,128]{2,1,0:T(8,128)(2,1)S(1)} collective-permute-done((bf16[2,64,128]{2,1,0:T(8,128)(2,1)S(1)}, bf16[2,64,128]{2,1,0:T(8,128)(2,1)S(1)}, u32[]{:S(2)}, u32[]{:S(2)}) %collective-permute-start.4) | collective-permute-done | bytes 32800 | tf_op jit(solution)/shard_map/ppermute | solution.py:339
  16.7 0.7 %shard_map.76 = (bf16[256,128]{1,0:T(8,128)(2,1)S(1)}, bf16[256,128]{1,0:T(8,128)(2,1)S(1)}) custom-call(bf16[2,64,128]{2,1,0:T(8,128)(2,1)S(1)} %shard_map.74.own_ref, bf16[2,64,128]{2,1,0:T(8,128)(2,1)S(1)} %collective-permute-done.2.core_ref, bf16[2,64,128]{2,1,0:T(8,128)(2,1)S(1)} %collective-permute-done.3.row_ref, ...), custom_call_target="tpu_custom_call" | custom-call | flops 452984832 | bytes 3145728 | tf_op jit(solution)/shard_map/pallas_call | solution.py:305
  17.4 0.1 collective-permute-start.5
  17.5 2.1 %collective-permute-start.6 = (bf16[256,128]{1,0:T(8,128)(2,1)S(1)}, bf16[256,128]{1,0:T(8,128)(2,1)S(1)}, u32[]{:S(2)}, u32[]{:S(2)}) collective-permute-start(bf16[256,128]{1,0:T(8,128)(2,1)S(1)} %get-tuple-element.15), channel_id=1, source_target_pairs={{0,12},{4,8},{8,4},{12,0},{1,13},{5,9},{9,5},{13,1},{2,14},{6,10},... | collective-permute-start | bytes 196616 | tf_op jit(solution)/shard_map/ppermute | solution.py:353
  19.6 0.7 %shard_map.75 = (f32[256,128]{1,0:T(8,128)S(1)}, bf16[256,128]{1,0:T(8,128)(2,1)S(1)}) custom-call(bf16[2,64,128]{2,1,0:T(8,128)(2,1)S(1)} %shard_map.74.own_ref, bf16[2,64,128]{2,1,0:T(8,128)(2,1)S(1)} %collective-permute-done.2.core_ref, bf16[2,64,128]{2,1,0:T(8,128)(2,1)S(1)} %collective-permute-done.3.row_ref, ...), custom_call_target="tpu_custom_call" | custom-call | flops 452984832 | bytes 3145728 | tf_op jit(solution)/shard_map/pallas_call | solution.py:305
  20.3 1.4 %collective-permute-start.7 = (bf16[256,128]{1,0:T(8,128)(2,1)S(1)}, bf16[256,128]{1,0:T(8,128)(2,1)S(1)}, u32[]{:S(2)}, u32[]{:S(2)}) collective-permute-start(bf16[256,128]{1,0:T(8,128)(2,1)S(1)} %get-tuple-element.16), channel_id=1, source_target_pairs={{0,4},{4,0},{8,12},{12,8},{1,5},{5,1},{9,13},{13,9},{2,6},{6,2},{1... | collective-permute-start | bytes 196616 | tf_op jit(solution)/shard_map/ppermute | solution.py:358
  21.7 3.1 %collective-permute-done.5.refs_1_ = bf16[256,128]{1,0:T(8,128)(2,1)S(1)} collective-permute-done((bf16[256,128]{1,0:T(8,128)(2,1)S(1)}, bf16[256,128]{1,0:T(8,128)(2,1)S(1)}, u32[]{:S(2)}, u32[]{:S(2)}) %collective-permute-start.5) | collective-permute-done | bytes 65568 | tf_op jit(solution)/shard_map/ppermute | solution.py:353
  24.8 0.0 collective-permute-done.6.refs_2_
  24.8 1.2 %collective-permute-done.7.refs_3_ = bf16[256,128]{1,0:T(8,128)(2,1)S(1)} collective-permute-done((bf16[256,128]{1,0:T(8,128)(2,1)S(1)}, bf16[256,128]{1,0:T(8,128)(2,1)S(1)}, u32[]{:S(2)}, u32[]{:S(2)}) %collective-permute-start.7) | collective-permute-done | bytes 65568 | tf_op jit(solution)/shard_map/ppermute | solution.py:358
  25.9 0.0 copy-done.3
  25.9 0.0 copy-done.4
  25.9 0.0 copy-done.5
  26.0 0.3 shard_map.77
  26.3 1.5 %collective-permute-start.10 = (bf16[3,32,128]{2,1,0:T(8,128)(2,1)S(1)}, bf16[3,32,128]{2,1,0:T(8,128)(2,1)S(1)}, u32[]{:S(2)}, u32[]{:S(2)}) collective-permute-start(bf16[3,32,128]{2,1,0:T(8,128)(2,1)S(1)} %get-tuple-element.20), channel_id=1, source_target_pairs={{0,12},{4,8},{8,4},{12,0},{1,13},{5,9},{9,5},{13,1},{2,14},{6,10},... | collective-permute-start | bytes 73736 | tf_op jit(solution)/shard_map/ppermute | solution.py:370
  27.8 0.0 collective-permute-start.8
  27.8 2.9 %collective-permute-start.9 = (bf16[3,32,128]{2,1,0:T(8,128)(2,1)S(1)}, bf16[3,32,128]{2,1,0:T(8,128)(2,1)S(1)}, u32[]{:S(2)}, u32[]{:S(2)}) collective-permute-start(bf16[3,32,128]{2,1,0:T(8,128)(2,1)S(1)} %get-tuple-element.19), channel_id=1, source_target_pairs={{0,8},{4,12},{8,0},{12,4},{1,9},{5,13},{9,1},{13,5},{2,10},{6,14},... | collective-permute-start | bytes 73736 | tf_op jit(solution)/shard_map/ppermute | solution.py:370
  30.8 1.2 %collective-permute-done.10.refs_3_ = bf16[3,32,128]{2,1,0:T(8,128)(2,1)S(1)} collective-permute-done((bf16[3,32,128]{2,1,0:T(8,128)(2,1)S(1)}, bf16[3,32,128]{2,1,0:T(8,128)(2,1)S(1)}, u32[]{:S(2)}, u32[]{:S(2)}) %collective-permute-start.10) | collective-permute-done | bytes 24608 | tf_op jit(solution)/shard_map/ppermute | solution.py:370
  32.0 0.0 collective-permute-done.8.refs_1_
  32.0 0.7 %collective-permute-done.9.refs_2_ = bf16[3,32,128]{2,1,0:T(8,128)(2,1)S(1)} collective-permute-done((bf16[3,32,128]{2,1,0:T(8,128)(2,1)S(1)}, bf16[3,32,128]{2,1,0:T(8,128)(2,1)S(1)}, u32[]{:S(2)}, u32[]{:S(2)}) %collective-permute-start.9) | collective-permute-done | bytes 24608 | tf_op jit(solution)/shard_map/ppermute | solution.py:370
  32.7 0.1 collective-permute-start.11
  32.8 0.0 copy-done
  32.8 0.0 copy-done.2
  32.8 0.5 %shard_map.79.total_ref = f32[256,256]{1,0:T(8,128)S(1)} custom-call(bf16[3,4,16,256]{3,2,1,0:T(8,128)(2,1)S(1)} %shard_map.78.cells_ref, bf16[3,3,512,256]{3,2,1,0:T(8,128)(2,1)S(1)} %copy-done, f32[1,256]{1,0:T(1,128)S(1)} %bitcast.5), custom_call_target="tpu_custom_call" | custom-call | flops 301989888 | bytes 2097152 | tf_op jit(solution)/shard_map/pallas_call | solution.py:305
  33.3 0.8 %collective-permute-done.11.cells_ref = bf16[3,4,16,256]{3,2,1,0:T(8,128)(2,1)S(1)} collective-permute-done((bf16[3,4,16,256]{3,2,1,0:T(8,128)(2,1)S(1)}, bf16[3,4,16,256]{3,2,1,0:T(8,128)(2,1)S(1)}, u32[]{:S(2)}, u32[]{:S(2)}) %collective-permute-start.11) | collective-permute-done | bytes 98336 | tf_op jit(solution)/shard_map/ppermute | solution.py:380
  34.1 1.2 %shard_map.80 = bf16[2,8,4,4,256]{4,3,2,1,0:T(4,128)(2,1)} custom-call(bf16[3,4,16,256]{3,2,1,0:T(8,128)(2,1)S(1)} %collective-permute-done.11.cells_ref, bf16[3,3,512,256]{3,2,1,0:T(8,128)(2,1)S(1)} %copy-done, f32[256,256]{1,0:T(8,128)S(1)} %shard_map.79.total_ref), custom_call_target="tpu_custom_call" | custom-call | flops 301989888 | bytes 2097152 | tf_op jit(solution)/shard_map/pallas_call | solution.py:305
  (2 shorter events, 0.1 us)
Async XLA Ops:
  0.0 6.3 %collective-permute-start = (bf16[64,256]{1,0:T(8,128)(2,1)}, bf16[64,256]{1,0:T(8,128)(2,1)S(1)}, u32[]{:S(2)}, u32[]{:S(2)}) collective-permute-start(bf16[64,256]{1,0:T(8,128)(2,1)} %bitcast.9), channel_id=1, source_target_pairs={{0,4},{1,8},{4,0},{5,12},{8,1},{9,13},{12,5},{13,9},{2,6},{3,10},{... | collective-permute-start | bytes 98312 | tf_op jit(solution)/shard_map/ppermute | solution.py:335
  3.0 3.3 %collective-permute-start.1 = (bf16[64,256]{1,0:T(8,128)(2,1)}, bf16[64,256]{1,0:T(8,128)(2,1)S(1)}, u32[]{:S(2)}, u32[]{:S(2)}) collective-permute-start(bf16[64,256]{1,0:T(8,128)(2,1)} %bitcast.10), channel_id=1, source_target_pairs={{0,0},{1,12},{4,4},{5,8},{8,5},{9,9},{12,1},{13,13},{2,2},{3,14},{... | collective-permute-start | bytes 98312 | tf_op jit(solution)/shard_map/ppermute | solution.py:335
  4.4 1.5 %copy-start.1 = (bf16[3,3,3,128,256]{4,3,2,1,0:T(8,128)(2,1)S(1)}, bf16[3,3,3,128,256]{4,3,2,1,0:T(8,128)(2,1)}, u32[]{:S(2)}) copy-start(bf16[3,3,3,128,256]{4,3,2,1,0:T(8,128)(2,1)} %weight_ref.3) | copy-start | bytes 5308420
  6.3 19.6 %copy-start.3 = (f32[256]{0:T(256)S(1)}, f32[256]{0:T(256)}, u32[]{:S(2)}) copy-start(f32[256]{0:T(256)} %param.9) | copy-start | bytes 3076
  6.3 19.6 %copy-start.4 = (f32[256]{0:T(256)S(1)}, f32[256]{0:T(256)}, u32[]{:S(2)}) copy-start(f32[256]{0:T(256)} %param.10) | copy-start | bytes 3076
  6.4 19.6 %copy-start.5 = (f32[256]{0:T(256)S(1)}, f32[256]{0:T(256)}, u32[]{:S(2)}) copy-start(f32[256]{0:T(256)} %param.11) | copy-start | bytes 3076
  6.4 26.4 %copy-start = (bf16[3,3,512,256]{3,2,1,0:T(8,128)(2,1)S(1)}, bf16[3,3,512,256]{3,2,1,0:T(8,128)(2,1)}, u32[]{:S(2)}) copy-start(bf16[3,3,512,256]{3,2,1,0:T(8,128)(2,1)} %weight_ref.5) | copy-start | bytes 7077892
  6.4 26.4 %copy-start.2 = (f32[256]{0:T(256)S(1)}, f32[256]{0:T(256)}, u32[]{:S(2)}) copy-start(f32[256]{0:T(256)} %param.13) | copy-start | bytes 3076
  6.4 6.6 %collective-permute-start.2 = (bf16[2,64,128]{2,1,0:T(8,128)(2,1)S(1)}, bf16[2,64,128]{2,1,0:T(8,128)(2,1)S(1)}, u32[]{:S(2)}, u32[]{:S(2)}) collective-permute-start(bf16[2,64,128]{2,1,0:T(8,128)(2,1)S(1)} %shard_map.74.own_ref), channel_id=1, source_target_pairs={{0,1},{1,0},{2,3},{3,2},{4,5},{5,4},{6,7},{7,6},{8,9},{9,8},{10,11... | collective-permute-start | bytes 98312 | tf_op jit(solution)/shard_map/ppermute | solution.py:339
  11.5 3.9 %collective-permute-start.3 = (bf16[2,64,128]{2,1,0:T(8,128)(2,1)S(1)}, bf16[2,64,128]{2,1,0:T(8,128)(2,1)S(1)}, u32[]{:S(2)}, u32[]{:S(2)}) collective-permute-start(bf16[2,64,128]{2,1,0:T(8,128)(2,1)S(1)} %shard_map.74.own_ref), channel_id=1, source_target_pairs={{0,2},{1,3},{2,0},{3,1},{4,6},{5,7},{6,4},{7,5},{8,10},{9,11},{10,... | collective-permute-start | bytes 98312 | tf_op jit(solution)/shard_map/ppermute | solution.py:339
  13.0 3.7 %collective-permute-start.4 = (bf16[2,64,128]{2,1,0:T(8,128)(2,1)S(1)}, bf16[2,64,128]{2,1,0:T(8,128)(2,1)S(1)}, u32[]{:S(2)}, u32[]{:S(2)}) collective-permute-start(bf16[2,64,128]{2,1,0:T(8,128)(2,1)S(1)} %shard_map.74.own_ref), channel_id=1, source_target_pairs={{0,3},{1,2},{2,1},{3,0},{4,7},{5,6},{6,5},{7,4},{8,11},{9,10},{10,... | collective-permute-start | bytes 98312 | tf_op jit(solution)/shard_map/ppermute | solution.py:339
  17.4 7.4 %collective-permute-start.5 = (bf16[256,128]{1,0:T(8,128)(2,1)S(1)}, bf16[256,128]{1,0:T(8,128)(2,1)S(1)}, u32[]{:S(2)}, u32[]{:S(2)}) collective-permute-start(bf16[256,128]{1,0:T(8,128)(2,1)S(1)} %get-tuple-element.14), channel_id=1, source_target_pairs={{0,8},{4,12},{8,0},{12,4},{1,9},{5,13},{9,1},{13,5},{2,10},{6,14},... | collective-permute-start | bytes 196616 | tf_op jit(solution)/shard_map/ppermute | solution.py:353
  17.5 7.3 %collective-permute-start.6 = (bf16[256,128]{1,0:T(8,128)(2,1)S(1)}, bf16[256,128]{1,0:T(8,128)(2,1)S(1)}, u32[]{:S(2)}, u32[]{:S(2)}) collective-permute-start(bf16[256,128]{1,0:T(8,128)(2,1)S(1)} %get-tuple-element.15), channel_id=1, source_target_pairs={{0,12},{4,8},{8,4},{12,0},{1,13},{5,9},{9,5},{13,1},{2,14},{6,10},... | collective-permute-start | bytes 196616 | tf_op jit(solution)/shard_map/ppermute | solution.py:353
  20.3 5.7 %collective-permute-start.7 = (bf16[256,128]{1,0:T(8,128)(2,1)S(1)}, bf16[256,128]{1,0:T(8,128)(2,1)S(1)}, u32[]{:S(2)}, u32[]{:S(2)}) collective-permute-start(bf16[256,128]{1,0:T(8,128)(2,1)S(1)} %get-tuple-element.16), channel_id=1, source_target_pairs={{0,4},{4,0},{8,12},{12,8},{1,5},{5,1},{9,13},{13,9},{2,6},{6,2},{1... | collective-permute-start | bytes 196616 | tf_op jit(solution)/shard_map/ppermute | solution.py:358
  26.3 5.7 %collective-permute-start.10 = (bf16[3,32,128]{2,1,0:T(8,128)(2,1)S(1)}, bf16[3,32,128]{2,1,0:T(8,128)(2,1)S(1)}, u32[]{:S(2)}, u32[]{:S(2)}) collective-permute-start(bf16[3,32,128]{2,1,0:T(8,128)(2,1)S(1)} %get-tuple-element.20), channel_id=1, source_target_pairs={{0,12},{4,8},{8,4},{12,0},{1,13},{5,9},{9,5},{13,1},{2,14},{6,10},... | collective-permute-start | bytes 73736 | tf_op jit(solution)/shard_map/ppermute | solution.py:370
  27.8 4.2 %collective-permute-start.8 = (bf16[3,32,128]{2,1,0:T(8,128)(2,1)S(1)}, bf16[3,32,128]{2,1,0:T(8,128)(2,1)S(1)}, u32[]{:S(2)}, u32[]{:S(2)}) collective-permute-start(bf16[3,32,128]{2,1,0:T(8,128)(2,1)S(1)} %get-tuple-element.18), channel_id=1, source_target_pairs={{0,4},{4,0},{8,12},{12,8},{1,5},{5,1},{9,13},{13,9},{2,6},{6,2},{1... | collective-permute-start | bytes 73736 | tf_op jit(solution)/shard_map/ppermute | solution.py:370
  27.8 4.9 %collective-permute-start.9 = (bf16[3,32,128]{2,1,0:T(8,128)(2,1)S(1)}, bf16[3,32,128]{2,1,0:T(8,128)(2,1)S(1)}, u32[]{:S(2)}, u32[]{:S(2)}) collective-permute-start(bf16[3,32,128]{2,1,0:T(8,128)(2,1)S(1)} %get-tuple-element.19), channel_id=1, source_target_pairs={{0,8},{4,12},{8,0},{12,4},{1,9},{5,13},{9,1},{13,5},{2,10},{6,14},... | collective-permute-start | bytes 73736 | tf_op jit(solution)/shard_map/ppermute | solution.py:370
  32.7 1.4 %collective-permute-start.11 = (bf16[3,4,16,256]{3,2,1,0:T(8,128)(2,1)S(1)}, bf16[3,4,16,256]{3,2,1,0:T(8,128)(2,1)S(1)}, u32[]{:S(2)}, u32[]{:S(2)}) collective-permute-start(bf16[3,4,16,256]{3,2,1,0:T(8,128)(2,1)S(1)} %shard_map.78.cells_ref), channel_id=1, source_target_pairs={{0,1},{1,0},{2,3},{3,2},{4,5},{5,4},{6,7},{7,6},{8,9},{9,8},{10,11... | collective-permute-start | bytes 294920 | tf_op jit(solution)/shard_map/ppermute | solution.py:380

commit v6 on v5

--- a/solution.py
+++ b/solution.py
@@ -141,17 +141,22 @@
         out_ref[i] = jnp.where(upper, ref[:, depth:], ref[:, :depth])
 
 
-def conv_of_clip(clip, got, weight_ref, latents, taps):
+def stack_kernel(own_ref, row_ref, out_ref):
+    out_ref[0] = own_ref[...]
+    out_ref[1] = row_ref[...]
+
+
+def conv_of_clip(clip, near_ref, far_ref, weight_ref, latents, taps):
     spans, spaces, span, rows, cols, depth = latents.shape
     frames, tall = spans * span, spaces * rows
     tm, side, chan = placed_at()
     size = span * rows * cols
     part = pl.ds(pl.multiple_of(clip * size, size), size)
-    for i, ref in enumerate(got):
-        at = side if i < 2 else 1 - side
-        home = (chan if i % 2 == 0 else 1 - chan) == tm // 2
+    for ref, core in ((near_ref, chan), (far_ref, 1 - chan)):
+        home = core == tm // 2
         for j, source in enumerate((jnp.where(home, tm ^ 1, tm ^ 2), jnp.where(home, tm, tm ^ 3))):
-            latents[source, at] = ref[j, part, :].astype(jnp.float32).reshape(latents.shape[2:])
+            for i, at in enumerate((side, 1 - side)):
+                latents[source, at] = ref[i, j, part, :].astype(jnp.float32).reshape(latents.shape[2:])
     column = lax.broadcasted_iota(jnp.int32, (1, cols, depth), 1)
     empty = jnp.zeros((frames, cols, depth), jnp.float32)
     lines = [[empty] * 3]
@@ -181,25 +186,27 @@
     return jnp.where(swapped, upper, lower), jnp.where(swapped, lower, upper)
 
 
-def conv_far_kernel(own_ref, core_ref, row_ref, both_ref, weight_ref, same_ref, other_ref, latents, taps):
+def conv_far_kernel(near_ref, far_ref, weight_ref, keep_ref, sent_ref, latents, taps):
     tm, _, _ = placed_at()
-    got = (own_ref, core_ref, row_ref, both_ref)
-    same, other = conv_of_clip(1 - tm // 2, got, weight_ref, latents, taps)
-    same_ref[...] = same.astype(same_ref.dtype)
-    other_ref[...] = other.astype(other_ref.dtype)
-
-
-def conv_near_kernel(own_ref, core_ref, row_ref, both_ref, weight_ref, keep_ref, other_ref, latents, taps):
+    keep, sent = conv_of_clip(1 - tm // 2, near_ref, far_ref, weight_ref, latents, taps)
+    keep_ref[...] = keep
+    sent_ref[...] = sent.astype(sent_ref.dtype)
+
+
+def conv_near_kernel(near_ref, far_ref, weight_ref, keep_ref, sent_ref, latents, taps):
     tm, _, _ = placed_at()
-    got = (own_ref, core_ref, row_ref, both_ref)
-    keep, other = conv_of_clip(tm // 2, got, weight_ref, latents, taps)
+    keep, sent = conv_of_clip(tm // 2, near_ref, far_ref, weight_ref, latents, taps)
     keep_ref[...] = keep
-    other_ref[...] = other.astype(other_ref.dtype)
+    sent_ref[...] = sent.astype(sent_ref.dtype)
+
+
+def add_kernel(keep_ref, got_ref, out_ref):
+    out_ref[...] = (keep_ref[...] + got_ref[...].astype(jnp.float32)).astype(out_ref.dtype)
 
 
 def norm_kernel(*refs):
-    partial, (bias_ref, gain_ref, shift_ref), sent = refs[:4], refs[4:7], refs[7:11]
-    tiles = refs[11]
+    partial, (bias_ref, gain_ref, shift_ref), sent = refs[:3], refs[3:6], refs[6:10]
+    tiles = refs[10]
     tm, side, _ = placed_at()
     owners, reach, strip, depth = tiles.shape
     cols = 8
@@ -333,29 +340,28 @@
                 target = (source ^ at_home, chan) if home else (source ^ across, 1 - chan)
                 pairs.append((source * chans + chan, target[0] * chans + target[1]))
         got.append(lax.ppermute(cells_in, ("tm", "chan"), pairs))
+    def across(value, axes, m):
+        count = lax.axis_size(axes)
+        return lax.ppermute(value, axes, [(i, i ^ m) for i in range(count)])
+
     weight = run(fetch_kernel, shape(conv_weight.shape, low), [pltpu.SemaphoreType.DMA], conv_weight, moved=4 << 20)
     own = run(select_kernel, shape((2, cells_in.shape[0], depth), low), [], *got, weight, moved=1 << 17)
-    every = [own] + [
-        lax.ppermute(own, ("space", "chan"), [(i, i ^ m) for i in range(spaces * chans)]) for m in range(1, spaces * chans)
-    ]
+    row = across(own, "space", 1)
+    near = run(stack_kernel, shape((spaces,) + own.shape, low), [], own, row, moved=1 << 17)
+    far = across(near, "chan", 1)
 
     count = frames * tall * cols
-    part = shape((count, depth), low)
+    part = [shape((count, depth), full), shape((count, depth), low)]
     scratch = [
         pltpu.VMEM((spans, spaces, span, rows, cols, depth), full),
         pltpu.VMEM((tall // 2 + 2, frames + 2, 2 * cols, 3 * depth), low),
     ]
-    flops = 2 * count * 27 * depth * half
-    far_same, far_other = run(
-        conv_far_kernel, [part, part], scratch, *every, weight, flops=flops, moved=3 << 20
-    )
-    partial = [
-        lax.ppermute(value, "tm", [(i, i ^ m) for i in range(spans)]) for m, value in ((2, far_same), (3, far_other))
-    ]
-    keep, near_other = run(
-        conv_near_kernel, [shape(part.shape, full), part], scratch, *every, weight, flops=flops, moved=3 << 20
-    )
-    partial = [keep] + partial + [lax.ppermute(near_other, "tm", [(i, i ^ 1) for i in range(spans)])]
+    cost = {"flops": 2 * count * 27 * depth * half, "moved": 3 << 20}
+    far_keep, far_sent = run(conv_far_kernel, part, scratch, near, far, weight, **cost)
+    far_got = across(far_sent, "tm", 1)
+    keep, sent = run(conv_near_kernel, part, scratch, near, far, weight, **cost)
+    summed = run(add_kernel, part[1], [], far_keep, far_got, moved=1 << 18)
+    partial = [keep, across(summed, "tm", 2), across(sent, "tm", 1)]
 
     tile = shape((rows + 1, (width + 2) * frames, depth), low)
     tiles = run(
@@ -366,9 +372,7 @@
         *(vector.reshape(los, depth) for vector in (conv_bias, gn_gain, gn_shift)),
         moved=1 << 19,
     )
-    tiles = [tiles[0]] + [
-        lax.ppermute(tiles[m], "tm", [(i, i ^ m) for i in range(spans)]) for m in range(1, spans)
-    ]
+    tiles = [tiles[0]] + [across(tiles[m], "tm", m) for m in range(1, spans)]
 
     near = run(
         cells_kernel,

time: 35.5 us -> 38 us (1.070)
  waiting for transfers between devices: 10.6 us -> 15.1 us
  starting transfers between devices: 19.2 us -> 17.2 us
    ppermute x9 -> x8, waiting for transfers between devices: 9.84 us -> 14.3 us  [across(): return lax.ppermute(value, axes, [(i, i ^ m) for i in range(count)])]
    ppermute x9 -> x8, starting transfers between devices: 14.7 us -> 12.7 us  [across(): return lax.ppermute(value, axes, [(i, i ^ m) for i in range(count)])]
    pallas_call x8 -> x10, Pallas kernels: 3.79 us -> 3.8 us  [run(): pl.pallas_call(kernel, out_shape=shapes, in_specs=[vmem] * len(operands),...]
  transfers between devices with their start and end apart: 12 -> 11, of which waited for: 7 -> 8; matrix products, arithmetic and copies ran while one was open for 0% -> 0% of each run, Pallas kernels for 4% -> 4%
where the time goes in v6:
time: 38 us; the launch traced here: 37.8 us
  starting transfers between devices  17.2 us (45%)
  waiting for transfers between devices  15.1 us (40%)
  Pallas kernels  3.8 us (10%)
  local copies, waits for them, and re-layouts  1.5 us (4%)
    ppermute x8, waiting for transfers between devices, across(): return lax.ppermute(value, axes, [(i, i ^ m) for i in range(count)])  14.3 us
    ppermute x8, starting transfers between devices, across(): return lax.ppermute(value, axes, [(i, i ^ m) for i in range(count)])  12.7 us
    ppermute x2, starting transfers between devices, small_plan(): got.append(lax.ppermute(cells_in, ('tm', 'chan'), pairs))  4.43 us
    pallas_call x10, Pallas kernels, run(): pl.pallas_call(kernel, out_shape=shapes, in_specs=[vmem] * len(operands),...  3.8 us
    unnamed x12, local copies, waits for them, and re-layouts  1.5 us
    ppermute x1, waiting for transfers between devices, small_plan(): far = lax.ppermute(near, 'chan', flip)  0.77 us
  transfers between devices with their start and end apart: 11, of which 8 were waited for; matrix products, arithmetic and copies ran while one was open for 0% of the time, Pallas kernels for 4%

profile of v6, /device:TPU:0, one launch (start us, length us, event | category | flops | bytes accessed | tf_op | source)
XLA Modules:
  0.0 37.8 jit_solution(14217262570717318922)
XLA Ops:
  0.0 3.0 %collective-permute-start = (bf16[64,256]{1,0:T(8,128)(2,1)}, bf16[64,256]{1,0:T(8,128)(2,1)S(1)}, u32[]{:S(2)}, u32[]{:S(2)}) collective-permute-start(bf16[64,256]{1,0:T(8,128)(2,1)} %bitcast.9), channel_id=1, source_target_pairs={{0,4},{1,8},{4,0},{5,12},{8,1},{9,13},{12,5},{13,9},{2,6},{3,10},{... | collective-permute-start | bytes 98312 | tf_op jit(solution)/shard_map/ppermute | solution.py:342
  3.0 1.4 %collective-permute-start.1 = (bf16[64,256]{1,0:T(8,128)(2,1)}, bf16[64,256]{1,0:T(8,128)(2,1)S(1)}, u32[]{:S(2)}, u32[]{:S(2)}) collective-permute-start(bf16[64,256]{1,0:T(8,128)(2,1)} %bitcast.10), channel_id=1, source_target_pairs={{0,0},{1,12},{4,4},{5,8},{8,5},{9,9},{12,1},{13,13},{2,2},{3,14},{... | collective-permute-start | bytes 98312 | tf_op jit(solution)/shard_map/ppermute | solution.py:342
  4.4 0.0 copy-start.1
  4.4 1.5 %copy-done.1 = bf16[3,3,3,128,256]{4,3,2,1,0:T(8,128)(2,1)S(1)} copy-done((bf16[3,3,3,128,256]{4,3,2,1,0:T(8,128)(2,1)S(1)}, bf16[3,3,3,128,256]{4,3,2,1,0:T(8,128)(2,1)}, u32[]{:S(2)}) %copy-start.1) | copy-done | bytes 1769496
  5.9 0.4 shard_map.73.after_ref.weight_ref
  6.3 0.0 collective-permute-done.first_ref
  6.3 0.0 collective-permute-done.1.second_ref
  6.3 1.6 %collective-permute-start.2 = (bf16[2,64,128]{2,1,0:T(8,128)(2,1)S(1)}, bf16[2,64,128]{2,1,0:T(8,128)(2,1)S(1)}, u32[]{:S(2)}, u32[]{:S(2)}) collective-permute-start(bf16[2,64,128]{2,1,0:T(8,128)(2,1)S(1)} %shard_map.74.own_ref), channel_id=1, source_target_pairs={{0,2},{2,0},{1,3},{3,1},{4,6},{6,4},{5,7},{7,5},{8,10},{10,8},{9,1... | collective-permute-start | bytes 98312 | tf_op jit(solution)/shard_map/ppermute | solution.py:345
  7.9 2.4 %collective-permute-done.2.row_ref = bf16[2,64,128]{2,1,0:T(8,128)(2,1)S(1)} collective-permute-done((bf16[2,64,128]{2,1,0:T(8,128)(2,1)S(1)}, bf16[2,64,128]{2,1,0:T(8,128)(2,1)S(1)}, u32[]{:S(2)}, u32[]{:S(2)}) %collective-permute-start.2) | collective-permute-done | bytes 32800 | tf_op jit(solution)/shard_map/ppermute | solution.py:345
  10.3 0.0 copy-start.3
  10.3 0.0 copy-start.4
  10.3 0.0 copy-start.5
  10.3 4.0 %collective-permute-start.3 = (bf16[2,2,64,128]{3,2,1,0:T(8,128)(2,1)S(1)}, bf16[2,2,64,128]{3,2,1,0:T(8,128)(2,1)S(1)}, u32[]{:S(2)}, u32[]{:S(2)}) collective-permute-start(bf16[2,2,64,128]{3,2,1,0:T(8,128)(2,1)S(1)} %shard_map.75.near_ref), channel_id=1, source_target_pairs={{0,1},{1,0},{2,3},{3,2},{4,5},{5,4},{6,7},{7,6},{8,9},{9,8},{10,11... | collective-permute-start | bytes 196616 | tf_op jit(solution)/shard_map/ppermute | solution.py:345
  14.3 0.9 %collective-permute-done.3.far_ref = bf16[2,2,64,128]{3,2,1,0:T(8,128)(2,1)S(1)} collective-permute-done((bf16[2,2,64,128]{3,2,1,0:T(8,128)(2,1)S(1)}, bf16[2,2,64,128]{3,2,1,0:T(8,128)(2,1)S(1)}, u32[]{:S(2)}, u32[]{:S(2)}) %collective-permute-start.3) | collective-permute-done | bytes 65568 | tf_op jit(solution)/shard_map/ppermute | solution.py:345
  15.2 0.7 %shard_map.77 = (f32[256,128]{1,0:T(8,128)S(1)}, bf16[256,128]{1,0:T(8,128)(2,1)S(1)}) custom-call(bf16[2,2,64,128]{3,2,1,0:T(8,128)(2,1)S(1)} %shard_map.75.near_ref, bf16[2,2,64,128]{3,2,1,0:T(8,128)(2,1)S(1)} %collective-permute-done.3.far_ref, bf16[3,3,3,128,256]{4,3,2,1,0:T(8,128)(2,1)S(1)} %shard_map.73.after_ref.weight_ref), custom_call_target="tpu_custom_call" | custom-call | flops 452984832 | bytes 3145728 | tf_op jit(solution)/shard_map/pallas_call | solution.py:312
  15.9 0.0 copy-start
  15.9 0.0 copy-start.2
  16.0 0.1 collective-permute-start.4
  16.0 0.7 %shard_map.76 = (f32[256,128]{1,0:T(8,128)S(1)}, bf16[256,128]{1,0:T(8,128)(2,1)S(1)}) custom-call(bf16[2,2,64,128]{3,2,1,0:T(8,128)(2,1)S(1)} %shard_map.75.near_ref, bf16[2,2,64,128]{3,2,1,0:T(8,128)(2,1)S(1)} %collective-permute-done.3.far_ref, bf16[3,3,3,128,256]{4,3,2,1,0:T(8,128)(2,1)S(1)} %shard_map.73.after_ref.weight_ref), custom_call_target="tpu_custom_call" | custom-call | flops 452984832 | bytes 3145728 | tf_op jit(solution)/shard_map/pallas_call | solution.py:312
  16.7 2.1 %collective-permute-start.6 = (bf16[256,128]{1,0:T(8,128)(2,1)S(1)}, bf16[256,128]{1,0:T(8,128)(2,1)S(1)}, u32[]{:S(2)}, u32[]{:S(2)}) collective-permute-start(bf16[256,128]{1,0:T(8,128)(2,1)S(1)} %get-tuple-element.16), channel_id=1, source_target_pairs={{0,4},{4,0},{8,12},{12,8},{1,5},{5,1},{9,13},{13,9},{2,6},{6,2},{1... | collective-permute-start | bytes 196616 | tf_op jit(solution)/shard_map/ppermute | solution.py:345
  18.8 2.1 %collective-permute-done.4.got_ref = bf16[256,128]{1,0:T(8,128)(2,1)S(1)} collective-permute-done((bf16[256,128]{1,0:T(8,128)(2,1)S(1)}, bf16[256,128]{1,0:T(8,128)(2,1)S(1)}, u32[]{:S(2)}, u32[]{:S(2)}) %collective-permute-start.4) | collective-permute-done | bytes 65568 | tf_op jit(solution)/shard_map/ppermute | solution.py:345
  20.9 0.6 %collective-permute-start.5 = (bf16[256,128]{1,0:T(8,128)(2,1)S(1)}, bf16[256,128]{1,0:T(8,128)(2,1)S(1)}, u32[]{:S(2)}, u32[]{:S(2)}) collective-permute-start(bf16[256,128]{1,0:T(8,128)(2,1)S(1)} %shard_map.78), channel_id=1, source_target_pairs={{0,8},{4,12},{8,0},{12,4},{1,9},{5,13},{9,1},{13,5},{2,10},{6,14},... | collective-permute-start | bytes 196616 | tf_op jit(solution)/shard_map/ppermute | solution.py:345
  21.6 0.2 collective-permute-done.6.refs_2_
  21.8 4.6 %collective-permute-done.5.refs_1_ = bf16[256,128]{1,0:T(8,128)(2,1)S(1)} collective-permute-done((bf16[256,128]{1,0:T(8,128)(2,1)S(1)}, bf16[256,128]{1,0:T(8,128)(2,1)S(1)}, u32[]{:S(2)}, u32[]{:S(2)}) %collective-permute-start.5) | collective-permute-done | bytes 65568 | tf_op jit(solution)/shard_map/ppermute | solution.py:345
  26.4 0.0 copy-done.3
  26.4 0.0 copy-done.4
  26.4 0.0 copy-done.5
  26.4 0.3 shard_map.79
  26.7 0.1 collective-permute-start.7
  26.8 2.8 %collective-permute-start.8 = (bf16[3,32,128]{2,1,0:T(8,128)(2,1)S(1)}, bf16[3,32,128]{2,1,0:T(8,128)(2,1)S(1)}, u32[]{:S(2)}, u32[]{:S(2)}) collective-permute-start(bf16[3,32,128]{2,1,0:T(8,128)(2,1)S(1)} %get-tuple-element.19), channel_id=1, source_target_pairs={{0,8},{4,12},{8,0},{12,4},{1,9},{5,13},{9,1},{13,5},{2,10},{6,14},... | collective-permute-start | bytes 73736 | tf_op jit(solution)/shard_map/ppermute | solution.py:345
  29.6 1.6 %collective-permute-start.9 = (bf16[3,32,128]{2,1,0:T(8,128)(2,1)S(1)}, bf16[3,32,128]{2,1,0:T(8,128)(2,1)S(1)}, u32[]{:S(2)}, u32[]{:S(2)}) collective-permute-start(bf16[3,32,128]{2,1,0:T(8,128)(2,1)S(1)} %get-tuple-element.20), channel_id=1, source_target_pairs={{0,12},{4,8},{8,4},{12,0},{1,13},{5,9},{9,5},{13,1},{2,14},{6,10},... | collective-permute-start | bytes 73736 | tf_op jit(solution)/shard_map/ppermute | solution.py:345
  31.2 0.0 collective-permute-done.7.refs_1_
  31.2 0.6 %collective-permute-done.8.refs_2_ = bf16[3,32,128]{2,1,0:T(8,128)(2,1)S(1)} collective-permute-done((bf16[3,32,128]{2,1,0:T(8,128)(2,1)S(1)}, bf16[3,32,128]{2,1,0:T(8,128)(2,1)S(1)}, u32[]{:S(2)}, u32[]{:S(2)}) %collective-permute-start.8) | collective-permute-done | bytes 24608 | tf_op jit(solution)/shard_map/ppermute | solution.py:345
  31.8 3.4 %collective-permute-done.9.refs_3_ = bf16[3,32,128]{2,1,0:T(8,128)(2,1)S(1)} collective-permute-done((bf16[3,32,128]{2,1,0:T(8,128)(2,1)S(1)}, bf16[3,32,128]{2,1,0:T(8,128)(2,1)S(1)}, u32[]{:S(2)}, u32[]{:S(2)}) %collective-permute-start.9) | collective-permute-done | bytes 24608 | tf_op jit(solution)/shard_map/ppermute | solution.py:345
  35.2 0.1 collective-permute-start.10
  35.3 0.0 copy-done
  35.3 0.0 copy-done.2
  35.3 0.5 %shard_map.81.total_ref = f32[256,256]{1,0:T(8,128)S(1)} custom-call(bf16[3,4,16,256]{3,2,1,0:T(8,128)(2,1)S(1)} %shard_map.80.cells_ref, bf16[3,3,512,256]{3,2,1,0:T(8,128)(2,1)S(1)} %copy-done, f32[1,256]{1,0:T(1,128)S(1)} %bitcast.5), custom_call_target="tpu_custom_call" | custom-call | flops 301989888 | bytes 2097152 | tf_op jit(solution)/shard_map/pallas_call | solution.py:312
  35.8 0.8 %collective-permute-done.10.cells_ref = bf16[3,4,16,256]{3,2,1,0:T(8,128)(2,1)S(1)} collective-permute-done((bf16[3,4,16,256]{3,2,1,0:T(8,128)(2,1)S(1)}, bf16[3,4,16,256]{3,2,1,0:T(8,128)(2,1)S(1)}, u32[]{:S(2)}, u32[]{:S(2)}) %collective-permute-start.10) | collective-permute-done | bytes 98336 | tf_op jit(solution)/shard_map/ppermute | solution.py:384
  36.6 1.2 %shard_map.82 = bf16[2,8,4,4,256]{4,3,2,1,0:T(4,128)(2,1)} custom-call(bf16[3,4,16,256]{3,2,1,0:T(8,128)(2,1)S(1)} %collective-permute-done.10.cells_ref, bf16[3,3,512,256]{3,2,1,0:T(8,128)(2,1)S(1)} %copy-done, f32[256,256]{1,0:T(8,128)S(1)} %shard_map.81.total_ref), custom_call_target="tpu_custom_call" | custom-call | flops 301989888 | bytes 2097152 | tf_op jit(solution)/shard_map/pallas_call | solution.py:312
  (4 shorter events, 0.1 us)
Async XLA Ops:
  0.0 6.3 %collective-permute-start = (bf16[64,256]{1,0:T(8,128)(2,1)}, bf16[64,256]{1,0:T(8,128)(2,1)S(1)}, u32[]{:S(2)}, u32[]{:S(2)}) collective-permute-start(bf16[64,256]{1,0:T(8,128)(2,1)} %bitcast.9), channel_id=1, source_target_pairs={{0,4},{1,8},{4,0},{5,12},{8,1},{9,13},{12,5},{13,9},{2,6},{3,10},{... | collective-permute-start | bytes 98312 | tf_op jit(solution)/shard_map/ppermute | solution.py:342
  3.0 3.3 %collective-permute-start.1 = (bf16[64,256]{1,0:T(8,128)(2,1)}, bf16[64,256]{1,0:T(8,128)(2,1)S(1)}, u32[]{:S(2)}, u32[]{:S(2)}) collective-permute-start(bf16[64,256]{1,0:T(8,128)(2,1)} %bitcast.10), channel_id=1, source_target_pairs={{0,0},{1,12},{4,4},{5,8},{8,5},{9,9},{12,1},{13,13},{2,2},{3,14},{... | collective-permute-start | bytes 98312 | tf_op jit(solution)/shard_map/ppermute | solution.py:342
  4.4 1.5 %copy-start.1 = (bf16[3,3,3,128,256]{4,3,2,1,0:T(8,128)(2,1)S(1)}, bf16[3,3,3,128,256]{4,3,2,1,0:T(8,128)(2,1)}, u32[]{:S(2)}) copy-start(bf16[3,3,3,128,256]{4,3,2,1,0:T(8,128)(2,1)} %weight_ref.3) | copy-start | bytes 5308420
  6.3 4.0 %collective-permute-start.2 = (bf16[2,64,128]{2,1,0:T(8,128)(2,1)S(1)}, bf16[2,64,128]{2,1,0:T(8,128)(2,1)S(1)}, u32[]{:S(2)}, u32[]{:S(2)}) collective-permute-start(bf16[2,64,128]{2,1,0:T(8,128)(2,1)S(1)} %shard_map.74.own_ref), channel_id=1, source_target_pairs={{0,2},{2,0},{1,3},{3,1},{4,6},{6,4},{5,7},{7,5},{8,10},{10,8},{9,1... | collective-permute-start | bytes 98312 | tf_op jit(solution)/shard_map/ppermute | solution.py:345
  10.3 16.1 %copy-start.3 = (f32[256]{0:T(256)S(1)}, f32[256]{0:T(256)}, u32[]{:S(2)}) copy-start(f32[256]{0:T(256)} %param.9) | copy-start | bytes 3076
  10.3 16.1 %copy-start.4 = (f32[256]{0:T(256)S(1)}, f32[256]{0:T(256)}, u32[]{:S(2)}) copy-start(f32[256]{0:T(256)} %param.10) | copy-start | bytes 3076
  10.3 16.1 %copy-start.5 = (f32[256]{0:T(256)S(1)}, f32[256]{0:T(256)}, u32[]{:S(2)}) copy-start(f32[256]{0:T(256)} %param.11) | copy-start | bytes 3076
  10.3 4.9 %collective-permute-start.3 = (bf16[2,2,64,128]{3,2,1,0:T(8,128)(2,1)S(1)}, bf16[2,2,64,128]{3,2,1,0:T(8,128)(2,1)S(1)}, u32[]{:S(2)}, u32[]{:S(2)}) collective-permute-start(bf16[2,2,64,128]{3,2,1,0:T(8,128)(2,1)S(1)} %shard_map.75.near_ref), channel_id=1, source_target_pairs={{0,1},{1,0},{2,3},{3,2},{4,5},{5,4},{6,7},{7,6},{8,9},{9,8},{10,11... | collective-permute-start | bytes 196616 | tf_op jit(solution)/shard_map/ppermute | solution.py:345
  15.9 19.4 %copy-start = (bf16[3,3,512,256]{3,2,1,0:T(8,128)(2,1)S(1)}, bf16[3,3,512,256]{3,2,1,0:T(8,128)(2,1)}, u32[]{:S(2)}) copy-start(bf16[3,3,512,256]{3,2,1,0:T(8,128)(2,1)} %weight_ref.5) | copy-start | bytes 7077892
  15.9 19.4 %copy-start.2 = (f32[256]{0:T(256)S(1)}, f32[256]{0:T(256)}, u32[]{:S(2)}) copy-start(f32[256]{0:T(256)} %param.13) | copy-start | bytes 3076
  16.0 5.0 %collective-permute-start.4 = (bf16[256,128]{1,0:T(8,128)(2,1)S(1)}, bf16[256,128]{1,0:T(8,128)(2,1)S(1)}, u32[]{:S(2)}, u32[]{:S(2)}) collective-permute-start(bf16[256,128]{1,0:T(8,128)(2,1)S(1)} %get-tuple-element.15), channel_id=1, source_target_pairs={{0,4},{4,0},{8,12},{12,8},{1,5},{5,1},{9,13},{13,9},{2,6},{6,2},{1... | collective-permute-start | bytes 196616 | tf_op jit(solution)/shard_map/ppermute | solution.py:345
  16.7 5.0 %collective-permute-start.6 = (bf16[256,128]{1,0:T(8,128)(2,1)S(1)}, bf16[256,128]{1,0:T(8,128)(2,1)S(1)}, u32[]{:S(2)}, u32[]{:S(2)}) collective-permute-start(bf16[256,128]{1,0:T(8,128)(2,1)S(1)} %get-tuple-element.16), channel_id=1, source_target_pairs={{0,4},{4,0},{8,12},{12,8},{1,5},{5,1},{9,13},{13,9},{2,6},{6,2},{1... | collective-permute-start | bytes 196616 | tf_op jit(solution)/shard_map/ppermute | solution.py:345
  20.9 5.4 %collective-permute-start.5 = (bf16[256,128]{1,0:T(8,128)(2,1)S(1)}, bf16[256,128]{1,0:T(8,128)(2,1)S(1)}, u32[]{:S(2)}, u32[]{:S(2)}) collective-permute-start(bf16[256,128]{1,0:T(8,128)(2,1)S(1)} %shard_map.78), channel_id=1, source_target_pairs={{0,8},{4,12},{8,0},{12,4},{1,9},{5,13},{9,1},{13,5},{2,10},{6,14},... | collective-permute-start | bytes 196616 | tf_op jit(solution)/shard_map/ppermute | solution.py:345
  26.7 4.5 %collective-permute-start.7 = (bf16[3,32,128]{2,1,0:T(8,128)(2,1)S(1)}, bf16[3,32,128]{2,1,0:T(8,128)(2,1)S(1)}, u32[]{:S(2)}, u32[]{:S(2)}) collective-permute-start(bf16[3,32,128]{2,1,0:T(8,128)(2,1)S(1)} %get-tuple-element.18), channel_id=1, source_target_pairs={{0,4},{4,0},{8,12},{12,8},{1,5},{5,1},{9,13},{13,9},{2,6},{6,2},{1... | collective-permute-start | bytes 73736 | tf_op jit(solution)/shard_map/ppermute | solution.py:345
  26.8 5.0 %collective-permute-start.8 = (bf16[3,32,128]{2,1,0:T(8,128)(2,1)S(1)}, bf16[3,32,128]{2,1,0:T(8,128)(2,1)S(1)}, u32[]{:S(2)}, u32[]{:S(2)}) collective-permute-start(bf16[3,32,128]{2,1,0:T(8,128)(2,1)S(1)} %get-tuple-element.19), channel_id=1, source_target_pairs={{0,8},{4,12},{8,0},{12,4},{1,9},{5,13},{9,1},{13,5},{2,10},{6,14},... | collective-permute-start | bytes 73736 | tf_op jit(solution)/shard_map/ppermute | solution.py:345
  29.6 5.6 %collective-permute-start.9 = (bf16[3,32,128]{2,1,0:T(8,128)(2,1)S(1)}, bf16[3,32,128]{2,1,0:T(8,128)(2,1)S(1)}, u32[]{:S(2)}, u32[]{:S(2)}) collective-permute-start(bf16[3,32,128]{2,1,0:T(8,128)(2,1)S(1)} %get-tuple-element.20), channel_id=1, source_target_pairs={{0,12},{4,8},{8,4},{12,0},{1,13},{5,9},{9,5},{13,1},{2,14},{6,10},... | collective-permute-start | bytes 73736 | tf_op jit(solution)/shard_map/ppermute | solution.py:345
  35.2 1.4 %collective-permute-start.10 = (bf16[3,4,16,256]{3,2,1,0:T(8,128)(2,1)S(1)}, bf16[3,4,16,256]{3,2,1,0:T(8,128)(2,1)S(1)}, u32[]{:S(2)}, u32[]{:S(2)}) collective-permute-start(bf16[3,4,16,256]{3,2,1,0:T(8,128)(2,1)S(1)} %shard_map.80.cells_ref), channel_id=1, source_target_pairs={{0,1},{1,0},{2,3},{3,2},{4,5},{5,4},{6,7},{7,6},{8,9},{9,8},{10,11... | collective-permute-start | bytes 294920 | tf_op jit(solution)/shard_map/ppermute | solution.py:384

commit v7 on v6

--- a/solution.py
+++ b/solution.py
@@ -132,13 +132,20 @@
     copy.wait()
 
 
-def select_kernel(first_ref, second_ref, after_ref, out_ref):
+def relay_kernel(got_ref, after_ref, out_ref):
     del after_ref
     tm, _, _ = placed_at()
+    depth = out_ref.shape[1]
+    out_ref[...] = jnp.where(tm % 2 > 0, got_ref[:, :depth], got_ref[:, depth:])
+
+
+def select_kernel(own_ref, got_ref, passed_ref, out_ref):
+    tm, _, chan = placed_at()
     depth = out_ref.shape[2]
-    upper = tm % 2 > 0
-    for i, ref in enumerate((first_ref, second_ref)):
-        out_ref[i] = jnp.where(upper, ref[:, depth:], ref[:, :depth])
+    upper, home = tm % 2 > 0, chan == tm // 2
+    out_ref[0] = jnp.where(upper, got_ref[:, depth:], got_ref[:, :depth])
+    own = jnp.where(upper, own_ref[:, depth:], own_ref[:, :depth])
+    out_ref[1] = jnp.where(home, own, passed_ref[...])
 
 
 def stack_kernel(own_ref, row_ref, out_ref):
@@ -186,27 +193,23 @@
     return jnp.where(swapped, upper, lower), jnp.where(swapped, lower, upper)
 
 
-def conv_far_kernel(near_ref, far_ref, weight_ref, keep_ref, sent_ref, latents, taps):
+def conv_far_kernel(near_ref, far_ref, weight_ref, same_ref, other_ref, latents, taps):
     tm, _, _ = placed_at()
-    keep, sent = conv_of_clip(1 - tm // 2, near_ref, far_ref, weight_ref, latents, taps)
+    same, other = conv_of_clip(1 - tm // 2, near_ref, far_ref, weight_ref, latents, taps)
+    same_ref[...] = same.astype(same_ref.dtype)
+    other_ref[...] = other.astype(other_ref.dtype)
+
+
+def conv_near_kernel(near_ref, far_ref, weight_ref, keep_ref, other_ref, latents, taps):
+    tm, _, _ = placed_at()
+    keep, other = conv_of_clip(tm // 2, near_ref, far_ref, weight_ref, latents, taps)
     keep_ref[...] = keep
-    sent_ref[...] = sent.astype(sent_ref.dtype)
-
-
-def conv_near_kernel(near_ref, far_ref, weight_ref, keep_ref, sent_ref, latents, taps):
-    tm, _, _ = placed_at()
-    keep, sent = conv_of_clip(tm // 2, near_ref, far_ref, weight_ref, latents, taps)
-    keep_ref[...] = keep
-    sent_ref[...] = sent.astype(sent_ref.dtype)
-
-
-def add_kernel(keep_ref, got_ref, out_ref):
-    out_ref[...] = (keep_ref[...] + got_ref[...].astype(jnp.float32)).astype(out_ref.dtype)
+    other_ref[...] = other.astype(other_ref.dtype)
 
 
 def norm_kernel(*refs):
-    partial, (bias_ref, gain_ref, shift_ref), sent = refs[:3], refs[3:6], refs[6:10]
-    tiles = refs[10]
+    partial, (bias_ref, gain_ref, shift_ref) = refs[:4], refs[4:7]
+    keep_ref, next_ref, cross_ref, tiles = refs[7:]
     tm, side, _ = placed_at()
     owners, reach, strip, depth = tiles.shape
     cols = 8
@@ -241,15 +244,21 @@
             for j in range(owner * width - 1, (owner + 1) * width + 1):
                 picked.append(chosen[j] if 0 <= j < cols else empty)
             tiles[owner, i] = jnp.concatenate(picked, axis=0).astype(tiles.dtype)
-    for m in range(owners):
-        sent[m][...] = tiles[tm ^ m]
-
-
-def cells_kernel(*refs):
-    got, cells_ref, tiles = refs[:4], refs[4], refs[5]
+    keep_ref[...] = tiles[tm]
+    next_ref[...] = tiles[tm ^ 1]
+    for m in (2, 3):
+        cross_ref[m - 2] = tiles[tm ^ m]
+
+
+def hand_kernel(following_ref, crossed_ref, out_ref):
+    out_ref[0] = following_ref[...]
+    out_ref[1] = crossed_ref[1]
+
+
+def cells_kernel(kept_ref, crossed_ref, handed_ref, cells_ref, tiles):
     tm, _, _ = placed_at()
-    for m in range(len(got)):
-        tiles[tm ^ m] = got[m][...].astype(jnp.float32)
+    for m, value in enumerate((kept_ref[...], handed_ref[0], crossed_ref[0], handed_ref[1])):
+        tiles[tm ^ m] = value.astype(jnp.float32)
     reach, wide, tall, half = cells_ref.shape
     depth = tiles.shape[3]
     los = half // depth
@@ -330,22 +339,24 @@
     flip = ((0, 1), (1, 0))
 
     cells_in = latents.reshape(clips * span * rows * cols, half)
-    turns = ((1, 2), (0, 3))
-    got = []
-    for at_home, across in turns:
-        pairs = []
-        for source in range(spans):
-            for chan in range(chans):
-                home = chan == source // 2
-                target = (source ^ at_home, chan) if home else (source ^ across, 1 - chan)
-                pairs.append((source * chans + chan, target[0] * chans + target[1]))
-        got.append(lax.ppermute(cells_in, ("tm", "chan"), pairs))
+    first, second = [], []
+    for source in range(spans):
+        for chan in range(chans):
+            home = chan == source // 2
+            target = (source ^ 1, chan) if home else (source ^ 2, 1 - chan)
+            first.append((source * chans + chan, target[0] * chans + target[1]))
+            if not home:
+                second.append((source * chans + chan, (source ^ 1) * chans + chan))
+    got = lax.ppermute(cells_in, ("tm", "chan"), first)
+    weight = run(fetch_kernel, shape(conv_weight.shape, low), [pltpu.SemaphoreType.DMA], conv_weight, moved=4 << 20)
+    relayed = run(relay_kernel, shape((cells_in.shape[0], depth), low), [], got, weight, moved=1 << 17)
+    passed = lax.ppermute(relayed, ("tm", "chan"), second)
+
     def across(value, axes, m):
         count = lax.axis_size(axes)
         return lax.ppermute(value, axes, [(i, i ^ m) for i in range(count)])
 
-    weight = run(fetch_kernel, shape(conv_weight.shape, low), [pltpu.SemaphoreType.DMA], conv_weight, moved=4 << 20)
-    own = run(select_kernel, shape((2, cells_in.shape[0], depth), low), [], *got, weight, moved=1 << 17)
+    own = run(select_kernel, shape((2, cells_in.shape[0], depth), low), [], cells_in, got, passed, moved=1 << 17)
     row = across(own, "space", 1)
     near = run(stack_kernel, shape((spaces,) + own.shape, low), [], own, row, moved=1 << 17)
     far = across(near, "chan", 1)
@@ -357,22 +368,23 @@
         pltpu.VMEM((tall // 2 + 2, frames + 2, 2 * cols, 3 * depth), low),
     ]
     cost = {"flops": 2 * count * 27 * depth * half, "moved": 3 << 20}
-    far_keep, far_sent = run(conv_far_kernel, part, scratch, near, far, weight, **cost)
-    far_got = across(far_sent, "tm", 1)
-    keep, sent = run(conv_near_kernel, part, scratch, near, far, weight, **cost)
-    summed = run(add_kernel, part[1], [], far_keep, far_got, moved=1 << 18)
-    partial = [keep, across(summed, "tm", 2), across(sent, "tm", 1)]
+    far_same, far_other = run(conv_far_kernel, [part[1], part[1]], scratch, near, far, weight, **cost)
+    partial = [across(far_same, "tm", 2), across(far_other, "tm", 3)]
+    keep, near_other = run(conv_near_kernel, part, scratch, near, far, weight, **cost)
+    partial = [keep] + partial + [across(near_other, "tm", 1)]
 
     tile = shape((rows + 1, (width + 2) * frames, depth), low)
-    tiles = run(
+    kept, following, crossing = run(
         norm_kernel,
-        [tile] * spans,
+        [tile, tile, shape((2,) + tile.shape, low)],
         [pltpu.VMEM((spans,) + tile.shape, low)],
         *partial,
         *(vector.reshape(los, depth) for vector in (conv_bias, gn_gain, gn_shift)),
         moved=1 << 19,
     )
-    tiles = [tiles[0]] + [across(tiles[m], "tm", m) for m in range(1, spans)]
+    crossed = across(crossing, "tm", 2)
+    handed = run(hand_kernel, shape((2,) + tile.shape, low), [], following, crossed, moved=1 << 17)
+    tiles = [kept, crossed, across(handed, "tm", 1)]
 
     near = run(
         cells_kernel,

time: 38 us -> 40.3 us (1.061)
  starting transfers between devices: 17.2 us -> 18.9 us
  waiting for transfers between devices: 15.1 us -> 15.7 us
    ppermute x8 -> x7, starting transfers between devices: 12.7 us -> 15.2 us  [across(): return lax.ppermute(value, axes, [(i, i ^ m) for i in range(count)])]
    ppermute x2, starting transfers between devices: 4.43 us -> 3.69 us  [the longest x1 3.02 us: small_plan(): got = lax.ppermute(cells_in, ('tm', 'chan'), first)]
    ppermute x8 -> x7, waiting for transfers between devices: 14.3 us -> 14.7 us  [across(): return lax.ppermute(value, axes, [(i, i ^ m) for i in range(count)])]
    unnamed x12 -> x14, local copies, waits for them, and re-layouts: 1.5 us -> 1.51 us
    pallas_call x10 -> x11, Pallas kernels: 3.8 us -> 3.8 us  [run(): pl.pallas_call(kernel, out_shape=shapes, in_specs=[vmem] * len(operands),...]
  transfers between devices with their start and end apart: 11 -> 10, of which waited for: 8 -> 9; matrix products, arithmetic and copies ran while one was open for 0% -> 0% of each run, Pallas kernels for 4% -> 4%
where the time goes in v7:
time: 40.3 us; the launch traced here: 40.1 us
  starting transfers between devices  18.9 us (47%)
  waiting for transfers between devices  15.7 us (39%)
  Pallas kernels  3.8 us (9%)
  local copies, waits for them, and re-layouts  1.51 us (4%)
    ppermute x7, starting transfers between devices, across(): return lax.ppermute(value, axes, [(i, i ^ m) for i in range(count)])  15.2 us
    ppermute x7, waiting for transfers between devices, across(): return lax.ppermute(value, axes, [(i, i ^ m) for i in range(count)])  14.7 us
    pallas_call x11, Pallas kernels, run(): pl.pallas_call(kernel, out_shape=shapes, in_specs=[vmem] * len(operands),...  3.8 us
    ppermute x1, starting transfers between devices, small_plan(): got = lax.ppermute(cells_in, ('tm', 'chan'), first)  3.02 us
    unnamed x14, local copies, waits for them, and re-layouts  1.51 us
  transfers between devices with their start and end apart: 10, of which 9 were waited for; matrix products, arithmetic and copies ran while one was open for 0% of the time, Pallas kernels for 4%

profile of v7, /device:TPU:0, one launch (start us, length us, event | category | flops | bytes accessed | tf_op | source)
XLA Modules:
  0.0 40.1 jit_solution(13961231468378387572)
XLA Ops:
  0.0 3.0 %collective-permute-start = (bf16[64,256]{1,0:T(8,128)(2,1)}, bf16[64,256]{1,0:T(8,128)(2,1)S(1)}, u32[]{:S(2)}, u32[]{:S(2)}) collective-permute-start(bf16[64,256]{1,0:T(8,128)(2,1)} %bitcast.5), channel_id=1, source_target_pairs={{0,4},{1,8},{4,0},{5,12},{8,1},{9,13},{12,5},{13,9},{2,6},{3,10},{... | collective-permute-start | bytes 98312 | tf_op jit(solution)/shard_map/ppermute | solution.py:350
  3.0 0.0 copy-start.1
  3.0 1.5 %copy-done.1 = bf16[3,3,3,128,256]{4,3,2,1,0:T(8,128)(2,1)S(1)} copy-done((bf16[3,3,3,128,256]{4,3,2,1,0:T(8,128)(2,1)S(1)}, bf16[3,3,3,128,256]{4,3,2,1,0:T(8,128)(2,1)}, u32[]{:S(2)}) %copy-start.1) | copy-done | bytes 1769496
  4.5 0.4 shard_map.73.after_ref.weight_ref
  4.9 0.0 copy-start.2
  4.9 0.2 collective-permute-done.got_ref
  5.1 0.7 %collective-permute-start.1 = (bf16[64,128]{1,0:T(8,128)(2,1)S(1)}, bf16[64,128]{1,0:T(8,128)(2,1)S(1)}, u32[]{:S(2)}, u32[]{:S(2)}) collective-permute-start(bf16[64,128]{1,0:T(8,128)(2,1)S(1)} %shard_map.74), channel_id=1, source_target_pairs={{1,5},{5,1},{8,12},{12,8},{3,7},{7,3},{10,14},{14,10},{17,21},{21,... | collective-permute-start | bytes 49160 | tf_op jit(solution)/shard_map/ppermute | solution.py:353
  5.8 0.0 collective-permute-done.1.passed_ref
  5.8 0.0 copy-done.2
  5.9 2.0 %collective-permute-start.2 = (bf16[2,64,128]{2,1,0:T(8,128)(2,1)S(1)}, bf16[2,64,128]{2,1,0:T(8,128)(2,1)S(1)}, u32[]{:S(2)}, u32[]{:S(2)}) collective-permute-start(bf16[2,64,128]{2,1,0:T(8,128)(2,1)S(1)} %shard_map.75.own_ref), channel_id=1, source_target_pairs={{0,2},{2,0},{1,3},{3,1},{4,6},{6,4},{5,7},{7,5},{8,10},{10,8},{9,1... | collective-permute-start | bytes 98312 | tf_op jit(solution)/shard_map/ppermute | solution.py:357
  7.9 2.0 %collective-permute-done.2.row_ref = bf16[2,64,128]{2,1,0:T(8,128)(2,1)S(1)} collective-permute-done((bf16[2,64,128]{2,1,0:T(8,128)(2,1)S(1)}, bf16[2,64,128]{2,1,0:T(8,128)(2,1)S(1)}, u32[]{:S(2)}, u32[]{:S(2)}) %collective-permute-start.2) | collective-permute-done | bytes 32800 | tf_op jit(solution)/shard_map/ppermute | solution.py:357
  9.8 0.0 copy-start.4
  9.9 0.0 copy-start.5
  9.9 0.0 copy-start.6
  9.9 3.6 %collective-permute-start.3 = (bf16[2,2,64,128]{3,2,1,0:T(8,128)(2,1)S(1)}, bf16[2,2,64,128]{3,2,1,0:T(8,128)(2,1)S(1)}, u32[]{:S(2)}, u32[]{:S(2)}) collective-permute-start(bf16[2,2,64,128]{3,2,1,0:T(8,128)(2,1)S(1)} %shard_map.76.near_ref), channel_id=1, source_target_pairs={{0,1},{1,0},{2,3},{3,2},{4,5},{5,4},{6,7},{7,6},{8,9},{9,8},{10,11... | collective-permute-start | bytes 196616 | tf_op jit(solution)/shard_map/ppermute | solution.py:357
  13.5 0.9 %collective-permute-done.3.far_ref = bf16[2,2,64,128]{3,2,1,0:T(8,128)(2,1)S(1)} collective-permute-done((bf16[2,2,64,128]{3,2,1,0:T(8,128)(2,1)S(1)}, bf16[2,2,64,128]{3,2,1,0:T(8,128)(2,1)S(1)}, u32[]{:S(2)}, u32[]{:S(2)}) %collective-permute-start.3) | collective-permute-done | bytes 65568 | tf_op jit(solution)/shard_map/ppermute | solution.py:357
  14.4 0.7 %shard_map.78 = (bf16[256,128]{1,0:T(8,128)(2,1)S(1)}, bf16[256,128]{1,0:T(8,128)(2,1)S(1)}) custom-call(bf16[2,2,64,128]{3,2,1,0:T(8,128)(2,1)S(1)} %shard_map.76.near_ref, bf16[2,2,64,128]{3,2,1,0:T(8,128)(2,1)S(1)} %collective-permute-done.3.far_ref, bf16[3,3,3,128,256]{4,3,2,1,0:T(8,128)(2,1)S(1)} %shard_map.73.after_ref.weight_ref), custom_call_target="tpu_custom_call" | custom-call | flops 452984832 | bytes 3145728 | tf_op jit(solution)/shard_map/pallas_call | solution.py:321
  15.1 0.0 copy-start
  15.1 0.0 copy-start.3
  15.1 5.2 %collective-permute-start.4 = (bf16[256,128]{1,0:T(8,128)(2,1)S(1)}, bf16[256,128]{1,0:T(8,128)(2,1)S(1)}, u32[]{:S(2)}, u32[]{:S(2)}) collective-permute-start(bf16[256,128]{1,0:T(8,128)(2,1)S(1)} %get-tuple-element.13), channel_id=1, source_target_pairs={{0,8},{4,12},{8,0},{12,4},{1,9},{5,13},{9,1},{13,5},{2,10},{6,14},... | collective-permute-start | bytes 196616 | tf_op jit(solution)/shard_map/ppermute | solution.py:357
  20.3 1.3 %collective-permute-start.5 = (bf16[256,128]{1,0:T(8,128)(2,1)S(1)}, bf16[256,128]{1,0:T(8,128)(2,1)S(1)}, u32[]{:S(2)}, u32[]{:S(2)}) collective-permute-start(bf16[256,128]{1,0:T(8,128)(2,1)S(1)} %get-tuple-element.14), channel_id=1, source_target_pairs={{0,12},{4,8},{8,4},{12,0},{1,13},{5,9},{9,5},{13,1},{2,14},{6,10},... | collective-permute-start | bytes 196616 | tf_op jit(solution)/shard_map/ppermute | solution.py:357
  21.6 0.7 %shard_map.77 = (f32[256,128]{1,0:T(8,128)S(1)}, bf16[256,128]{1,0:T(8,128)(2,1)S(1)}) custom-call(bf16[2,2,64,128]{3,2,1,0:T(8,128)(2,1)S(1)} %shard_map.76.near_ref, bf16[2,2,64,128]{3,2,1,0:T(8,128)(2,1)S(1)} %collective-permute-done.3.far_ref, bf16[3,3,3,128,256]{4,3,2,1,0:T(8,128)(2,1)S(1)} %shard_map.73.after_ref.weight_ref), custom_call_target="tpu_custom_call" | custom-call | flops 452984832 | bytes 3145728 | tf_op jit(solution)/shard_map/pallas_call | solution.py:321
  22.3 0.6 %collective-permute-start.6 = (bf16[256,128]{1,0:T(8,128)(2,1)S(1)}, bf16[256,128]{1,0:T(8,128)(2,1)S(1)}, u32[]{:S(2)}, u32[]{:S(2)}) collective-permute-start(bf16[256,128]{1,0:T(8,128)(2,1)S(1)} %get-tuple-element.15), channel_id=1, source_target_pairs={{0,4},{4,0},{8,12},{12,8},{1,5},{5,1},{9,13},{13,9},{2,6},{6,2},{1... | collective-permute-start | bytes 196616 | tf_op jit(solution)/shard_map/ppermute | solution.py:357
  22.9 1.3 %collective-permute-done.4.refs_1_ = bf16[256,128]{1,0:T(8,128)(2,1)S(1)} collective-permute-done((bf16[256,128]{1,0:T(8,128)(2,1)S(1)}, bf16[256,128]{1,0:T(8,128)(2,1)S(1)}, u32[]{:S(2)}, u32[]{:S(2)}) %collective-permute-start.4) | collective-permute-done | bytes 65568 | tf_op jit(solution)/shard_map/ppermute | solution.py:357
  24.1 2.7 %collective-permute-done.5.refs_2_ = bf16[256,128]{1,0:T(8,128)(2,1)S(1)} collective-permute-done((bf16[256,128]{1,0:T(8,128)(2,1)S(1)}, bf16[256,128]{1,0:T(8,128)(2,1)S(1)}, u32[]{:S(2)}, u32[]{:S(2)}) %collective-permute-start.5) | collective-permute-done | bytes 65568 | tf_op jit(solution)/shard_map/ppermute | solution.py:357
  26.8 0.7 %collective-permute-done.6.refs_3_ = bf16[256,128]{1,0:T(8,128)(2,1)S(1)} collective-permute-done((bf16[256,128]{1,0:T(8,128)(2,1)S(1)}, bf16[256,128]{1,0:T(8,128)(2,1)S(1)}, u32[]{:S(2)}, u32[]{:S(2)}) %collective-permute-start.6) | collective-permute-done | bytes 65568 | tf_op jit(solution)/shard_map/ppermute | solution.py:357
  27.5 0.0 copy-done.4
  27.5 0.0 copy-done.5
  27.5 0.0 copy-done.6
  27.5 0.3 shard_map.79
  27.8 2.2 %collective-permute-start.7 = (bf16[2,3,32,128]{3,2,1,0:T(8,128)(2,1)S(1)}, bf16[2,3,32,128]{3,2,1,0:T(8,128)(2,1)S(1)}, u32[]{:S(2)}, u32[]{:S(2)}) collective-permute-start(bf16[2,3,32,128]{3,2,1,0:T(8,128)(2,1)S(1)} %get-tuple-element.17), channel_id=1, source_target_pairs={{0,8},{4,12},{8,0},{12,4},{1,9},{5,13},{9,1},{13,5},{2,10},{6,14},... | collective-permute-start | bytes 147464 | tf_op jit(solution)/shard_map/ppermute | solution.py:357
  30.0 3.4 %collective-permute-done.7.crossed_ref = bf16[2,3,32,128]{3,2,1,0:T(8,128)(2,1)S(1)} collective-permute-done((bf16[2,3,32,128]{3,2,1,0:T(8,128)(2,1)S(1)}, bf16[2,3,32,128]{3,2,1,0:T(8,128)(2,1)S(1)}, u32[]{:S(2)}, u32[]{:S(2)}) %collective-permute-start.7) | collective-permute-done | bytes 49184 | tf_op jit(solution)/shard_map/ppermute | solution.py:357
  33.4 0.3 collective-permute-start.8
  33.7 3.8 %collective-permute-done.8.handed_ref = bf16[2,3,32,128]{3,2,1,0:T(8,128)(2,1)S(1)} collective-permute-done((bf16[2,3,32,128]{3,2,1,0:T(8,128)(2,1)S(1)}, bf16[2,3,32,128]{3,2,1,0:T(8,128)(2,1)S(1)}, u32[]{:S(2)}, u32[]{:S(2)}) %collective-permute-start.8) | collective-permute-done | bytes 49184 | tf_op jit(solution)/shard_map/ppermute | solution.py:357
  37.6 0.1 collective-permute-start.9
  37.6 0.0 copy-done
  37.6 0.0 copy-done.3
  37.6 0.5 %shard_map.82.total_ref = f32[256,256]{1,0:T(8,128)S(1)} custom-call(bf16[3,4,16,256]{3,2,1,0:T(8,128)(2,1)S(1)} %shard_map.81.cells_ref, bf16[3,3,512,256]{3,2,1,0:T(8,128)(2,1)S(1)} %copy-done, f32[1,256]{1,0:T(1,128)S(1)} %bitcast.7), custom_call_target="tpu_custom_call" | custom-call | flops 301989888 | bytes 2097152 | tf_op jit(solution)/shard_map/pallas_call | solution.py:321
  38.1 0.8 %collective-permute-done.9.cells_ref = bf16[3,4,16,256]{3,2,1,0:T(8,128)(2,1)S(1)} collective-permute-done((bf16[3,4,16,256]{3,2,1,0:T(8,128)(2,1)S(1)}, bf16[3,4,16,256]{3,2,1,0:T(8,128)(2,1)S(1)}, u32[]{:S(2)}, u32[]{:S(2)}) %collective-permute-start.9) | collective-permute-done | bytes 98336 | tf_op jit(solution)/shard_map/ppermute | solution.py:396
  38.9 1.2 %shard_map.83 = bf16[2,8,4,4,256]{4,3,2,1,0:T(4,128)(2,1)} custom-call(bf16[3,4,16,256]{3,2,1,0:T(8,128)(2,1)S(1)} %collective-permute-done.9.cells_ref, bf16[3,3,512,256]{3,2,1,0:T(8,128)(2,1)S(1)} %copy-done, f32[256,256]{1,0:T(8,128)S(1)} %shard_map.82.total_ref), custom_call_target="tpu_custom_call" | custom-call | flops 301989888 | bytes 2097152 | tf_op jit(solution)/shard_map/pallas_call | solution.py:321
  (5 shorter events, 0.1 us)
Async XLA Ops:
  0.0 5.1 %collective-permute-start = (bf16[64,256]{1,0:T(8,128)(2,1)}, bf16[64,256]{1,0:T(8,128)(2,1)S(1)}, u32[]{:S(2)}, u32[]{:S(2)}) collective-permute-start(bf16[64,256]{1,0:T(8,128)(2,1)} %bitcast.5), channel_id=1, source_target_pairs={{0,4},{1,8},{4,0},{5,12},{8,1},{9,13},{12,5},{13,9},{2,6},{3,10},{... | collective-permute-start | bytes 98312 | tf_op jit(solution)/shard_map/ppermute | solution.py:350
  3.0 1.5 %copy-start.1 = (bf16[3,3,3,128,256]{4,3,2,1,0:T(8,128)(2,1)S(1)}, bf16[3,3,3,128,256]{4,3,2,1,0:T(8,128)(2,1)}, u32[]{:S(2)}) copy-start(bf16[3,3,3,128,256]{4,3,2,1,0:T(8,128)(2,1)} %weight_ref.3) | copy-start | bytes 5308420
  4.9 0.9 %copy-start.2 = (bf16[2,2,2,8,256]{4,3,2,1,0:T(8,128)(2,1)S(1)}, bf16[2,2,2,8,256]{4,3,2,1,0:T(8,128)(2,1)}, u32[]{:S(2)}) copy-start(bf16[2,2,2,8,256]{4,3,2,1,0:T(8,128)(2,1)} %param.7) | copy-start | bytes 98308
  5.1 0.7 %collective-permute-start.1 = (bf16[64,128]{1,0:T(8,128)(2,1)S(1)}, bf16[64,128]{1,0:T(8,128)(2,1)S(1)}, u32[]{:S(2)}, u32[]{:S(2)}) collective-permute-start(bf16[64,128]{1,0:T(8,128)(2,1)S(1)} %shard_map.74), channel_id=1, source_target_pairs={{1,5},{5,1},{8,12},{12,8},{3,7},{7,3},{10,14},{14,10},{17,21},{21,... | collective-permute-start | bytes 49160 | tf_op jit(solution)/shard_map/ppermute | solution.py:353
  5.9 4.0 %collective-permute-start.2 = (bf16[2,64,128]{2,1,0:T(8,128)(2,1)S(1)}, bf16[2,64,128]{2,1,0:T(8,128)(2,1)S(1)}, u32[]{:S(2)}, u32[]{:S(2)}) collective-permute-start(bf16[2,64,128]{2,1,0:T(8,128)(2,1)S(1)} %shard_map.75.own_ref), channel_id=1, source_target_pairs={{0,2},{2,0},{1,3},{3,1},{4,6},{6,4},{5,7},{7,5},{8,10},{10,8},{9,1... | collective-permute-start | bytes 98312 | tf_op jit(solution)/shard_map/ppermute | solution.py:357
  9.8 17.6 %copy-start.4 = (f32[256]{0:T(256)S(1)}, f32[256]{0:T(256)}, u32[]{:S(2)}) copy-start(f32[256]{0:T(256)} %param.9) | copy-start | bytes 3076
  9.9 17.6 %copy-start.5 = (f32[256]{0:T(256)S(1)}, f32[256]{0:T(256)}, u32[]{:S(2)}) copy-start(f32[256]{0:T(256)} %param.10) | copy-start | bytes 3076
  9.9 17.6 %copy-start.6 = (f32[256]{0:T(256)S(1)}, f32[256]{0:T(256)}, u32[]{:S(2)}) copy-start(f32[256]{0:T(256)} %param.11) | copy-start | bytes 3076
  9.9 4.5 %collective-permute-start.3 = (bf16[2,2,64,128]{3,2,1,0:T(8,128)(2,1)S(1)}, bf16[2,2,64,128]{3,2,1,0:T(8,128)(2,1)S(1)}, u32[]{:S(2)}, u32[]{:S(2)}) collective-permute-start(bf16[2,2,64,128]{3,2,1,0:T(8,128)(2,1)S(1)} %shard_map.76.near_ref), channel_id=1, source_target_pairs={{0,1},{1,0},{2,3},{3,2},{4,5},{5,4},{6,7},{7,6},{8,9},{9,8},{10,11... | collective-permute-start | bytes 196616 | tf_op jit(solution)/shard_map/ppermute | solution.py:357
  15.1 22.5 %copy-start = (bf16[3,3,512,256]{3,2,1,0:T(8,128)(2,1)S(1)}, bf16[3,3,512,256]{3,2,1,0:T(8,128)(2,1)}, u32[]{:S(2)}) copy-start(bf16[3,3,512,256]{3,2,1,0:T(8,128)(2,1)} %weight_ref.5) | copy-start | bytes 7077892
  15.1 22.5 %copy-start.3 = (f32[256]{0:T(256)S(1)}, f32[256]{0:T(256)}, u32[]{:S(2)}) copy-start(f32[256]{0:T(256)} %param.13) | copy-start | bytes 3076
  15.1 9.0 %collective-permute-start.4 = (bf16[256,128]{1,0:T(8,128)(2,1)S(1)}, bf16[256,128]{1,0:T(8,128)(2,1)S(1)}, u32[]{:S(2)}, u32[]{:S(2)}) collective-permute-start(bf16[256,128]{1,0:T(8,128)(2,1)S(1)} %get-tuple-element.13), channel_id=1, source_target_pairs={{0,8},{4,12},{8,0},{12,4},{1,9},{5,13},{9,1},{13,5},{2,10},{6,14},... | collective-permute-start | bytes 196616 | tf_op jit(solution)/shard_map/ppermute | solution.py:357
  20.3 6.5 %collective-permute-start.5 = (bf16[256,128]{1,0:T(8,128)(2,1)S(1)}, bf16[256,128]{1,0:T(8,128)(2,1)S(1)}, u32[]{:S(2)}, u32[]{:S(2)}) collective-permute-start(bf16[256,128]{1,0:T(8,128)(2,1)S(1)} %get-tuple-element.14), channel_id=1, source_target_pairs={{0,12},{4,8},{8,4},{12,0},{1,13},{5,9},{9,5},{13,1},{2,14},{6,10},... | collective-permute-start | bytes 196616 | tf_op jit(solution)/shard_map/ppermute | solution.py:357
  22.3 5.2 %collective-permute-start.6 = (bf16[256,128]{1,0:T(8,128)(2,1)S(1)}, bf16[256,128]{1,0:T(8,128)(2,1)S(1)}, u32[]{:S(2)}, u32[]{:S(2)}) collective-permute-start(bf16[256,128]{1,0:T(8,128)(2,1)S(1)} %get-tuple-element.15), channel_id=1, source_target_pairs={{0,4},{4,0},{8,12},{12,8},{1,5},{5,1},{9,13},{13,9},{2,6},{6,2},{1... | collective-permute-start | bytes 196616 | tf_op jit(solution)/shard_map/ppermute | solution.py:357
  27.8 5.6 %collective-permute-start.7 = (bf16[2,3,32,128]{3,2,1,0:T(8,128)(2,1)S(1)}, bf16[2,3,32,128]{3,2,1,0:T(8,128)(2,1)S(1)}, u32[]{:S(2)}, u32[]{:S(2)}) collective-permute-start(bf16[2,3,32,128]{3,2,1,0:T(8,128)(2,1)S(1)} %get-tuple-element.17), channel_id=1, source_target_pairs={{0,8},{4,12},{8,0},{12,4},{1,9},{5,13},{9,1},{13,5},{2,10},{6,14},... | collective-permute-start | bytes 147464 | tf_op jit(solution)/shard_map/ppermute | solution.py:357
  33.4 4.1 %collective-permute-start.8 = (bf16[2,3,32,128]{3,2,1,0:T(8,128)(2,1)S(1)}, bf16[2,3,32,128]{3,2,1,0:T(8,128)(2,1)S(1)}, u32[]{:S(2)}, u32[]{:S(2)}) collective-permute-start(bf16[2,3,32,128]{3,2,1,0:T(8,128)(2,1)S(1)} %shard_map.80), channel_id=1, source_target_pairs={{0,4},{4,0},{8,12},{12,8},{1,5},{5,1},{9,13},{13,9},{2,6},{6,2},{1... | collective-permute-start | bytes 147464 | tf_op jit(solution)/shard_map/ppermute | solution.py:357
  37.6 1.4 %collective-permute-start.9 = (bf16[3,4,16,256]{3,2,1,0:T(8,128)(2,1)S(1)}, bf16[3,4,16,256]{3,2,1,0:T(8,128)(2,1)S(1)}, u32[]{:S(2)}, u32[]{:S(2)}) collective-permute-start(bf16[3,4,16,256]{3,2,1,0:T(8,128)(2,1)S(1)} %shard_map.81.cells_ref), channel_id=1, source_target_pairs={{0,1},{1,0},{2,3},{3,2},{4,5},{5,4},{6,7},{7,6},{8,9},{9,8},{10,11... | collective-permute-start | bytes 294920 | tf_op jit(solution)/shard_map/ppermute | solution.py:396

commit v8 on v7

--- a/solution.py
+++ b/solution.py
@@ -208,8 +208,8 @@
 
 
 def norm_kernel(*refs):
-    partial, (bias_ref, gain_ref, shift_ref) = refs[:4], refs[4:7]
-    keep_ref, next_ref, cross_ref, tiles = refs[7:]
+    partial, (bias_ref, gain_ref, shift_ref), sent = refs[:4], refs[4:7], refs[7:11]
+    tiles = refs[11]
     tm, side, _ = placed_at()
     owners, reach, strip, depth = tiles.shape
     cols = 8
@@ -244,21 +244,15 @@
             for j in range(owner * width - 1, (owner + 1) * width + 1):
                 picked.append(chosen[j] if 0 <= j < cols else empty)
             tiles[owner, i] = jnp.concatenate(picked, axis=0).astype(tiles.dtype)
-    keep_ref[...] = tiles[tm]
-    next_ref[...] = tiles[tm ^ 1]
-    for m in (2, 3):
-        cross_ref[m - 2] = tiles[tm ^ m]
-
-
-def hand_kernel(following_ref, crossed_ref, out_ref):
-    out_ref[0] = following_ref[...]
-    out_ref[1] = crossed_ref[1]
-
-
-def cells_kernel(kept_ref, crossed_ref, handed_ref, cells_ref, tiles):
+    for m in range(owners):
+        sent[m][...] = tiles[tm ^ m]
+
+
+def cells_kernel(*refs):
+    got, cells_ref, tiles = refs[:4], refs[4], refs[5]
     tm, _, _ = placed_at()
-    for m, value in enumerate((kept_ref[...], handed_ref[0], crossed_ref[0], handed_ref[1])):
-        tiles[tm ^ m] = value.astype(jnp.float32)
+    for m in range(len(got)):
+        tiles[tm ^ m] = got[m][...].astype(jnp.float32)
     reach, wide, tall, half = cells_ref.shape
     depth = tiles.shape[3]
     los = half // depth
@@ -374,17 +368,15 @@
     partial = [keep] + partial + [across(near_other, "tm", 1)]
 
     tile = shape((rows + 1, (width + 2) * frames, depth), low)
-    kept, following, crossing = run(
+    tiles = run(
         norm_kernel,
-        [tile, tile, shape((2,) + tile.shape, low)],
+        [tile] * spans,
         [pltpu.VMEM((spans,) + tile.shape, low)],
         *partial,
         *(vector.reshape(los, depth) for vector in (conv_bias, gn_gain, gn_shift)),
         moved=1 << 19,
     )
-    crossed = across(crossing, "tm", 2)
-    handed = run(hand_kernel, shape((2,) + tile.shape, low), [], following, crossed, moved=1 << 17)
-    tiles = [kept, crossed, across(handed, "tm", 1)]
+    tiles = [tiles[0]] + [across(tiles[m], "tm", m) for m in range(1, spans)]
 
     near = run(
         cells_kernel,

time: 40.3 us -> 39.8 us (0.988)
  waiting for transfers between devices: 15.7 us -> 13.3 us
  starting transfers between devices: 18.9 us -> 20.9 us
    ppermute x7 -> x8, waiting for transfers between devices: 14.7 us -> 12.3 us  [across(): return lax.ppermute(value, axes, [(i, i ^ m) for i in range(count)])]
    ppermute x7 -> x8, starting transfers between devices: 15.2 us -> 17.1 us  [across(): return lax.ppermute(value, axes, [(i, i ^ m) for i in range(count)])]
    pallas_call x11 -> x10, Pallas kernels: 3.8 us -> 3.8 us  [run(): pl.pallas_call(kernel, out_shape=shapes, in_specs=[vmem] * len(operands),...]
  transfers between devices with their start and end apart: 10 -> 11, of which waited for: 9 -> 9; matrix products, arithmetic and copies ran while one was open for 0% -> 0% of each run, Pallas kernels for 4% -> 4%
where the time goes in v8:
time: 39.8 us; the launch traced here: 39.6 us
  starting transfers between devices  20.9 us (53%)
  waiting for transfers between devices  13.3 us (33%)
  Pallas kernels  3.8 us (10%)
  local copies, waits for them, and re-layouts  1.51 us (4%)
    ppermute x8, starting transfers between devices, across(): return lax.ppermute(value, axes, [(i, i ^ m) for i in range(count)])  17.1 us
    ppermute x8, waiting for transfers between devices, across(): return lax.ppermute(value, axes, [(i, i ^ m) for i in range(count)])  12.3 us
    pallas_call x10, Pallas kernels, run(): pl.pallas_call(kernel, out_shape=shapes, in_specs=[vmem] * len(operands),...  3.8 us
    ppermute x1, starting transfers between devices, small_plan(): got = lax.ppermute(cells_in, ('tm', 'chan'), first)  3.02 us
    unnamed x14, local copies, waits for them, and re-layouts  1.51 us
  transfers between devices with their start and end apart: 11, of which 9 were waited for; matrix products, arithmetic and copies ran while one was open for 0% of the time, Pallas kernels for 4%

profile of v8, /device:TPU:0, one launch (start us, length us, event | category | flops | bytes accessed | tf_op | source)
XLA Modules:
  0.0 39.6 jit_solution(5961170777892219526)
XLA Ops:
  0.0 3.0 %collective-permute-start = (bf16[64,256]{1,0:T(8,128)(2,1)}, bf16[64,256]{1,0:T(8,128)(2,1)S(1)}, u32[]{:S(2)}, u32[]{:S(2)}) collective-permute-start(bf16[64,256]{1,0:T(8,128)(2,1)} %bitcast.5), channel_id=1, source_target_pairs={{0,4},{1,8},{4,0},{5,12},{8,1},{9,13},{12,5},{13,9},{2,6},{3,10},{... | collective-permute-start | bytes 98312 | tf_op jit(solution)/shard_map/ppermute | solution.py:344
  3.0 0.0 copy-start.1
  3.0 1.5 %copy-done.1 = bf16[3,3,3,128,256]{4,3,2,1,0:T(8,128)(2,1)S(1)} copy-done((bf16[3,3,3,128,256]{4,3,2,1,0:T(8,128)(2,1)S(1)}, bf16[3,3,3,128,256]{4,3,2,1,0:T(8,128)(2,1)}, u32[]{:S(2)}) %copy-start.1) | copy-done | bytes 1769496
  4.5 0.4 shard_map.73.after_ref.weight_ref
  4.9 0.0 copy-start.2
  4.9 0.2 collective-permute-done.got_ref
  5.1 0.7 %collective-permute-start.1 = (bf16[64,128]{1,0:T(8,128)(2,1)S(1)}, bf16[64,128]{1,0:T(8,128)(2,1)S(1)}, u32[]{:S(2)}, u32[]{:S(2)}) collective-permute-start(bf16[64,128]{1,0:T(8,128)(2,1)S(1)} %shard_map.74), channel_id=1, source_target_pairs={{1,5},{5,1},{8,12},{12,8},{3,7},{7,3},{10,14},{14,10},{17,21},{21,... | collective-permute-start | bytes 49160 | tf_op jit(solution)/shard_map/ppermute | solution.py:347
  5.8 0.0 collective-permute-done.1.passed_ref
  5.8 0.0 copy-done.2
  5.9 2.0 %collective-permute-start.2 = (bf16[2,64,128]{2,1,0:T(8,128)(2,1)S(1)}, bf16[2,64,128]{2,1,0:T(8,128)(2,1)S(1)}, u32[]{:S(2)}, u32[]{:S(2)}) collective-permute-start(bf16[2,64,128]{2,1,0:T(8,128)(2,1)S(1)} %shard_map.75.own_ref), channel_id=1, source_target_pairs={{0,2},{2,0},{1,3},{3,1},{4,6},{6,4},{5,7},{7,5},{8,10},{10,8},{9,1... | collective-permute-start | bytes 98312 | tf_op jit(solution)/shard_map/ppermute | solution.py:351
  7.9 2.0 %collective-permute-done.2.row_ref = bf16[2,64,128]{2,1,0:T(8,128)(2,1)S(1)} collective-permute-done((bf16[2,64,128]{2,1,0:T(8,128)(2,1)S(1)}, bf16[2,64,128]{2,1,0:T(8,128)(2,1)S(1)}, u32[]{:S(2)}, u32[]{:S(2)}) %collective-permute-start.2) | collective-permute-done | bytes 32800 | tf_op jit(solution)/shard_map/ppermute | solution.py:351
  9.8 0.0 copy-start.4
  9.9 0.0 copy-start.5
  9.9 0.0 copy-start.6
  9.9 0.0 copy-start
  9.9 0.0 copy-start.3
  9.9 3.6 %collective-permute-start.3 = (bf16[2,2,64,128]{3,2,1,0:T(8,128)(2,1)S(1)}, bf16[2,2,64,128]{3,2,1,0:T(8,128)(2,1)S(1)}, u32[]{:S(2)}, u32[]{:S(2)}) collective-permute-start(bf16[2,2,64,128]{3,2,1,0:T(8,128)(2,1)S(1)} %shard_map.76.near_ref), channel_id=1, source_target_pairs={{0,1},{1,0},{2,3},{3,2},{4,5},{5,4},{6,7},{7,6},{8,9},{9,8},{10,11... | collective-permute-start | bytes 196616 | tf_op jit(solution)/shard_map/ppermute | solution.py:351
  13.5 0.9 %collective-permute-done.3.far_ref = bf16[2,2,64,128]{3,2,1,0:T(8,128)(2,1)S(1)} collective-permute-done((bf16[2,2,64,128]{3,2,1,0:T(8,128)(2,1)S(1)}, bf16[2,2,64,128]{3,2,1,0:T(8,128)(2,1)S(1)}, u32[]{:S(2)}, u32[]{:S(2)}) %collective-permute-start.3) | collective-permute-done | bytes 65568 | tf_op jit(solution)/shard_map/ppermute | solution.py:351
  14.4 0.7 %shard_map.78 = (bf16[256,128]{1,0:T(8,128)(2,1)S(1)}, bf16[256,128]{1,0:T(8,128)(2,1)S(1)}) custom-call(bf16[2,2,64,128]{3,2,1,0:T(8,128)(2,1)S(1)} %shard_map.76.near_ref, bf16[2,2,64,128]{3,2,1,0:T(8,128)(2,1)S(1)} %collective-permute-done.3.far_ref, bf16[3,3,3,128,256]{4,3,2,1,0:T(8,128)(2,1)S(1)} %shard_map.73.after_ref.weight_ref), custom_call_target="tpu_custom_call" | custom-call | flops 452984832 | bytes 3145728 | tf_op jit(solution)/shard_map/pallas_call | solution.py:315
  15.1 5.2 %collective-permute-start.4 = (bf16[256,128]{1,0:T(8,128)(2,1)S(1)}, bf16[256,128]{1,0:T(8,128)(2,1)S(1)}, u32[]{:S(2)}, u32[]{:S(2)}) collective-permute-start(bf16[256,128]{1,0:T(8,128)(2,1)S(1)} %get-tuple-element.14), channel_id=1, source_target_pairs={{0,8},{4,12},{8,0},{12,4},{1,9},{5,13},{9,1},{13,5},{2,10},{6,14},... | collective-permute-start | bytes 196616 | tf_op jit(solution)/shard_map/ppermute | solution.py:351
  20.3 1.3 %collective-permute-start.5 = (bf16[256,128]{1,0:T(8,128)(2,1)S(1)}, bf16[256,128]{1,0:T(8,128)(2,1)S(1)}, u32[]{:S(2)}, u32[]{:S(2)}) collective-permute-start(bf16[256,128]{1,0:T(8,128)(2,1)S(1)} %get-tuple-element.15), channel_id=1, source_target_pairs={{0,12},{4,8},{8,4},{12,0},{1,13},{5,9},{9,5},{13,1},{2,14},{6,10},... | collective-permute-start | bytes 196616 | tf_op jit(solution)/shard_map/ppermute | solution.py:351
  21.6 0.7 %shard_map.77 = (f32[256,128]{1,0:T(8,128)S(1)}, bf16[256,128]{1,0:T(8,128)(2,1)S(1)}) custom-call(bf16[2,2,64,128]{3,2,1,0:T(8,128)(2,1)S(1)} %shard_map.76.near_ref, bf16[2,2,64,128]{3,2,1,0:T(8,128)(2,1)S(1)} %collective-permute-done.3.far_ref, bf16[3,3,3,128,256]{4,3,2,1,0:T(8,128)(2,1)S(1)} %shard_map.73.after_ref.weight_ref), custom_call_target="tpu_custom_call" | custom-call | flops 452984832 | bytes 3145728 | tf_op jit(solution)/shard_map/pallas_call | solution.py:315
  22.3 0.6 %collective-permute-start.6 = (bf16[256,128]{1,0:T(8,128)(2,1)S(1)}, bf16[256,128]{1,0:T(8,128)(2,1)S(1)}, u32[]{:S(2)}, u32[]{:S(2)}) collective-permute-start(bf16[256,128]{1,0:T(8,128)(2,1)S(1)} %get-tuple-element.16), channel_id=1, source_target_pairs={{0,4},{4,0},{8,12},{12,8},{1,5},{5,1},{9,13},{13,9},{2,6},{6,2},{1... | collective-permute-start | bytes 196616 | tf_op jit(solution)/shard_map/ppermute | solution.py:351
  22.9 1.3 %collective-permute-done.4.refs_1_ = bf16[256,128]{1,0:T(8,128)(2,1)S(1)} collective-permute-done((bf16[256,128]{1,0:T(8,128)(2,1)S(1)}, bf16[256,128]{1,0:T(8,128)(2,1)S(1)}, u32[]{:S(2)}, u32[]{:S(2)}) %collective-permute-start.4) | collective-permute-done | bytes 65568 | tf_op jit(solution)/shard_map/ppermute | solution.py:351
  24.1 2.7 %collective-permute-done.5.refs_2_ = bf16[256,128]{1,0:T(8,128)(2,1)S(1)} collective-permute-done((bf16[256,128]{1,0:T(8,128)(2,1)S(1)}, bf16[256,128]{1,0:T(8,128)(2,1)S(1)}, u32[]{:S(2)}, u32[]{:S(2)}) %collective-permute-start.5) | collective-permute-done | bytes 65568 | tf_op jit(solution)/shard_map/ppermute | solution.py:351
  26.8 0.7 %collective-permute-done.6.refs_3_ = bf16[256,128]{1,0:T(8,128)(2,1)S(1)} collective-permute-done((bf16[256,128]{1,0:T(8,128)(2,1)S(1)}, bf16[256,128]{1,0:T(8,128)(2,1)S(1)}, u32[]{:S(2)}, u32[]{:S(2)}) %collective-permute-start.6) | collective-permute-done | bytes 65568 | tf_op jit(solution)/shard_map/ppermute | solution.py:351
  27.5 0.0 copy-done.4
  27.5 0.0 copy-done.5
  27.5 0.0 copy-done.6
  27.5 0.3 shard_map.79
  27.8 0.3 collective-permute-start.7
  28.1 3.3 %collective-permute-start.8 = (bf16[3,32,128]{2,1,0:T(8,128)(2,1)S(1)}, bf16[3,32,128]{2,1,0:T(8,128)(2,1)S(1)}, u32[]{:S(2)}, u32[]{:S(2)}) collective-permute-start(bf16[3,32,128]{2,1,0:T(8,128)(2,1)S(1)} %get-tuple-element.19), channel_id=1, source_target_pairs={{0,8},{4,12},{8,0},{12,4},{1,9},{5,13},{9,1},{13,5},{2,10},{6,14},... | collective-permute-start | bytes 73736 | tf_op jit(solution)/shard_map/ppermute | solution.py:351
  31.5 0.8 %collective-permute-start.9 = (bf16[3,32,128]{2,1,0:T(8,128)(2,1)S(1)}, bf16[3,32,128]{2,1,0:T(8,128)(2,1)S(1)}, u32[]{:S(2)}, u32[]{:S(2)}) collective-permute-start(bf16[3,32,128]{2,1,0:T(8,128)(2,1)S(1)} %get-tuple-element.20), channel_id=1, source_target_pairs={{0,12},{4,8},{8,4},{12,0},{1,13},{5,9},{9,5},{13,1},{2,14},{6,10},... | collective-permute-start | bytes 73736 | tf_op jit(solution)/shard_map/ppermute | solution.py:351
  32.3 0.0 collective-permute-done.7.refs_1_
  32.3 1.0 %collective-permute-done.8.refs_2_ = bf16[3,32,128]{2,1,0:T(8,128)(2,1)S(1)} collective-permute-done((bf16[3,32,128]{2,1,0:T(8,128)(2,1)S(1)}, bf16[3,32,128]{2,1,0:T(8,128)(2,1)S(1)}, u32[]{:S(2)}, u32[]{:S(2)}) %collective-permute-start.8) | collective-permute-done | bytes 24608 | tf_op jit(solution)/shard_map/ppermute | solution.py:351
  33.3 3.8 %collective-permute-done.9.refs_3_ = bf16[3,32,128]{2,1,0:T(8,128)(2,1)S(1)} collective-permute-done((bf16[3,32,128]{2,1,0:T(8,128)(2,1)S(1)}, bf16[3,32,128]{2,1,0:T(8,128)(2,1)S(1)}, u32[]{:S(2)}, u32[]{:S(2)}) %collective-permute-start.9) | collective-permute-done | bytes 24608 | tf_op jit(solution)/shard_map/ppermute | solution.py:351
  37.1 0.1 collective-permute-start.10
  37.2 0.0 copy-done
  37.2 0.0 copy-done.3
  37.2 0.5 %shard_map.81.total_ref = f32[256,256]{1,0:T(8,128)S(1)} custom-call(bf16[3,4,16,256]{3,2,1,0:T(8,128)(2,1)S(1)} %shard_map.80.cells_ref, bf16[3,3,512,256]{3,2,1,0:T(8,128)(2,1)S(1)} %copy-done, f32[1,256]{1,0:T(1,128)S(1)} %bitcast.7), custom_call_target="tpu_custom_call" | custom-call | flops 301989888 | bytes 2097152 | tf_op jit(solution)/shard_map/pallas_call | solution.py:315
  37.7 0.8 %collective-permute-done.10.cells_ref = bf16[3,4,16,256]{3,2,1,0:T(8,128)(2,1)S(1)} collective-permute-done((bf16[3,4,16,256]{3,2,1,0:T(8,128)(2,1)S(1)}, bf16[3,4,16,256]{3,2,1,0:T(8,128)(2,1)S(1)}, u32[]{:S(2)}, u32[]{:S(2)}) %collective-permute-start.10) | collective-permute-done | bytes 98336 | tf_op jit(solution)/shard_map/ppermute | solution.py:388
  38.5 1.2 %shard_map.82 = bf16[2,8,4,4,256]{4,3,2,1,0:T(4,128)(2,1)} custom-call(bf16[3,4,16,256]{3,2,1,0:T(8,128)(2,1)S(1)} %collective-permute-done.10.cells_ref, bf16[3,3,512,256]{3,2,1,0:T(8,128)(2,1)S(1)} %copy-done, f32[256,256]{1,0:T(8,128)S(1)} %shard_map.81.total_ref), custom_call_target="tpu_custom_call" | custom-call | flops 301989888 | bytes 2097152 | tf_op jit(solution)/shard_map/pallas_call | solution.py:315
  (4 shorter events, 0.1 us)
Async XLA Ops:
  0.0 5.1 %collective-permute-start = (bf16[64,256]{1,0:T(8,128)(2,1)}, bf16[64,256]{1,0:T(8,128)(2,1)S(1)}, u32[]{:S(2)}, u32[]{:S(2)}) collective-permute-start(bf16[64,256]{1,0:T(8,128)(2,1)} %bitcast.5), channel_id=1, source_target_pairs={{0,4},{1,8},{4,0},{5,12},{8,1},{9,13},{12,5},{13,9},{2,6},{3,10},{... | collective-permute-start | bytes 98312 | tf_op jit(solution)/shard_map/ppermute | solution.py:344
  3.0 1.5 %copy-start.1 = (bf16[3,3,3,128,256]{4,3,2,1,0:T(8,128)(2,1)S(1)}, bf16[3,3,3,128,256]{4,3,2,1,0:T(8,128)(2,1)}, u32[]{:S(2)}) copy-start(bf16[3,3,3,128,256]{4,3,2,1,0:T(8,128)(2,1)} %weight_ref.3) | copy-start | bytes 5308420
  4.9 0.9 %copy-start.2 = (bf16[2,2,2,8,256]{4,3,2,1,0:T(8,128)(2,1)S(1)}, bf16[2,2,2,8,256]{4,3,2,1,0:T(8,128)(2,1)}, u32[]{:S(2)}) copy-start(bf16[2,2,2,8,256]{4,3,2,1,0:T(8,128)(2,1)} %param.7) | copy-start | bytes 98308
  5.1 0.7 %collective-permute-start.1 = (bf16[64,128]{1,0:T(8,128)(2,1)S(1)}, bf16[64,128]{1,0:T(8,128)(2,1)S(1)}, u32[]{:S(2)}, u32[]{:S(2)}) collective-permute-start(bf16[64,128]{1,0:T(8,128)(2,1)S(1)} %shard_map.74), channel_id=1, source_target_pairs={{1,5},{5,1},{8,12},{12,8},{3,7},{7,3},{10,14},{14,10},{17,21},{21,... | collective-permute-start | bytes 49160 | tf_op jit(solution)/shard_map/ppermute | solution.py:347
  5.9 4.0 %collective-permute-start.2 = (bf16[2,64,128]{2,1,0:T(8,128)(2,1)S(1)}, bf16[2,64,128]{2,1,0:T(8,128)(2,1)S(1)}, u32[]{:S(2)}, u32[]{:S(2)}) collective-permute-start(bf16[2,64,128]{2,1,0:T(8,128)(2,1)S(1)} %shard_map.75.own_ref), channel_id=1, source_target_pairs={{0,2},{2,0},{1,3},{3,1},{4,6},{6,4},{5,7},{7,5},{8,10},{10,8},{9,1... | collective-permute-start | bytes 98312 | tf_op jit(solution)/shard_map/ppermute | solution.py:351
  9.8 17.6 %copy-start.4 = (f32[256]{0:T(256)S(1)}, f32[256]{0:T(256)}, u32[]{:S(2)}) copy-start(f32[256]{0:T(256)} %param.9) | copy-start | bytes 3076
  9.9 17.6 %copy-start.5 = (f32[256]{0:T(256)S(1)}, f32[256]{0:T(256)}, u32[]{:S(2)}) copy-start(f32[256]{0:T(256)} %param.10) | copy-start | bytes 3076
  9.9 17.6 %copy-start.6 = (f32[256]{0:T(256)S(1)}, f32[256]{0:T(256)}, u32[]{:S(2)}) copy-start(f32[256]{0:T(256)} %param.11) | copy-start | bytes 3076
  9.9 27.3 %copy-start = (bf16[3,3,512,256]{3,2,1,0:T(8,128)(2,1)S(1)}, bf16[3,3,512,256]{3,2,1,0:T(8,128)(2,1)}, u32[]{:S(2)}) copy-start(bf16[3,3,512,256]{3,2,1,0:T(8,128)(2,1)} %weight_ref.5) | copy-start | bytes 7077892
  9.9 27.3 %copy-start.3 = (f32[256]{0:T(256)S(1)}, f32[256]{0:T(256)}, u32[]{:S(2)}) copy-start(f32[256]{0:T(256)} %param.13) | copy-start | bytes 3076
  9.9 4.5 %collective-permute-start.3 = (bf16[2,2,64,128]{3,2,1,0:T(8,128)(2,1)S(1)}, bf16[2,2,64,128]{3,2,1,0:T(8,128)(2,1)S(1)}, u32[]{:S(2)}, u32[]{:S(2)}) collective-permute-start(bf16[2,2,64,128]{3,2,1,0:T(8,128)(2,1)S(1)} %shard_map.76.near_ref), channel_id=1, source_target_pairs={{0,1},{1,0},{2,3},{3,2},{4,5},{5,4},{6,7},{7,6},{8,9},{9,8},{10,11... | collective-permute-start | bytes 196616 | tf_op jit(solution)/shard_map/ppermute | solution.py:351
  15.1 9.0 %collective-permute-start.4 = (bf16[256,128]{1,0:T(8,128)(2,1)S(1)}, bf16[256,128]{1,0:T(8,128)(2,1)S(1)}, u32[]{:S(2)}, u32[]{:S(2)}) collective-permute-start(bf16[256,128]{1,0:T(8,128)(2,1)S(1)} %get-tuple-element.14), channel_id=1, source_target_pairs={{0,8},{4,12},{8,0},{12,4},{1,9},{5,13},{9,1},{13,5},{2,10},{6,14},... | collective-permute-start | bytes 196616 | tf_op jit(solution)/shard_map/ppermute | solution.py:351
  20.3 6.5 %collective-permute-start.5 = (bf16[256,128]{1,0:T(8,128)(2,1)S(1)}, bf16[256,128]{1,0:T(8,128)(2,1)S(1)}, u32[]{:S(2)}, u32[]{:S(2)}) collective-permute-start(bf16[256,128]{1,0:T(8,128)(2,1)S(1)} %get-tuple-element.15), channel_id=1, source_target_pairs={{0,12},{4,8},{8,4},{12,0},{1,13},{5,9},{9,5},{13,1},{2,14},{6,10},... | collective-permute-start | bytes 196616 | tf_op jit(solution)/shard_map/ppermute | solution.py:351
  22.3 5.2 %collective-permute-start.6 = (bf16[256,128]{1,0:T(8,128)(2,1)S(1)}, bf16[256,128]{1,0:T(8,128)(2,1)S(1)}, u32[]{:S(2)}, u32[]{:S(2)}) collective-permute-start(bf16[256,128]{1,0:T(8,128)(2,1)S(1)} %get-tuple-element.16), channel_id=1, source_target_pairs={{0,4},{4,0},{8,12},{12,8},{1,5},{5,1},{9,13},{13,9},{2,6},{6,2},{1... | collective-permute-start | bytes 196616 | tf_op jit(solution)/shard_map/ppermute | solution.py:351
  27.8 4.5 %collective-permute-start.7 = (bf16[3,32,128]{2,1,0:T(8,128)(2,1)S(1)}, bf16[3,32,128]{2,1,0:T(8,128)(2,1)S(1)}, u32[]{:S(2)}, u32[]{:S(2)}) collective-permute-start(bf16[3,32,128]{2,1,0:T(8,128)(2,1)S(1)} %get-tuple-element.18), channel_id=1, source_target_pairs={{0,4},{4,0},{8,12},{12,8},{1,5},{5,1},{9,13},{13,9},{2,6},{6,2},{1... | collective-permute-start | bytes 73736 | tf_op jit(solution)/shard_map/ppermute | solution.py:351
  28.1 5.1 %collective-permute-start.8 = (bf16[3,32,128]{2,1,0:T(8,128)(2,1)S(1)}, bf16[3,32,128]{2,1,0:T(8,128)(2,1)S(1)}, u32[]{:S(2)}, u32[]{:S(2)}) collective-permute-start(bf16[3,32,128]{2,1,0:T(8,128)(2,1)S(1)} %get-tuple-element.19), channel_id=1, source_target_pairs={{0,8},{4,12},{8,0},{12,4},{1,9},{5,13},{9,1},{13,5},{2,10},{6,14},... | collective-permute-start | bytes 73736 | tf_op jit(solution)/shard_map/ppermute | solution.py:351
  31.5 5.6 %collective-permute-start.9 = (bf16[3,32,128]{2,1,0:T(8,128)(2,1)S(1)}, bf16[3,32,128]{2,1,0:T(8,128)(2,1)S(1)}, u32[]{:S(2)}, u32[]{:S(2)}) collective-permute-start(bf16[3,32,128]{2,1,0:T(8,128)(2,1)S(1)} %get-tuple-element.20), channel_id=1, source_target_pairs={{0,12},{4,8},{8,4},{12,0},{1,13},{5,9},{9,5},{13,1},{2,14},{6,10},... | collective-permute-start | bytes 73736 | tf_op jit(solution)/shard_map/ppermute | solution.py:351
  37.1 1.4 %collective-permute-start.10 = (bf16[3,4,16,256]{3,2,1,0:T(8,128)(2,1)S(1)}, bf16[3,4,16,256]{3,2,1,0:T(8,128)(2,1)S(1)}, u32[]{:S(2)}, u32[]{:S(2)}) collective-permute-start(bf16[3,4,16,256]{3,2,1,0:T(8,128)(2,1)S(1)} %shard_map.80.cells_ref), channel_id=1, source_target_pairs={{0,1},{1,0},{2,3},{3,2},{4,5},{5,4},{6,7},{7,6},{8,9},{9,8},{10,11... | collective-permute-start | bytes 294920 | tf_op jit(solution)/shard_map/ppermute | solution.py:388

commit v9 on v8

--- a/solution.py
+++ b/solution.py
@@ -251,8 +251,8 @@
 def cells_kernel(*refs):
     got, cells_ref, tiles = refs[:4], refs[4], refs[5]
     tm, _, _ = placed_at()
-    for m in range(len(got)):
-        tiles[tm ^ m] = got[m][...].astype(jnp.float32)
+    for ref, m in zip(got, (0, 3, 2, 1)):
+        tiles[tm ^ m] = ref[...].astype(jnp.float32)
     reach, wide, tall, half = cells_ref.shape
     depth = tiles.shape[3]
     los = half // depth
@@ -339,8 +339,7 @@
             home = chan == source // 2
             target = (source ^ 1, chan) if home else (source ^ 2, 1 - chan)
             first.append((source * chans + chan, target[0] * chans + target[1]))
-            if not home:
-                second.append((source * chans + chan, (source ^ 1) * chans + chan))
+            second.append((source * chans + chan, (source ^ 1) * chans + chan))
     got = lax.ppermute(cells_in, ("tm", "chan"), first)
     weight = run(fetch_kernel, shape(conv_weight.shape, low), [pltpu.SemaphoreType.DMA], conv_weight, moved=4 << 20)
     relayed = run(relay_kernel, shape((cells_in.shape[0], depth), low), [], got, weight, moved=1 << 17)
@@ -376,7 +375,7 @@
         *(vector.reshape(los, depth) for vector in (conv_bias, gn_gain, gn_shift)),
         moved=1 << 19,
     )
-    tiles = [tiles[0]] + [across(tiles[m], "tm", m) for m in range(1, spans)]
+    tiles = [tiles[0]] + [across(tiles[m], "tm", m) for m in range(spans - 1, 0, -1)]
 
     near = run(
         cells_kernel,

time: 39.8 us -> 36.5 us (0.917)
  starting transfers between devices: 20.9 us -> 16.8 us
  waiting for transfers between devices: 13.3 us -> 14.1 us
    ppermute x8, starting transfers between devices: 17.1 us -> 11.6 us  [across(): return lax.ppermute(value, axes, [(i, i ^ m) for i in range(count)])]
    ppermute x1, waiting for transfers between devices: 0.01 us -> 1.84 us  [small_plan(): passed = lax.ppermute(relayed, ('tm', 'chan'), second)]
    ppermute x1, starting transfers between devices: 0.66 us -> 2.09 us  [small_plan(): passed = lax.ppermute(relayed, ('tm', 'chan'), second)]
    ppermute x8, waiting for transfers between devices: 12.3 us -> 11.3 us  [across(): return lax.ppermute(value, axes, [(i, i ^ m) for i in range(count)])]
  transfers between devices with their start and end apart: 11 -> 11, of which waited for: 9 -> 10; matrix products, arithmetic and copies ran while one was open for 0% -> 0% of each run, Pallas kernels for 4% -> 4%
where the time goes in v9:
time: 36.5 us; the launch traced here: 36.4 us
  starting transfers between devices  16.8 us (46%)
  waiting for transfers between devices  14.1 us (39%)
  Pallas kernels  3.79 us (10%)
  local copies, waits for them, and re-layouts  1.51 us (4%)
    ppermute x8, starting transfers between devices, across(): return lax.ppermute(value, axes, [(i, i ^ m) for i in range(count)])  11.6 us
    ppermute x8, waiting for transfers between devices, across(): return lax.ppermute(value, axes, [(i, i ^ m) for i in range(count)])  11.3 us
    pallas_call x10, Pallas kernels, run(): pl.pallas_call(kernel, out_shape=shapes, in_specs=[vmem] * len(operands),...  3.79 us
    ppermute x1, starting transfers between devices, small_plan(): got = lax.ppermute(cells_in, ('tm', 'chan'), first)  3.02 us
    ppermute x1, starting transfers between devices, small_plan(): passed = lax.ppermute(relayed, ('tm', 'chan'), second)  2.09 us
    ppermute x1, waiting for transfers between devices, small_plan(): passed = lax.ppermute(relayed, ('tm', 'chan'), second)  1.84 us
    unnamed x14, local copies, waits for them, and re-layouts  1.51 us
    ppermute x1, waiting for transfers between devices, small_plan(): far = lax.ppermute(near, 'chan', flip)  0.78 us
  transfers between devices with their start and end apart: 11, of which 10 were waited for; matrix products, arithmetic and copies ran while one was open for 0% of the time, Pallas kernels for 4%

profile of v9, /device:TPU:0, one launch (start us, length us, event | category | flops | bytes accessed | tf_op | source)
XLA Modules:
  0.0 36.4 jit_solution(12329937194045570688)
XLA Ops:
  0.0 3.0 %collective-permute-start = (bf16[64,256]{1,0:T(8,128)(2,1)}, bf16[64,256]{1,0:T(8,128)(2,1)S(1)}, u32[]{:S(2)}, u32[]{:S(2)}) collective-permute-start(bf16[64,256]{1,0:T(8,128)(2,1)} %bitcast.5), channel_id=1, source_target_pairs={{0,4},{1,8},{4,0},{5,12},{8,1},{9,13},{12,5},{13,9},{2,6},{3,10},{... | collective-permute-start | bytes 98312 | tf_op jit(solution)/shard_map/ppermute | solution.py:343
  3.0 0.0 copy-start.1
  3.0 1.5 %copy-done.1 = bf16[3,3,3,128,256]{4,3,2,1,0:T(8,128)(2,1)S(1)} copy-done((bf16[3,3,3,128,256]{4,3,2,1,0:T(8,128)(2,1)S(1)}, bf16[3,3,3,128,256]{4,3,2,1,0:T(8,128)(2,1)}, u32[]{:S(2)}) %copy-start.1) | copy-done | bytes 1769496
  4.5 0.4 %shard_map.73.after_ref.weight_ref = bf16[3,3,3,128,256]{4,3,2,1,0:T(8,128)(2,1)S(1)} custom-call(bf16[3,3,3,128,256]{4,3,2,1,0:T(8,128)(2,1)S(1)} %copy-done.1), custom_call_target="tpu_custom_call" | custom-call | bytes 4194304 | tf_op jit(solution)/shard_map/pallas_call | solution.py:315
  4.9 0.0 copy-start.2
  4.9 0.2 collective-permute-done.got_ref
  5.1 2.1 %collective-permute-start.1 = (bf16[64,128]{1,0:T(8,128)(2,1)S(1)}, bf16[64,128]{1,0:T(8,128)(2,1)S(1)}, u32[]{:S(2)}, u32[]{:S(2)}) collective-permute-start(bf16[64,128]{1,0:T(8,128)(2,1)S(1)} %shard_map.74), channel_id=1, source_target_pairs={{0,4},{1,5},{4,0},{5,1},{8,12},{9,13},{12,8},{13,9},{2,6},{3,7},{6... | collective-permute-start | bytes 49160 | tf_op jit(solution)/shard_map/ppermute | solution.py:346
  7.2 1.8 %collective-permute-done.1.passed_ref = bf16[64,128]{1,0:T(8,128)(2,1)S(1)} collective-permute-done((bf16[64,128]{1,0:T(8,128)(2,1)S(1)}, bf16[64,128]{1,0:T(8,128)(2,1)S(1)}, u32[]{:S(2)}, u32[]{:S(2)}) %collective-permute-start.1) | collective-permute-done | bytes 16416 | tf_op jit(solution)/shard_map/ppermute | solution.py:346
  9.1 0.0 copy-done.2
  9.1 1.9 %collective-permute-start.2 = (bf16[2,64,128]{2,1,0:T(8,128)(2,1)S(1)}, bf16[2,64,128]{2,1,0:T(8,128)(2,1)S(1)}, u32[]{:S(2)}, u32[]{:S(2)}) collective-permute-start(bf16[2,64,128]{2,1,0:T(8,128)(2,1)S(1)} %shard_map.75.own_ref), channel_id=1, source_target_pairs={{0,2},{2,0},{1,3},{3,1},{4,6},{6,4},{5,7},{7,5},{8,10},{10,8},{9,1... | collective-permute-start | bytes 98312 | tf_op jit(solution)/shard_map/ppermute | solution.py:350
  11.0 2.1 %collective-permute-done.2.row_ref = bf16[2,64,128]{2,1,0:T(8,128)(2,1)S(1)} collective-permute-done((bf16[2,64,128]{2,1,0:T(8,128)(2,1)S(1)}, bf16[2,64,128]{2,1,0:T(8,128)(2,1)S(1)}, u32[]{:S(2)}, u32[]{:S(2)}) %collective-permute-start.2) | collective-permute-done | bytes 32800 | tf_op jit(solution)/shard_map/ppermute | solution.py:350
  13.1 0.0 copy-start.4
  13.1 0.0 copy-start.5
  13.1 0.0 copy-start.6
  13.1 0.0 copy-start
  13.1 0.0 copy-start.3
  13.1 0.1 collective-permute-start.3
  13.2 1.2 %collective-permute-done.3.far_ref = bf16[2,2,64,128]{3,2,1,0:T(8,128)(2,1)S(1)} collective-permute-done((bf16[2,2,64,128]{3,2,1,0:T(8,128)(2,1)S(1)}, bf16[2,2,64,128]{3,2,1,0:T(8,128)(2,1)S(1)}, u32[]{:S(2)}, u32[]{:S(2)}) %collective-permute-start.3) | collective-permute-done | bytes 65568 | tf_op jit(solution)/shard_map/ppermute | solution.py:350
  14.5 0.7 %shard_map.78 = (bf16[256,128]{1,0:T(8,128)(2,1)S(1)}, bf16[256,128]{1,0:T(8,128)(2,1)S(1)}) custom-call(bf16[2,2,64,128]{3,2,1,0:T(8,128)(2,1)S(1)} %shard_map.76.near_ref, bf16[2,2,64,128]{3,2,1,0:T(8,128)(2,1)S(1)} %collective-permute-done.3.far_ref, bf16[3,3,3,128,256]{4,3,2,1,0:T(8,128)(2,1)S(1)} %shard_map.73.after_ref.weight_ref), custom_call_target="tpu_custom_call" | custom-call | flops 452984832 | bytes 3145728 | tf_op jit(solution)/shard_map/pallas_call | solution.py:315
  15.1 3.3 %collective-permute-start.4 = (bf16[256,128]{1,0:T(8,128)(2,1)S(1)}, bf16[256,128]{1,0:T(8,128)(2,1)S(1)}, u32[]{:S(2)}, u32[]{:S(2)}) collective-permute-start(bf16[256,128]{1,0:T(8,128)(2,1)S(1)} %get-tuple-element.14), channel_id=1, source_target_pairs={{0,8},{4,12},{8,0},{12,4},{1,9},{5,13},{9,1},{13,5},{2,10},{6,14},... | collective-permute-start | bytes 196616 | tf_op jit(solution)/shard_map/ppermute | solution.py:350
  18.5 1.3 %collective-permute-start.5 = (bf16[256,128]{1,0:T(8,128)(2,1)S(1)}, bf16[256,128]{1,0:T(8,128)(2,1)S(1)}, u32[]{:S(2)}, u32[]{:S(2)}) collective-permute-start(bf16[256,128]{1,0:T(8,128)(2,1)S(1)} %get-tuple-element.15), channel_id=1, source_target_pairs={{0,12},{4,8},{8,4},{12,0},{1,13},{5,9},{9,5},{13,1},{2,14},{6,10},... | collective-permute-start | bytes 196616 | tf_op jit(solution)/shard_map/ppermute | solution.py:350
  19.8 0.7 %shard_map.77 = (f32[256,128]{1,0:T(8,128)S(1)}, bf16[256,128]{1,0:T(8,128)(2,1)S(1)}) custom-call(bf16[2,2,64,128]{3,2,1,0:T(8,128)(2,1)S(1)} %shard_map.76.near_ref, bf16[2,2,64,128]{3,2,1,0:T(8,128)(2,1)S(1)} %collective-permute-done.3.far_ref, bf16[3,3,3,128,256]{4,3,2,1,0:T(8,128)(2,1)S(1)} %shard_map.73.after_ref.weight_ref), custom_call_target="tpu_custom_call" | custom-call | flops 452984832 | bytes 3145728 | tf_op jit(solution)/shard_map/pallas_call | solution.py:315
  20.5 0.6 %collective-permute-start.6 = (bf16[256,128]{1,0:T(8,128)(2,1)S(1)}, bf16[256,128]{1,0:T(8,128)(2,1)S(1)}, u32[]{:S(2)}, u32[]{:S(2)}) collective-permute-start(bf16[256,128]{1,0:T(8,128)(2,1)S(1)} %get-tuple-element.16), channel_id=1, source_target_pairs={{0,4},{4,0},{8,12},{12,8},{1,5},{5,1},{9,13},{13,9},{2,6},{6,2},{1... | collective-permute-start | bytes 196616 | tf_op jit(solution)/shard_map/ppermute | solution.py:350
  21.0 1.3 %collective-permute-done.4.refs_1_ = bf16[256,128]{1,0:T(8,128)(2,1)S(1)} collective-permute-done((bf16[256,128]{1,0:T(8,128)(2,1)S(1)}, bf16[256,128]{1,0:T(8,128)(2,1)S(1)}, u32[]{:S(2)}, u32[]{:S(2)}) %collective-permute-start.4) | collective-permute-done | bytes 65568 | tf_op jit(solution)/shard_map/ppermute | solution.py:350
  22.3 2.7 %collective-permute-done.5.refs_2_ = bf16[256,128]{1,0:T(8,128)(2,1)S(1)} collective-permute-done((bf16[256,128]{1,0:T(8,128)(2,1)S(1)}, bf16[256,128]{1,0:T(8,128)(2,1)S(1)}, u32[]{:S(2)}, u32[]{:S(2)}) %collective-permute-start.5) | collective-permute-done | bytes 65568 | tf_op jit(solution)/shard_map/ppermute | solution.py:350
  25.0 0.7 %collective-permute-done.6.refs_3_ = bf16[256,128]{1,0:T(8,128)(2,1)S(1)} collective-permute-done((bf16[256,128]{1,0:T(8,128)(2,1)S(1)}, bf16[256,128]{1,0:T(8,128)(2,1)S(1)}, u32[]{:S(2)}, u32[]{:S(2)}) %collective-permute-start.6) | collective-permute-done | bytes 65568 | tf_op jit(solution)/shard_map/ppermute | solution.py:350
  25.6 0.0 copy-done.4
  25.7 0.0 copy-done.5
  25.7 0.0 copy-done.6
  25.7 0.3 shard_map.79
  26.0 3.1 %collective-permute-start.7 = (bf16[3,32,128]{2,1,0:T(8,128)(2,1)S(1)}, bf16[3,32,128]{2,1,0:T(8,128)(2,1)S(1)}, u32[]{:S(2)}, u32[]{:S(2)}) collective-permute-start(bf16[3,32,128]{2,1,0:T(8,128)(2,1)S(1)} %get-tuple-element.18), channel_id=1, source_target_pairs={{0,12},{4,8},{8,4},{12,0},{1,13},{5,9},{9,5},{13,1},{2,14},{6,10},... | collective-permute-start | bytes 73736 | tf_op jit(solution)/shard_map/ppermute | solution.py:350
  29.1 0.0 collective-permute-start.8
  29.1 1.4 %collective-permute-start.9 = (bf16[3,32,128]{2,1,0:T(8,128)(2,1)S(1)}, bf16[3,32,128]{2,1,0:T(8,128)(2,1)S(1)}, u32[]{:S(2)}, u32[]{:S(2)}) collective-permute-start(bf16[3,32,128]{2,1,0:T(8,128)(2,1)S(1)} %get-tuple-element.20), channel_id=1, source_target_pairs={{0,4},{4,0},{8,12},{12,8},{1,5},{5,1},{9,13},{13,9},{2,6},{6,2},{1... | collective-permute-start | bytes 73736 | tf_op jit(solution)/shard_map/ppermute | solution.py:350
  30.5 1.5 %collective-permute-done.7.refs_1_ = bf16[3,32,128]{2,1,0:T(8,128)(2,1)S(1)} collective-permute-done((bf16[3,32,128]{2,1,0:T(8,128)(2,1)S(1)}, bf16[3,32,128]{2,1,0:T(8,128)(2,1)S(1)}, u32[]{:S(2)}, u32[]{:S(2)}) %collective-permute-start.7) | collective-permute-done | bytes 24608 | tf_op jit(solution)/shard_map/ppermute | solution.py:350
  32.0 1.8 %collective-permute-done.8.refs_2_ = bf16[3,32,128]{2,1,0:T(8,128)(2,1)S(1)} collective-permute-done((bf16[3,32,128]{2,1,0:T(8,128)(2,1)S(1)}, bf16[3,32,128]{2,1,0:T(8,128)(2,1)S(1)}, u32[]{:S(2)}, u32[]{:S(2)}) %collective-permute-start.8) | collective-permute-done | bytes 24608 | tf_op jit(solution)/shard_map/ppermute | solution.py:350
  33.8 0.0 collective-permute-done.9.refs_3_
  33.8 0.1 collective-permute-start.10
  33.9 0.0 copy-done
  33.9 0.0 copy-done.3
  33.9 0.5 %shard_map.81.total_ref = f32[256,256]{1,0:T(8,128)S(1)} custom-call(bf16[3,4,16,256]{3,2,1,0:T(8,128)(2,1)S(1)} %shard_map.80.cells_ref, bf16[3,3,512,256]{3,2,1,0:T(8,128)(2,1)S(1)} %copy-done, f32[1,256]{1,0:T(1,128)S(1)} %bitcast.7), custom_call_target="tpu_custom_call" | custom-call | flops 301989888 | bytes 2097152 | tf_op jit(solution)/shard_map/pallas_call | solution.py:315
  34.4 0.8 %collective-permute-done.10.cells_ref = bf16[3,4,16,256]{3,2,1,0:T(8,128)(2,1)S(1)} collective-permute-done((bf16[3,4,16,256]{3,2,1,0:T(8,128)(2,1)S(1)}, bf16[3,4,16,256]{3,2,1,0:T(8,128)(2,1)S(1)}, u32[]{:S(2)}, u32[]{:S(2)}) %collective-permute-start.10) | collective-permute-done | bytes 98336 | tf_op jit(solution)/shard_map/ppermute | solution.py:387
  35.2 1.2 %shard_map.82 = bf16[2,8,4,4,256]{4,3,2,1,0:T(4,128)(2,1)} custom-call(bf16[3,4,16,256]{3,2,1,0:T(8,128)(2,1)S(1)} %collective-permute-done.10.cells_ref, bf16[3,3,512,256]{3,2,1,0:T(8,128)(2,1)S(1)} %copy-done, f32[256,256]{1,0:T(8,128)S(1)} %shard_map.81.total_ref), custom_call_target="tpu_custom_call" | custom-call | flops 301989888 | bytes 2097152 | tf_op jit(solution)/shard_map/pallas_call | solution.py:315
  (4 shorter events, 0.1 us)
Async XLA Ops:
  0.0 5.1 %collective-permute-start = (bf16[64,256]{1,0:T(8,128)(2,1)}, bf16[64,256]{1,0:T(8,128)(2,1)S(1)}, u32[]{:S(2)}, u32[]{:S(2)}) collective-permute-start(bf16[64,256]{1,0:T(8,128)(2,1)} %bitcast.5), channel_id=1, source_target_pairs={{0,4},{1,8},{4,0},{5,12},{8,1},{9,13},{12,5},{13,9},{2,6},{3,10},{... | collective-permute-start | bytes 98312 | tf_op jit(solution)/shard_map/ppermute | solution.py:343
  3.0 1.5 %copy-start.1 = (bf16[3,3,3,128,256]{4,3,2,1,0:T(8,128)(2,1)S(1)}, bf16[3,3,3,128,256]{4,3,2,1,0:T(8,128)(2,1)}, u32[]{:S(2)}) copy-start(bf16[3,3,3,128,256]{4,3,2,1,0:T(8,128)(2,1)} %weight_ref.3) | copy-start | bytes 5308420
  4.9 4.2 %copy-start.2 = (bf16[2,2,2,8,256]{4,3,2,1,0:T(8,128)(2,1)S(1)}, bf16[2,2,2,8,256]{4,3,2,1,0:T(8,128)(2,1)}, u32[]{:S(2)}) copy-start(bf16[2,2,2,8,256]{4,3,2,1,0:T(8,128)(2,1)} %param.7) | copy-start | bytes 98308
  5.1 3.9 %collective-permute-start.1 = (bf16[64,128]{1,0:T(8,128)(2,1)S(1)}, bf16[64,128]{1,0:T(8,128)(2,1)S(1)}, u32[]{:S(2)}, u32[]{:S(2)}) collective-permute-start(bf16[64,128]{1,0:T(8,128)(2,1)S(1)} %shard_map.74), channel_id=1, source_target_pairs={{0,4},{1,5},{4,0},{5,1},{8,12},{9,13},{12,8},{13,9},{2,6},{3,7},{6... | collective-permute-start | bytes 49160 | tf_op jit(solution)/shard_map/ppermute | solution.py:346
  9.1 4.0 %collective-permute-start.2 = (bf16[2,64,128]{2,1,0:T(8,128)(2,1)S(1)}, bf16[2,64,128]{2,1,0:T(8,128)(2,1)S(1)}, u32[]{:S(2)}, u32[]{:S(2)}) collective-permute-start(bf16[2,64,128]{2,1,0:T(8,128)(2,1)S(1)} %shard_map.75.own_ref), channel_id=1, source_target_pairs={{0,2},{2,0},{1,3},{3,1},{4,6},{6,4},{5,7},{7,5},{8,10},{10,8},{9,1... | collective-permute-start | bytes 98312 | tf_op jit(solution)/shard_map/ppermute | solution.py:350
  13.1 12.6 %copy-start.4 = (f32[256]{0:T(256)S(1)}, f32[256]{0:T(256)}, u32[]{:S(2)}) copy-start(f32[256]{0:T(256)} %param.9) | copy-start | bytes 3076
  13.1 12.6 %copy-start.5 = (f32[256]{0:T(256)S(1)}, f32[256]{0:T(256)}, u32[]{:S(2)}) copy-start(f32[256]{0:T(256)} %param.10) | copy-start | bytes 3076
  13.1 12.6 %copy-start.6 = (f32[256]{0:T(256)S(1)}, f32[256]{0:T(256)}, u32[]{:S(2)}) copy-start(f32[256]{0:T(256)} %param.11) | copy-start | bytes 3076
  13.1 20.8 %copy-start = (bf16[3,3,512,256]{3,2,1,0:T(8,128)(2,1)S(1)}, bf16[3,3,512,256]{3,2,1,0:T(8,128)(2,1)}, u32[]{:S(2)}) copy-start(bf16[3,3,512,256]{3,2,1,0:T(8,128)(2,1)} %weight_ref.5) | copy-start | bytes 7077892
  13.1 20.8 %copy-start.3 = (f32[256]{0:T(256)S(1)}, f32[256]{0:T(256)}, u32[]{:S(2)}) copy-start(f32[256]{0:T(256)} %param.13) | copy-start | bytes 3076
  13.1 1.3 %collective-permute-start.3 = (bf16[2,2,64,128]{3,2,1,0:T(8,128)(2,1)S(1)}, bf16[2,2,64,128]{3,2,1,0:T(8,128)(2,1)S(1)}, u32[]{:S(2)}, u32[]{:S(2)}) collective-permute-start(bf16[2,2,64,128]{3,2,1,0:T(8,128)(2,1)S(1)} %shard_map.76.near_ref), channel_id=1, source_target_pairs={{0,1},{1,0},{2,3},{3,2},{4,5},{5,4},{6,7},{7,6},{8,9},{9,8},{10,11... | collective-permute-start | bytes 196616 | tf_op jit(solution)/shard_map/ppermute | solution.py:350
  15.1 7.1 %collective-permute-start.4 = (bf16[256,128]{1,0:T(8,128)(2,1)S(1)}, bf16[256,128]{1,0:T(8,128)(2,1)S(1)}, u32[]{:S(2)}, u32[]{:S(2)}) collective-permute-start(bf16[256,128]{1,0:T(8,128)(2,1)S(1)} %get-tuple-element.14), channel_id=1, source_target_pairs={{0,8},{4,12},{8,0},{12,4},{1,9},{5,13},{9,1},{13,5},{2,10},{6,14},... | collective-permute-start | bytes 196616 | tf_op jit(solution)/shard_map/ppermute | solution.py:350
  18.5 6.5 %collective-permute-start.5 = (bf16[256,128]{1,0:T(8,128)(2,1)S(1)}, bf16[256,128]{1,0:T(8,128)(2,1)S(1)}, u32[]{:S(2)}, u32[]{:S(2)}) collective-permute-start(bf16[256,128]{1,0:T(8,128)(2,1)S(1)} %get-tuple-element.15), channel_id=1, source_target_pairs={{0,12},{4,8},{8,4},{12,0},{1,13},{5,9},{9,5},{13,1},{2,14},{6,10},... | collective-permute-start | bytes 196616 | tf_op jit(solution)/shard_map/ppermute | solution.py:350
  20.5 5.2 %collective-permute-start.6 = (bf16[256,128]{1,0:T(8,128)(2,1)S(1)}, bf16[256,128]{1,0:T(8,128)(2,1)S(1)}, u32[]{:S(2)}, u32[]{:S(2)}) collective-permute-start(bf16[256,128]{1,0:T(8,128)(2,1)S(1)} %get-tuple-element.16), channel_id=1, source_target_pairs={{0,4},{4,0},{8,12},{12,8},{1,5},{5,1},{9,13},{13,9},{2,6},{6,2},{1... | collective-permute-start | bytes 196616 | tf_op jit(solution)/shard_map/ppermute | solution.py:350
  26.0 5.9 %collective-permute-start.7 = (bf16[3,32,128]{2,1,0:T(8,128)(2,1)S(1)}, bf16[3,32,128]{2,1,0:T(8,128)(2,1)S(1)}, u32[]{:S(2)}, u32[]{:S(2)}) collective-permute-start(bf16[3,32,128]{2,1,0:T(8,128)(2,1)S(1)} %get-tuple-element.18), channel_id=1, source_target_pairs={{0,12},{4,8},{8,4},{12,0},{1,13},{5,9},{9,5},{13,1},{2,14},{6,10},... | collective-permute-start | bytes 73736 | tf_op jit(solution)/shard_map/ppermute | solution.py:350
  29.1 4.7 %collective-permute-start.8 = (bf16[3,32,128]{2,1,0:T(8,128)(2,1)S(1)}, bf16[3,32,128]{2,1,0:T(8,128)(2,1)S(1)}, u32[]{:S(2)}, u32[]{:S(2)}) collective-permute-start(bf16[3,32,128]{2,1,0:T(8,128)(2,1)S(1)} %get-tuple-element.19), channel_id=1, source_target_pairs={{0,8},{4,12},{8,0},{12,4},{1,9},{5,13},{9,1},{13,5},{2,10},{6,14},... | collective-permute-start | bytes 73736 | tf_op jit(solution)/shard_map/ppermute | solution.py:350
  29.1 4.7 %collective-permute-start.9 = (bf16[3,32,128]{2,1,0:T(8,128)(2,1)S(1)}, bf16[3,32,128]{2,1,0:T(8,128)(2,1)S(1)}, u32[]{:S(2)}, u32[]{:S(2)}) collective-permute-start(bf16[3,32,128]{2,1,0:T(8,128)(2,1)S(1)} %get-tuple-element.20), channel_id=1, source_target_pairs={{0,4},{4,0},{8,12},{12,8},{1,5},{5,1},{9,13},{13,9},{2,6},{6,2},{1... | collective-permute-start | bytes 73736 | tf_op jit(solution)/shard_map/ppermute | solution.py:350
  33.8 1.4 %collective-permute-start.10 = (bf16[3,4,16,256]{3,2,1,0:T(8,128)(2,1)S(1)}, bf16[3,4,16,256]{3,2,1,0:T(8,128)(2,1)S(1)}, u32[]{:S(2)}, u32[]{:S(2)}) collective-permute-start(bf16[3,4,16,256]{3,2,1,0:T(8,128)(2,1)S(1)} %shard_map.80.cells_ref), channel_id=1, source_target_pairs={{0,1},{1,0},{2,3},{3,2},{4,5},{5,4},{6,7},{7,6},{8,9},{9,8},{10,11... | collective-permute-start | bytes 294920 | tf_op jit(solution)/shard_map/ppermute | solution.py:387

commit v10 on v5

--- a/solution.py
+++ b/solution.py
@@ -132,13 +132,20 @@
     copy.wait()
 
 
-def select_kernel(first_ref, second_ref, after_ref, out_ref):
+def relay_kernel(got_ref, after_ref, out_ref):
     del after_ref
     tm, _, _ = placed_at()
+    depth = out_ref.shape[1]
+    out_ref[...] = jnp.where(tm % 2 > 0, got_ref[:, :depth], got_ref[:, depth:])
+
+
+def select_kernel(own_ref, got_ref, passed_ref, out_ref):
+    tm, _, chan = placed_at()
     depth = out_ref.shape[2]
-    upper = tm % 2 > 0
-    for i, ref in enumerate((first_ref, second_ref)):
-        out_ref[i] = jnp.where(upper, ref[:, depth:], ref[:, :depth])
+    upper, home = tm % 2 > 0, chan == tm // 2
+    out_ref[0] = jnp.where(upper, got_ref[:, depth:], got_ref[:, :depth])
+    own = jnp.where(upper, own_ref[:, depth:], own_ref[:, :depth])
+    out_ref[1] = jnp.where(home, own, passed_ref[...])
 
 
 def conv_of_clip(clip, got, weight_ref, latents, taps):
@@ -323,18 +330,19 @@
     flip = ((0, 1), (1, 0))
 
     cells_in = latents.reshape(clips * span * rows * cols, half)
-    turns = ((1, 2), (0, 3))
-    got = []
-    for at_home, across in turns:
-        pairs = []
-        for source in range(spans):
-            for chan in range(chans):
-                home = chan == source // 2
-                target = (source ^ at_home, chan) if home else (source ^ across, 1 - chan)
-                pairs.append((source * chans + chan, target[0] * chans + target[1]))
-        got.append(lax.ppermute(cells_in, ("tm", "chan"), pairs))
+    first, second = [], []
+    for source in range(spans):
+        for chan in range(chans):
+            home = chan == source // 2
+            target = (source ^ 1, chan) if home else (source ^ 2, 1 - chan)
+            first.append((source * chans + chan, target[0] * chans + target[1]))
+            second.append((source * chans + chan, (source ^ 1) * chans + chan))
+    got = lax.ppermute(cells_in, ("tm", "chan"), first)
     weight = run(fetch_kernel, shape(conv_weight.shape, low), [pltpu.SemaphoreType.DMA], conv_weight, moved=4 << 20)
-    own = run(select_kernel, shape((2, cells_in.shape[0], depth), low), [], *got, weight, moved=1 << 17)
+    relayed = run(relay_kernel, shape((cells_in.shape[0], depth), low), [], got, weight, moved=1 << 17)
+    passed = lax.ppermute(relayed, ("tm", "chan"), second)
+
+    own = run(select_kernel, shape((2, cells_in.shape[0], depth), low), [], cells_in, got, passed, moved=1 << 17)
     every = [own] + [
         lax.ppermute(own, ("space", "chan"), [(i, i ^ m) for i in range(spaces * chans)]) for m in range(1, spaces * chans)
     ]

time: 35.5 us -> 36.4 us (1.025)
  waiting for transfers between devices: 10.6 us -> 14.3 us
  starting transfers between devices: 19.2 us -> 16.5 us
    ppermute x3, starting transfers between devices: 6.63 us -> 2.03 us  [small_plan(): lax.ppermute(own, ('space', 'chan'), [(i, i ^ m) for i in range(spaces *...]
    ppermute x2, starting transfers between devices: 2.2 us -> 4.31 us  [small_plan(): lax.ppermute(value, 'tm', [(i, i ^ m) for i in range(spans)])]
    ppermute x2, waiting for transfers between devices: 0.01 us -> 2.08 us  [the longest x1 1.84 us: small_plan(): passed = lax.ppermute(relayed, ('tm', 'chan'), second)]
    ppermute x3, waiting for transfers between devices: 1.93 us -> 3.54 us  [small_plan(): lax.ppermute(tiles[m], 'tm', [(i, i ^ m) for i in range(spans)])]
    ppermute x1, starting transfers between devices: 1.42 us -> 0.55 us  [small_plan(): lax.ppermute(near_other, 'tm', [(i, i ^ 1) for i in range(spans)])]
    ppermute x2, waiting for transfers between devices: 3.08 us -> 3.91 us  [small_plan(): lax.ppermute(value, 'tm', [(i, i ^ m) for i in range(spans)])]
    ppermute x2, starting transfers between devices: 4.43 us -> 5.11 us  [the longest x1 3.02 us: small_plan(): got = lax.ppermute(cells_in, ('tm', 'chan'), first)]
    ppermute x1, waiting for transfers between devices: 1.16 us -> 0.72 us  [small_plan(): lax.ppermute(near_other, 'tm', [(i, i ^ 1) for i in range(spans)])]
  transfers between devices with their start and end apart: 12 -> 12, of which waited for: 7 -> 11; matrix products, arithmetic and copies ran while one was open for 0% -> 0% of each run, Pallas kernels for 4% -> 4%
where the time goes in v10:
time: 36.4 us; the launch traced here: 36.3 us
  starting transfers between devices  16.5 us (45%)
  waiting for transfers between devices  14.3 us (39%)
  Pallas kernels  3.79 us (10%)
  local copies, waits for them, and re-layouts  1.51 us (4%)
    ppermute x3, starting transfers between devices, small_plan(): lax.ppermute(tiles[m], 'tm', [(i, i ^ m) for i in range(spans)])  4.45 us
    ppermute x2, starting transfers between devices, small_plan(): lax.ppermute(value, 'tm', [(i, i ^ m) for i in range(spans)])  4.31 us
    ppermute x2, waiting for transfers between devices, small_plan(): lax.ppermute(value, 'tm', [(i, i ^ m) for i in range(spans)])  3.91 us
    pallas_call x9, Pallas kernels, run(): pl.pallas_call(kernel, out_shape=shapes, in_specs=[vmem] * len(operands),...  3.79 us
    ppermute x3, waiting for transfers between devices, small_plan(): lax.ppermute(tiles[m], 'tm', [(i, i ^ m) for i in range(spans)])  3.54 us
    ppermute x3, waiting for transfers between devices, small_plan(): lax.ppermute(own, ('space', 'chan'), [(i, i ^ m) for i in range(spaces *...  3.27 us
    ppermute x1, starting transfers between devices, small_plan(): got = lax.ppermute(cells_in, ('tm', 'chan'), first)  3.02 us
    ppermute x1, starting transfers between devices, small_plan(): passed = lax.ppermute(relayed, ('tm', 'chan'), second)  2.09 us
  transfers between devices with their start and end apart: 12, of which 11 were waited for; matrix products, arithmetic and copies ran while one was open for 0% of the time, Pallas kernels for 4%

profile of v10, /device:TPU:0, one launch (start us, length us, event | category | flops | bytes accessed | tf_op | source)
XLA Modules:
  0.0 36.3 jit_solution(1324991117269221533)
XLA Ops:
  0.0 3.0 %collective-permute-start = (bf16[64,256]{1,0:T(8,128)(2,1)}, bf16[64,256]{1,0:T(8,128)(2,1)S(1)}, u32[]{:S(2)}, u32[]{:S(2)}) collective-permute-start(bf16[64,256]{1,0:T(8,128)(2,1)} %bitcast.5), channel_id=1, source_target_pairs={{0,4},{1,8},{4,0},{5,12},{8,1},{9,13},{12,5},{13,9},{2,6},{3,10},{... | collective-permute-start | bytes 98312 | tf_op jit(solution)/shard_map/ppermute | solution.py:340
  3.0 0.0 copy-start.1
  3.0 1.5 %copy-done.1 = bf16[3,3,3,128,256]{4,3,2,1,0:T(8,128)(2,1)S(1)} copy-done((bf16[3,3,3,128,256]{4,3,2,1,0:T(8,128)(2,1)S(1)}, bf16[3,3,3,128,256]{4,3,2,1,0:T(8,128)(2,1)}, u32[]{:S(2)}) %copy-start.1) | copy-done | bytes 1769496
  4.5 0.4 %shard_map.73.after_ref.weight_ref = bf16[3,3,3,128,256]{4,3,2,1,0:T(8,128)(2,1)S(1)} custom-call(bf16[3,3,3,128,256]{4,3,2,1,0:T(8,128)(2,1)S(1)} %copy-done.1), custom_call_target="tpu_custom_call" | custom-call | bytes 4194304 | tf_op jit(solution)/shard_map/pallas_call | solution.py:312
  4.9 0.0 copy-start.2
  4.9 0.2 collective-permute-done.got_ref
  5.1 2.1 %collective-permute-start.1 = (bf16[64,128]{1,0:T(8,128)(2,1)S(1)}, bf16[64,128]{1,0:T(8,128)(2,1)S(1)}, u32[]{:S(2)}, u32[]{:S(2)}) collective-permute-start(bf16[64,128]{1,0:T(8,128)(2,1)S(1)} %shard_map.74), channel_id=1, source_target_pairs={{0,4},{1,5},{4,0},{5,1},{8,12},{9,13},{12,8},{13,9},{2,6},{3,7},{6... | collective-permute-start | bytes 49160 | tf_op jit(solution)/shard_map/ppermute | solution.py:343
  7.2 1.8 %collective-permute-done.1.passed_ref = bf16[64,128]{1,0:T(8,128)(2,1)S(1)} collective-permute-done((bf16[64,128]{1,0:T(8,128)(2,1)S(1)}, bf16[64,128]{1,0:T(8,128)(2,1)S(1)}, u32[]{:S(2)}, u32[]{:S(2)}) %collective-permute-start.1) | collective-permute-done | bytes 16416 | tf_op jit(solution)/shard_map/ppermute | solution.py:343
  9.1 0.0 copy-done.2
  9.1 0.0 copy-start.4
  9.1 0.0 copy-start.5
  9.1 0.0 copy-start.6
  9.1 0.0 copy-start
  9.1 0.0 copy-start.3
  9.2 0.1 collective-permute-start.2
  9.3 1.8 %collective-permute-start.3 = (bf16[2,64,128]{2,1,0:T(8,128)(2,1)S(1)}, bf16[2,64,128]{2,1,0:T(8,128)(2,1)S(1)}, u32[]{:S(2)}, u32[]{:S(2)}) collective-permute-start(bf16[2,64,128]{2,1,0:T(8,128)(2,1)S(1)} %shard_map.75.own_ref), channel_id=1, source_target_pairs={{0,2},{1,3},{2,0},{3,1},{4,6},{5,7},{6,4},{7,5},{8,10},{9,11},{10,... | collective-permute-start | bytes 98312 | tf_op jit(solution)/shard_map/ppermute | solution.py:347
  11.1 0.1 collective-permute-start.4
  11.2 0.0 collective-permute-done.2.core_ref
  11.2 2.0 %collective-permute-done.3.row_ref = bf16[2,64,128]{2,1,0:T(8,128)(2,1)S(1)} collective-permute-done((bf16[2,64,128]{2,1,0:T(8,128)(2,1)S(1)}, bf16[2,64,128]{2,1,0:T(8,128)(2,1)S(1)}, u32[]{:S(2)}, u32[]{:S(2)}) %collective-permute-start.3) | collective-permute-done | bytes 32800 | tf_op jit(solution)/shard_map/ppermute | solution.py:347
  13.2 1.2 %collective-permute-done.4.both_ref = bf16[2,64,128]{2,1,0:T(8,128)(2,1)S(1)} collective-permute-done((bf16[2,64,128]{2,1,0:T(8,128)(2,1)S(1)}, bf16[2,64,128]{2,1,0:T(8,128)(2,1)S(1)}, u32[]{:S(2)}, u32[]{:S(2)}) %collective-permute-start.4) | collective-permute-done | bytes 32800 | tf_op jit(solution)/shard_map/ppermute | solution.py:347
  14.5 0.7 %shard_map.77 = (bf16[256,128]{1,0:T(8,128)(2,1)S(1)}, bf16[256,128]{1,0:T(8,128)(2,1)S(1)}) custom-call(bf16[2,64,128]{2,1,0:T(8,128)(2,1)S(1)} %shard_map.75.own_ref, bf16[2,64,128]{2,1,0:T(8,128)(2,1)S(1)} %collective-permute-done.2.core_ref, bf16[2,64,128]{2,1,0:T(8,128)(2,1)S(1)} %collective-permute-done.3.row_ref, ...), custom_call_target="tpu_custom_call" | custom-call | flops 452984832 | bytes 3145728 | tf_op jit(solution)/shard_map/pallas_call | solution.py:312
  15.2 3.0 %collective-permute-start.5 = (bf16[256,128]{1,0:T(8,128)(2,1)S(1)}, bf16[256,128]{1,0:T(8,128)(2,1)S(1)}, u32[]{:S(2)}, u32[]{:S(2)}) collective-permute-start(bf16[256,128]{1,0:T(8,128)(2,1)S(1)} %get-tuple-element.14), channel_id=1, source_target_pairs={{0,8},{4,12},{8,0},{12,4},{1,9},{5,13},{9,1},{13,5},{2,10},{6,14},... | collective-permute-start | bytes 196616 | tf_op jit(solution)/shard_map/ppermute | solution.py:361
  18.2 1.3 %collective-permute-start.6 = (bf16[256,128]{1,0:T(8,128)(2,1)S(1)}, bf16[256,128]{1,0:T(8,128)(2,1)S(1)}, u32[]{:S(2)}, u32[]{:S(2)}) collective-permute-start(bf16[256,128]{1,0:T(8,128)(2,1)S(1)} %get-tuple-element.15), channel_id=1, source_target_pairs={{0,12},{4,8},{8,4},{12,0},{1,13},{5,9},{9,5},{13,1},{2,14},{6,10},... | collective-permute-start | bytes 196616 | tf_op jit(solution)/shard_map/ppermute | solution.py:361
  19.5 0.7 %shard_map.76 = (f32[256,128]{1,0:T(8,128)S(1)}, bf16[256,128]{1,0:T(8,128)(2,1)S(1)}) custom-call(bf16[2,64,128]{2,1,0:T(8,128)(2,1)S(1)} %shard_map.75.own_ref, bf16[2,64,128]{2,1,0:T(8,128)(2,1)S(1)} %collective-permute-done.2.core_ref, bf16[2,64,128]{2,1,0:T(8,128)(2,1)S(1)} %collective-permute-done.3.row_ref, ...), custom_call_target="tpu_custom_call" | custom-call | flops 452984832 | bytes 3145728 | tf_op jit(solution)/shard_map/pallas_call | solution.py:312
  20.2 0.6 %collective-permute-start.7 = (bf16[256,128]{1,0:T(8,128)(2,1)S(1)}, bf16[256,128]{1,0:T(8,128)(2,1)S(1)}, u32[]{:S(2)}, u32[]{:S(2)}) collective-permute-start(bf16[256,128]{1,0:T(8,128)(2,1)S(1)} %get-tuple-element.16), channel_id=1, source_target_pairs={{0,4},{4,0},{8,12},{12,8},{1,5},{5,1},{9,13},{13,9},{2,6},{6,2},{1... | collective-permute-start | bytes 196616 | tf_op jit(solution)/shard_map/ppermute | solution.py:366
  20.7 1.3 %collective-permute-done.5.refs_1_ = bf16[256,128]{1,0:T(8,128)(2,1)S(1)} collective-permute-done((bf16[256,128]{1,0:T(8,128)(2,1)S(1)}, bf16[256,128]{1,0:T(8,128)(2,1)S(1)}, u32[]{:S(2)}, u32[]{:S(2)}) %collective-permute-start.5) | collective-permute-done | bytes 65568 | tf_op jit(solution)/shard_map/ppermute | solution.py:361
  22.0 2.6 %collective-permute-done.6.refs_2_ = bf16[256,128]{1,0:T(8,128)(2,1)S(1)} collective-permute-done((bf16[256,128]{1,0:T(8,128)(2,1)S(1)}, bf16[256,128]{1,0:T(8,128)(2,1)S(1)}, u32[]{:S(2)}, u32[]{:S(2)}) %collective-permute-start.6) | collective-permute-done | bytes 65568 | tf_op jit(solution)/shard_map/ppermute | solution.py:361
  24.6 0.7 %collective-permute-done.7.refs_3_ = bf16[256,128]{1,0:T(8,128)(2,1)S(1)} collective-permute-done((bf16[256,128]{1,0:T(8,128)(2,1)S(1)}, bf16[256,128]{1,0:T(8,128)(2,1)S(1)}, u32[]{:S(2)}, u32[]{:S(2)}) %collective-permute-start.7) | collective-permute-done | bytes 65568 | tf_op jit(solution)/shard_map/ppermute | solution.py:366
  25.3 0.0 copy-done.4
  25.3 0.0 copy-done.5
  25.3 0.0 copy-done.6
  25.4 0.3 shard_map.78
  25.7 3.1 %collective-permute-start.10 = (bf16[3,32,128]{2,1,0:T(8,128)(2,1)S(1)}, bf16[3,32,128]{2,1,0:T(8,128)(2,1)S(1)}, u32[]{:S(2)}, u32[]{:S(2)}) collective-permute-start(bf16[3,32,128]{2,1,0:T(8,128)(2,1)S(1)} %get-tuple-element.20), channel_id=1, source_target_pairs={{0,12},{4,8},{8,4},{12,0},{1,13},{5,9},{9,5},{13,1},{2,14},{6,10},... | collective-permute-start | bytes 73736 | tf_op jit(solution)/shard_map/ppermute | solution.py:378
  28.8 0.0 collective-permute-start.8
  28.8 1.4 %collective-permute-start.9 = (bf16[3,32,128]{2,1,0:T(8,128)(2,1)S(1)}, bf16[3,32,128]{2,1,0:T(8,128)(2,1)S(1)}, u32[]{:S(2)}, u32[]{:S(2)}) collective-permute-start(bf16[3,32,128]{2,1,0:T(8,128)(2,1)S(1)} %get-tuple-element.19), channel_id=1, source_target_pairs={{0,8},{4,12},{8,0},{12,4},{1,9},{5,13},{9,1},{13,5},{2,10},{6,14},... | collective-permute-start | bytes 73736 | tf_op jit(solution)/shard_map/ppermute | solution.py:378
  30.2 1.3 %collective-permute-done.10.refs_3_ = bf16[3,32,128]{2,1,0:T(8,128)(2,1)S(1)} collective-permute-done((bf16[3,32,128]{2,1,0:T(8,128)(2,1)S(1)}, bf16[3,32,128]{2,1,0:T(8,128)(2,1)S(1)}, u32[]{:S(2)}, u32[]{:S(2)}) %collective-permute-start.10) | collective-permute-done | bytes 24608 | tf_op jit(solution)/shard_map/ppermute | solution.py:378
  31.5 1.1 %collective-permute-done.8.refs_1_ = bf16[3,32,128]{2,1,0:T(8,128)(2,1)S(1)} collective-permute-done((bf16[3,32,128]{2,1,0:T(8,128)(2,1)S(1)}, bf16[3,32,128]{2,1,0:T(8,128)(2,1)S(1)}, u32[]{:S(2)}, u32[]{:S(2)}) %collective-permute-start.8) | collective-permute-done | bytes 24608 | tf_op jit(solution)/shard_map/ppermute | solution.py:378
  32.6 1.1 %collective-permute-done.9.refs_2_ = bf16[3,32,128]{2,1,0:T(8,128)(2,1)S(1)} collective-permute-done((bf16[3,32,128]{2,1,0:T(8,128)(2,1)S(1)}, bf16[3,32,128]{2,1,0:T(8,128)(2,1)S(1)}, u32[]{:S(2)}, u32[]{:S(2)}) %collective-permute-start.9) | collective-permute-done | bytes 24608 | tf_op jit(solution)/shard_map/ppermute | solution.py:378
  33.7 0.1 collective-permute-start.11
  33.8 0.0 copy-done
  33.8 0.0 copy-done.3
  33.8 0.5 %shard_map.80.total_ref = f32[256,256]{1,0:T(8,128)S(1)} custom-call(bf16[3,4,16,256]{3,2,1,0:T(8,128)(2,1)S(1)} %shard_map.79.cells_ref, bf16[3,3,512,256]{3,2,1,0:T(8,128)(2,1)S(1)} %copy-done, f32[1,256]{1,0:T(1,128)S(1)} %bitcast.7), custom_call_target="tpu_custom_call" | custom-call | flops 301989888 | bytes 2097152 | tf_op jit(solution)/shard_map/pallas_call | solution.py:312
  34.3 0.8 %collective-permute-done.11.cells_ref = bf16[3,4,16,256]{3,2,1,0:T(8,128)(2,1)S(1)} collective-permute-done((bf16[3,4,16,256]{3,2,1,0:T(8,128)(2,1)S(1)}, bf16[3,4,16,256]{3,2,1,0:T(8,128)(2,1)S(1)}, u32[]{:S(2)}, u32[]{:S(2)}) %collective-permute-start.11) | collective-permute-done | bytes 98336 | tf_op jit(solution)/shard_map/ppermute | solution.py:388
  35.1 1.2 %shard_map.81 = bf16[2,8,4,4,256]{4,3,2,1,0:T(4,128)(2,1)} custom-call(bf16[3,4,16,256]{3,2,1,0:T(8,128)(2,1)S(1)} %collective-permute-done.11.cells_ref, bf16[3,3,512,256]{3,2,1,0:T(8,128)(2,1)S(1)} %copy-done, f32[256,256]{1,0:T(8,128)S(1)} %shard_map.80.total_ref), custom_call_target="tpu_custom_call" | custom-call | flops 301989888 | bytes 2097152 | tf_op jit(solution)/shard_map/pallas_call | solution.py:312
  (3 shorter events, 0.1 us)
Async XLA Ops:
  0.0 5.1 %collective-permute-start = (bf16[64,256]{1,0:T(8,128)(2,1)}, bf16[64,256]{1,0:T(8,128)(2,1)S(1)}, u32[]{:S(2)}, u32[]{:S(2)}) collective-permute-start(bf16[64,256]{1,0:T(8,128)(2,1)} %bitcast.5), channel_id=1, source_target_pairs={{0,4},{1,8},{4,0},{5,12},{8,1},{9,13},{12,5},{13,9},{2,6},{3,10},{... | collective-permute-start | bytes 98312 | tf_op jit(solution)/shard_map/ppermute | solution.py:340
  3.0 1.5 %copy-start.1 = (bf16[3,3,3,128,256]{4,3,2,1,0:T(8,128)(2,1)S(1)}, bf16[3,3,3,128,256]{4,3,2,1,0:T(8,128)(2,1)}, u32[]{:S(2)}) copy-start(bf16[3,3,3,128,256]{4,3,2,1,0:T(8,128)(2,1)} %weight_ref.3) | copy-start | bytes 5308420
  4.9 4.2 %copy-start.2 = (bf16[2,2,2,8,256]{4,3,2,1,0:T(8,128)(2,1)S(1)}, bf16[2,2,2,8,256]{4,3,2,1,0:T(8,128)(2,1)}, u32[]{:S(2)}) copy-start(bf16[2,2,2,8,256]{4,3,2,1,0:T(8,128)(2,1)} %param.7) | copy-start | bytes 98308
  5.1 3.9 %collective-permute-start.1 = (bf16[64,128]{1,0:T(8,128)(2,1)S(1)}, bf16[64,128]{1,0:T(8,128)(2,1)S(1)}, u32[]{:S(2)}, u32[]{:S(2)}) collective-permute-start(bf16[64,128]{1,0:T(8,128)(2,1)S(1)} %shard_map.74), channel_id=1, source_target_pairs={{0,4},{1,5},{4,0},{5,1},{8,12},{9,13},{12,8},{13,9},{2,6},{3,7},{6... | collective-permute-start | bytes 49160 | tf_op jit(solution)/shard_map/ppermute | solution.py:343
  9.1 16.3 %copy-start.4 = (f32[256]{0:T(256)S(1)}, f32[256]{0:T(256)}, u32[]{:S(2)}) copy-start(f32[256]{0:T(256)} %param.9) | copy-start | bytes 3076
  9.1 16.2 %copy-start.5 = (f32[256]{0:T(256)S(1)}, f32[256]{0:T(256)}, u32[]{:S(2)}) copy-start(f32[256]{0:T(256)} %param.10) | copy-start | bytes 3076
  9.1 16.2 %copy-start.6 = (f32[256]{0:T(256)S(1)}, f32[256]{0:T(256)}, u32[]{:S(2)}) copy-start(f32[256]{0:T(256)} %param.11) | copy-start | bytes 3076
  9.1 24.7 %copy-start = (bf16[3,3,512,256]{3,2,1,0:T(8,128)(2,1)S(1)}, bf16[3,3,512,256]{3,2,1,0:T(8,128)(2,1)}, u32[]{:S(2)}) copy-start(bf16[3,3,512,256]{3,2,1,0:T(8,128)(2,1)} %weight_ref.5) | copy-start | bytes 7077892
  9.1 24.7 %copy-start.3 = (f32[256]{0:T(256)S(1)}, f32[256]{0:T(256)}, u32[]{:S(2)}) copy-start(f32[256]{0:T(256)} %param.13) | copy-start | bytes 3076
  9.2 2.0 %collective-permute-start.2 = (bf16[2,64,128]{2,1,0:T(8,128)(2,1)S(1)}, bf16[2,64,128]{2,1,0:T(8,128)(2,1)S(1)}, u32[]{:S(2)}, u32[]{:S(2)}) collective-permute-start(bf16[2,64,128]{2,1,0:T(8,128)(2,1)S(1)} %shard_map.75.own_ref), channel_id=1, source_target_pairs={{0,1},{1,0},{2,3},{3,2},{4,5},{5,4},{6,7},{7,6},{8,9},{9,8},{10,11... | collective-permute-start | bytes 98312 | tf_op jit(solution)/shard_map/ppermute | solution.py:347
  9.3 3.9 %collective-permute-start.3 = (bf16[2,64,128]{2,1,0:T(8,128)(2,1)S(1)}, bf16[2,64,128]{2,1,0:T(8,128)(2,1)S(1)}, u32[]{:S(2)}, u32[]{:S(2)}) collective-permute-start(bf16[2,64,128]{2,1,0:T(8,128)(2,1)S(1)} %shard_map.75.own_ref), channel_id=1, source_target_pairs={{0,2},{1,3},{2,0},{3,1},{4,6},{5,7},{6,4},{7,5},{8,10},{9,11},{10,... | collective-permute-start | bytes 98312 | tf_op jit(solution)/shard_map/ppermute | solution.py:347
  11.1 3.3 %collective-permute-start.4 = (bf16[2,64,128]{2,1,0:T(8,128)(2,1)S(1)}, bf16[2,64,128]{2,1,0:T(8,128)(2,1)S(1)}, u32[]{:S(2)}, u32[]{:S(2)}) collective-permute-start(bf16[2,64,128]{2,1,0:T(8,128)(2,1)S(1)} %shard_map.75.own_ref), channel_id=1, source_target_pairs={{0,3},{1,2},{2,1},{3,0},{4,7},{5,6},{6,5},{7,4},{8,11},{9,10},{10,... | collective-permute-start | bytes 98312 | tf_op jit(solution)/shard_map/ppermute | solution.py:347
  15.2 6.8 %collective-permute-start.5 = (bf16[256,128]{1,0:T(8,128)(2,1)S(1)}, bf16[256,128]{1,0:T(8,128)(2,1)S(1)}, u32[]{:S(2)}, u32[]{:S(2)}) collective-permute-start(bf16[256,128]{1,0:T(8,128)(2,1)S(1)} %get-tuple-element.14), channel_id=1, source_target_pairs={{0,8},{4,12},{8,0},{12,4},{1,9},{5,13},{9,1},{13,5},{2,10},{6,14},... | collective-permute-start | bytes 196616 | tf_op jit(solution)/shard_map/ppermute | solution.py:361
  18.2 6.5 %collective-permute-start.6 = (bf16[256,128]{1,0:T(8,128)(2,1)S(1)}, bf16[256,128]{1,0:T(8,128)(2,1)S(1)}, u32[]{:S(2)}, u32[]{:S(2)}) collective-permute-start(bf16[256,128]{1,0:T(8,128)(2,1)S(1)} %get-tuple-element.15), channel_id=1, source_target_pairs={{0,12},{4,8},{8,4},{12,0},{1,13},{5,9},{9,5},{13,1},{2,14},{6,10},... | collective-permute-start | bytes 196616 | tf_op jit(solution)/shard_map/ppermute | solution.py:361
  20.2 5.2 %collective-permute-start.7 = (bf16[256,128]{1,0:T(8,128)(2,1)S(1)}, bf16[256,128]{1,0:T(8,128)(2,1)S(1)}, u32[]{:S(2)}, u32[]{:S(2)}) collective-permute-start(bf16[256,128]{1,0:T(8,128)(2,1)S(1)} %get-tuple-element.16), channel_id=1, source_target_pairs={{0,4},{4,0},{8,12},{12,8},{1,5},{5,1},{9,13},{13,9},{2,6},{6,2},{1... | collective-permute-start | bytes 196616 | tf_op jit(solution)/shard_map/ppermute | solution.py:366
  25.7 5.8 %collective-permute-start.10 = (bf16[3,32,128]{2,1,0:T(8,128)(2,1)S(1)}, bf16[3,32,128]{2,1,0:T(8,128)(2,1)S(1)}, u32[]{:S(2)}, u32[]{:S(2)}) collective-permute-start(bf16[3,32,128]{2,1,0:T(8,128)(2,1)S(1)} %get-tuple-element.20), channel_id=1, source_target_pairs={{0,12},{4,8},{8,4},{12,0},{1,13},{5,9},{9,5},{13,1},{2,14},{6,10},... | collective-permute-start | bytes 73736 | tf_op jit(solution)/shard_map/ppermute | solution.py:378
  28.8 3.8 %collective-permute-start.8 = (bf16[3,32,128]{2,1,0:T(8,128)(2,1)S(1)}, bf16[3,32,128]{2,1,0:T(8,128)(2,1)S(1)}, u32[]{:S(2)}, u32[]{:S(2)}) collective-permute-start(bf16[3,32,128]{2,1,0:T(8,128)(2,1)S(1)} %get-tuple-element.18), channel_id=1, source_target_pairs={{0,4},{4,0},{8,12},{12,8},{1,5},{5,1},{9,13},{13,9},{2,6},{6,2},{1... | collective-permute-start | bytes 73736 | tf_op jit(solution)/shard_map/ppermute | solution.py:378
  28.8 4.9 %collective-permute-start.9 = (bf16[3,32,128]{2,1,0:T(8,128)(2,1)S(1)}, bf16[3,32,128]{2,1,0:T(8,128)(2,1)S(1)}, u32[]{:S(2)}, u32[]{:S(2)}) collective-permute-start(bf16[3,32,128]{2,1,0:T(8,128)(2,1)S(1)} %get-tuple-element.19), channel_id=1, source_target_pairs={{0,8},{4,12},{8,0},{12,4},{1,9},{5,13},{9,1},{13,5},{2,10},{6,14},... | collective-permute-start | bytes 73736 | tf_op jit(solution)/shard_map/ppermute | solution.py:378
  33.7 1.4 %collective-permute-start.11 = (bf16[3,4,16,256]{3,2,1,0:T(8,128)(2,1)S(1)}, bf16[3,4,16,256]{3,2,1,0:T(8,128)(2,1)S(1)}, u32[]{:S(2)}, u32[]{:S(2)}) collective-permute-start(bf16[3,4,16,256]{3,2,1,0:T(8,128)(2,1)S(1)} %shard_map.79.cells_ref), channel_id=1, source_target_pairs={{0,1},{1,0},{2,3},{3,2},{4,5},{5,4},{6,7},{7,6},{8,9},{9,8},{10,11... | collective-permute-start | bytes 294920 | tf_op jit(solution)/shard_map/ppermute | solution.py:388

commit v11 on v6

--- a/solution.py
+++ b/solution.py
@@ -186,27 +186,23 @@
     return jnp.where(swapped, upper, lower), jnp.where(swapped, lower, upper)
 
 
-def conv_far_kernel(near_ref, far_ref, weight_ref, keep_ref, sent_ref, latents, taps):
+def conv_far_kernel(near_ref, far_ref, weight_ref, same_ref, other_ref, latents, taps):
     tm, _, _ = placed_at()
-    keep, sent = conv_of_clip(1 - tm // 2, near_ref, far_ref, weight_ref, latents, taps)
+    same, other = conv_of_clip(1 - tm // 2, near_ref, far_ref, weight_ref, latents, taps)
+    same_ref[...] = same.astype(same_ref.dtype)
+    other_ref[...] = other.astype(other_ref.dtype)
+
+
+def conv_near_kernel(near_ref, far_ref, weight_ref, keep_ref, other_ref, latents, taps):
+    tm, _, _ = placed_at()
+    keep, other = conv_of_clip(tm // 2, near_ref, far_ref, weight_ref, latents, taps)
     keep_ref[...] = keep
-    sent_ref[...] = sent.astype(sent_ref.dtype)
-
-
-def conv_near_kernel(near_ref, far_ref, weight_ref, keep_ref, sent_ref, latents, taps):
-    tm, _, _ = placed_at()
-    keep, sent = conv_of_clip(tm // 2, near_ref, far_ref, weight_ref, latents, taps)
-    keep_ref[...] = keep
-    sent_ref[...] = sent.astype(sent_ref.dtype)
-
-
-def add_kernel(keep_ref, got_ref, out_ref):
-    out_ref[...] = (keep_ref[...] + got_ref[...].astype(jnp.float32)).astype(out_ref.dtype)
+    other_ref[...] = other.astype(other_ref.dtype)
 
 
 def norm_kernel(*refs):
-    partial, (bias_ref, gain_ref, shift_ref), sent = refs[:3], refs[3:6], refs[6:10]
-    tiles = refs[10]
+    partial, (bias_ref, gain_ref, shift_ref), sent = refs[:4], refs[4:7], refs[7:11]
+    tiles = refs[11]
     tm, side, _ = placed_at()
     owners, reach, strip, depth = tiles.shape
     cols = 8
@@ -357,11 +353,10 @@
         pltpu.VMEM((tall // 2 + 2, frames + 2, 2 * cols, 3 * depth), low),
     ]
     cost = {"flops": 2 * count * 27 * depth * half, "moved": 3 << 20}
-    far_keep, far_sent = run(conv_far_kernel, part, scratch, near, far, weight, **cost)
-    far_got = across(far_sent, "tm", 1)
-    keep, sent = run(conv_near_kernel, part, scratch, near, far, weight, **cost)
-    summed = run(add_kernel, part[1], [], far_keep, far_got, moved=1 << 18)
-    partial = [keep, across(summed, "tm", 2), across(sent, "tm", 1)]
+    far_same, far_other = run(conv_far_kernel, [part[1], part[1]], scratch, near, far, weight, **cost)
+    partial = [across(far_same, "tm", 2), across(far_other, "tm", 3)]
+    keep, near_other = run(conv_near_kernel, part, scratch, near, far, weight, **cost)
+    partial = [keep] + partial + [across(near_other, "tm", 1)]
 
     tile = shape((rows + 1, (width + 2) * frames, depth), low)
     tiles = run(

time: 38 us -> 36.4 us (0.958)
  waiting for transfers between devices: 15.1 us -> 12.6 us
  starting transfers between devices: 17.2 us -> 18.1 us
    ppermute x8, waiting for transfers between devices: 14.3 us -> 11.8 us  [across(): return lax.ppermute(value, axes, [(i, i ^ m) for i in range(count)])]
    ppermute x8, starting transfers between devices: 12.7 us -> 13.6 us  [across(): return lax.ppermute(value, axes, [(i, i ^ m) for i in range(count)])]
    pallas_call x10 -> x9, Pallas kernels: 3.8 us -> 3.79 us  [run(): pl.pallas_call(kernel, out_shape=shapes, in_specs=[vmem] * len(operands),...]
  transfers between devices with their start and end apart: 11 -> 11, of which waited for: 8 -> 7; matrix products, arithmetic and copies ran while one was open for 0% -> 0% of each run, Pallas kernels for 4% -> 4%
where the time goes in v11:
time: 36.4 us; the launch traced here: 36.2 us
  starting transfers between devices  18.1 us (50%)
  waiting for transfers between devices  12.6 us (35%)
  Pallas kernels  3.79 us (10%)
  local copies, waits for them, and re-layouts  1.5 us (4%)
    ppermute x8, starting transfers between devices, across(): return lax.ppermute(value, axes, [(i, i ^ m) for i in range(count)])  13.6 us
    ppermute x8, waiting for transfers between devices, across(): return lax.ppermute(value, axes, [(i, i ^ m) for i in range(count)])  11.8 us
    ppermute x2, starting transfers between devices, small_plan(): got.append(lax.ppermute(cells_in, ('tm', 'chan'), pairs))  4.43 us
    pallas_call x9, Pallas kernels, run(): pl.pallas_call(kernel, out_shape=shapes, in_specs=[vmem] * len(operands),...  3.79 us
    unnamed x12, local copies, waits for them, and re-layouts  1.5 us
    ppermute x1, waiting for transfers between devices, small_plan(): far = lax.ppermute(near, 'chan', flip)  0.78 us
  transfers between devices with their start and end apart: 11, of which 7 were waited for; matrix products, arithmetic and copies ran while one was open for 0% of the time, Pallas kernels for 4%

profile of v11, /device:TPU:0, one launch (start us, length us, event | category | flops | bytes accessed | tf_op | source)
XLA Modules:
  0.0 36.2 jit_solution(10897321355166506350)
XLA Ops:
  0.0 3.0 %collective-permute-start = (bf16[64,256]{1,0:T(8,128)(2,1)}, bf16[64,256]{1,0:T(8,128)(2,1)S(1)}, u32[]{:S(2)}, u32[]{:S(2)}) collective-permute-start(bf16[64,256]{1,0:T(8,128)(2,1)} %bitcast.9), channel_id=1, source_target_pairs={{0,4},{1,8},{4,0},{5,12},{8,1},{9,13},{12,5},{13,9},{2,6},{3,10},{... | collective-permute-start | bytes 98312 | tf_op jit(solution)/shard_map/ppermute | solution.py:338
  3.0 1.4 %collective-permute-start.1 = (bf16[64,256]{1,0:T(8,128)(2,1)}, bf16[64,256]{1,0:T(8,128)(2,1)S(1)}, u32[]{:S(2)}, u32[]{:S(2)}) collective-permute-start(bf16[64,256]{1,0:T(8,128)(2,1)} %bitcast.10), channel_id=1, source_target_pairs={{0,0},{1,12},{4,4},{5,8},{8,5},{9,9},{12,1},{13,13},{2,2},{3,14},{... | collective-permute-start | bytes 98312 | tf_op jit(solution)/shard_map/ppermute | solution.py:338
  4.4 0.0 copy-start.1
  4.4 1.5 %copy-done.1 = bf16[3,3,3,128,256]{4,3,2,1,0:T(8,128)(2,1)S(1)} copy-done((bf16[3,3,3,128,256]{4,3,2,1,0:T(8,128)(2,1)S(1)}, bf16[3,3,3,128,256]{4,3,2,1,0:T(8,128)(2,1)}, u32[]{:S(2)}) %copy-start.1) | copy-done | bytes 1769496
  5.9 0.4 %shard_map.73.after_ref.weight_ref = bf16[3,3,3,128,256]{4,3,2,1,0:T(8,128)(2,1)S(1)} custom-call(bf16[3,3,3,128,256]{4,3,2,1,0:T(8,128)(2,1)S(1)} %copy-done.1), custom_call_target="tpu_custom_call" | custom-call | bytes 4194304 | tf_op jit(solution)/shard_map/pallas_call | solution.py:308
  6.3 0.0 collective-permute-done.first_ref
  6.3 0.0 collective-permute-done.1.second_ref
  6.3 1.6 %collective-permute-start.2 = (bf16[2,64,128]{2,1,0:T(8,128)(2,1)S(1)}, bf16[2,64,128]{2,1,0:T(8,128)(2,1)S(1)}, u32[]{:S(2)}, u32[]{:S(2)}) collective-permute-start(bf16[2,64,128]{2,1,0:T(8,128)(2,1)S(1)} %shard_map.74.own_ref), channel_id=1, source_target_pairs={{0,2},{2,0},{1,3},{3,1},{4,6},{6,4},{5,7},{7,5},{8,10},{10,8},{9,1... | collective-permute-start | bytes 98312 | tf_op jit(solution)/shard_map/ppermute | solution.py:341
  7.9 2.4 %collective-permute-done.2.row_ref = bf16[2,64,128]{2,1,0:T(8,128)(2,1)S(1)} collective-permute-done((bf16[2,64,128]{2,1,0:T(8,128)(2,1)S(1)}, bf16[2,64,128]{2,1,0:T(8,128)(2,1)S(1)}, u32[]{:S(2)}, u32[]{:S(2)}) %collective-permute-start.2) | collective-permute-done | bytes 32800 | tf_op jit(solution)/shard_map/ppermute | solution.py:341
  10.3 0.0 copy-start.3
  10.3 0.0 copy-start.4
  10.3 0.0 copy-start.5
  10.3 0.0 copy-start
  10.4 0.0 copy-start.2
  10.4 4.0 %collective-permute-start.3 = (bf16[2,2,64,128]{3,2,1,0:T(8,128)(2,1)S(1)}, bf16[2,2,64,128]{3,2,1,0:T(8,128)(2,1)S(1)}, u32[]{:S(2)}, u32[]{:S(2)}) collective-permute-start(bf16[2,2,64,128]{3,2,1,0:T(8,128)(2,1)S(1)} %shard_map.75.near_ref), channel_id=1, source_target_pairs={{0,1},{1,0},{2,3},{3,2},{4,5},{5,4},{6,7},{7,6},{8,9},{9,8},{10,11... | collective-permute-start | bytes 196616 | tf_op jit(solution)/shard_map/ppermute | solution.py:341
  14.4 0.9 %collective-permute-done.3.far_ref = bf16[2,2,64,128]{3,2,1,0:T(8,128)(2,1)S(1)} collective-permute-done((bf16[2,2,64,128]{3,2,1,0:T(8,128)(2,1)S(1)}, bf16[2,2,64,128]{3,2,1,0:T(8,128)(2,1)S(1)}, u32[]{:S(2)}, u32[]{:S(2)}) %collective-permute-start.3) | collective-permute-done | bytes 65568 | tf_op jit(solution)/shard_map/ppermute | solution.py:341
  15.3 0.7 %shard_map.77 = (bf16[256,128]{1,0:T(8,128)(2,1)S(1)}, bf16[256,128]{1,0:T(8,128)(2,1)S(1)}) custom-call(bf16[2,2,64,128]{3,2,1,0:T(8,128)(2,1)S(1)} %shard_map.75.near_ref, bf16[2,2,64,128]{3,2,1,0:T(8,128)(2,1)S(1)} %collective-permute-done.3.far_ref, bf16[3,3,3,128,256]{4,3,2,1,0:T(8,128)(2,1)S(1)} %shard_map.73.after_ref.weight_ref), custom_call_target="tpu_custom_call" | custom-call | flops 452984832 | bytes 3145728 | tf_op jit(solution)/shard_map/pallas_call | solution.py:308
  16.0 0.8 %collective-permute-start.4 = (bf16[256,128]{1,0:T(8,128)(2,1)S(1)}, bf16[256,128]{1,0:T(8,128)(2,1)S(1)}, u32[]{:S(2)}, u32[]{:S(2)}) collective-permute-start(bf16[256,128]{1,0:T(8,128)(2,1)S(1)} %get-tuple-element.14), channel_id=1, source_target_pairs={{0,8},{4,12},{8,0},{12,4},{1,9},{5,13},{9,1},{13,5},{2,10},{6,14},... | collective-permute-start | bytes 196616 | tf_op jit(solution)/shard_map/ppermute | solution.py:341
  16.7 1.8 %collective-permute-start.5 = (bf16[256,128]{1,0:T(8,128)(2,1)S(1)}, bf16[256,128]{1,0:T(8,128)(2,1)S(1)}, u32[]{:S(2)}, u32[]{:S(2)}) collective-permute-start(bf16[256,128]{1,0:T(8,128)(2,1)S(1)} %get-tuple-element.15), channel_id=1, source_target_pairs={{0,12},{4,8},{8,4},{12,0},{1,13},{5,9},{9,5},{13,1},{2,14},{6,10},... | collective-permute-start | bytes 196616 | tf_op jit(solution)/shard_map/ppermute | solution.py:341
  18.5 0.7 %shard_map.76 = (f32[256,128]{1,0:T(8,128)S(1)}, bf16[256,128]{1,0:T(8,128)(2,1)S(1)}) custom-call(bf16[2,2,64,128]{3,2,1,0:T(8,128)(2,1)S(1)} %shard_map.75.near_ref, bf16[2,2,64,128]{3,2,1,0:T(8,128)(2,1)S(1)} %collective-permute-done.3.far_ref, bf16[3,3,3,128,256]{4,3,2,1,0:T(8,128)(2,1)S(1)} %shard_map.73.after_ref.weight_ref), custom_call_target="tpu_custom_call" | custom-call | flops 452984832 | bytes 3145728 | tf_op jit(solution)/shard_map/pallas_call | solution.py:308
  19.2 1.1 %collective-permute-start.6 = (bf16[256,128]{1,0:T(8,128)(2,1)S(1)}, bf16[256,128]{1,0:T(8,128)(2,1)S(1)}, u32[]{:S(2)}, u32[]{:S(2)}) collective-permute-start(bf16[256,128]{1,0:T(8,128)(2,1)S(1)} %get-tuple-element.16), channel_id=1, source_target_pairs={{0,4},{4,0},{8,12},{12,8},{1,5},{5,1},{9,13},{13,9},{2,6},{6,2},{1... | collective-permute-start | bytes 196616 | tf_op jit(solution)/shard_map/ppermute | solution.py:341
  20.3 3.5 %collective-permute-done.4.refs_1_ = bf16[256,128]{1,0:T(8,128)(2,1)S(1)} collective-permute-done((bf16[256,128]{1,0:T(8,128)(2,1)S(1)}, bf16[256,128]{1,0:T(8,128)(2,1)S(1)}, u32[]{:S(2)}, u32[]{:S(2)}) %collective-permute-start.4) | collective-permute-done | bytes 65568 | tf_op jit(solution)/shard_map/ppermute | solution.py:341
  23.8 0.0 collective-permute-done.5.refs_2_
  23.8 1.3 %collective-permute-done.6.refs_3_ = bf16[256,128]{1,0:T(8,128)(2,1)S(1)} collective-permute-done((bf16[256,128]{1,0:T(8,128)(2,1)S(1)}, bf16[256,128]{1,0:T(8,128)(2,1)S(1)}, u32[]{:S(2)}, u32[]{:S(2)}) %collective-permute-start.6) | collective-permute-done | bytes 65568 | tf_op jit(solution)/shard_map/ppermute | solution.py:341
  25.1 0.0 copy-done.3
  25.1 0.0 copy-done.4
  25.1 0.0 copy-done.5
  25.1 0.3 shard_map.78
  25.4 0.7 %collective-permute-start.7 = (bf16[3,32,128]{2,1,0:T(8,128)(2,1)S(1)}, bf16[3,32,128]{2,1,0:T(8,128)(2,1)S(1)}, u32[]{:S(2)}, u32[]{:S(2)}) collective-permute-start(bf16[3,32,128]{2,1,0:T(8,128)(2,1)S(1)} %get-tuple-element.18), channel_id=1, source_target_pairs={{0,4},{4,0},{8,12},{12,8},{1,5},{5,1},{9,13},{13,9},{2,6},{6,2},{1... | collective-permute-start | bytes 73736 | tf_op jit(solution)/shard_map/ppermute | solution.py:341
  26.1 1.9 %collective-permute-start.8 = (bf16[3,32,128]{2,1,0:T(8,128)(2,1)S(1)}, bf16[3,32,128]{2,1,0:T(8,128)(2,1)S(1)}, u32[]{:S(2)}, u32[]{:S(2)}) collective-permute-start(bf16[3,32,128]{2,1,0:T(8,128)(2,1)S(1)} %get-tuple-element.19), channel_id=1, source_target_pairs={{0,8},{4,12},{8,0},{12,4},{1,9},{5,13},{9,1},{13,5},{2,10},{6,14},... | collective-permute-start | bytes 73736 | tf_op jit(solution)/shard_map/ppermute | solution.py:341
  28.0 1.9 %collective-permute-start.9 = (bf16[3,32,128]{2,1,0:T(8,128)(2,1)S(1)}, bf16[3,32,128]{2,1,0:T(8,128)(2,1)S(1)}, u32[]{:S(2)}, u32[]{:S(2)}) collective-permute-start(bf16[3,32,128]{2,1,0:T(8,128)(2,1)S(1)} %get-tuple-element.20), channel_id=1, source_target_pairs={{0,12},{4,8},{8,4},{12,0},{1,13},{5,9},{9,5},{13,1},{2,14},{6,10},... | collective-permute-start | bytes 73736 | tf_op jit(solution)/shard_map/ppermute | solution.py:341
  29.9 0.0 collective-permute-done.7.refs_1_
  29.9 1.0 %collective-permute-done.8.refs_2_ = bf16[3,32,128]{2,1,0:T(8,128)(2,1)S(1)} collective-permute-done((bf16[3,32,128]{2,1,0:T(8,128)(2,1)S(1)}, bf16[3,32,128]{2,1,0:T(8,128)(2,1)S(1)}, u32[]{:S(2)}, u32[]{:S(2)}) %collective-permute-start.8) | collective-permute-done | bytes 24608 | tf_op jit(solution)/shard_map/ppermute | solution.py:341
  30.9 2.7 %collective-permute-done.9.refs_3_ = bf16[3,32,128]{2,1,0:T(8,128)(2,1)S(1)} collective-permute-done((bf16[3,32,128]{2,1,0:T(8,128)(2,1)S(1)}, bf16[3,32,128]{2,1,0:T(8,128)(2,1)S(1)}, u32[]{:S(2)}, u32[]{:S(2)}) %collective-permute-start.9) | collective-permute-done | bytes 24608 | tf_op jit(solution)/shard_map/ppermute | solution.py:341
  33.6 0.1 collective-permute-start.10
  33.7 0.0 copy-done
  33.7 0.0 copy-done.2
  33.7 0.5 %shard_map.80.total_ref = f32[256,256]{1,0:T(8,128)S(1)} custom-call(bf16[3,4,16,256]{3,2,1,0:T(8,128)(2,1)S(1)} %shard_map.79.cells_ref, bf16[3,3,512,256]{3,2,1,0:T(8,128)(2,1)S(1)} %copy-done, f32[1,256]{1,0:T(1,128)S(1)} %bitcast.5), custom_call_target="tpu_custom_call" | custom-call | flops 301989888 | bytes 2097152 | tf_op jit(solution)/shard_map/pallas_call | solution.py:308
  34.2 0.8 %collective-permute-done.10.cells_ref = bf16[3,4,16,256]{3,2,1,0:T(8,128)(2,1)S(1)} collective-permute-done((bf16[3,4,16,256]{3,2,1,0:T(8,128)(2,1)S(1)}, bf16[3,4,16,256]{3,2,1,0:T(8,128)(2,1)S(1)}, u32[]{:S(2)}, u32[]{:S(2)}) %collective-permute-start.10) | collective-permute-done | bytes 98336 | tf_op jit(solution)/shard_map/ppermute | solution.py:379
  35.0 1.2 %shard_map.81 = bf16[2,8,4,4,256]{4,3,2,1,0:T(4,128)(2,1)} custom-call(bf16[3,4,16,256]{3,2,1,0:T(8,128)(2,1)S(1)} %collective-permute-done.10.cells_ref, bf16[3,3,512,256]{3,2,1,0:T(8,128)(2,1)S(1)} %copy-done, f32[256,256]{1,0:T(8,128)S(1)} %shard_map.80.total_ref), custom_call_target="tpu_custom_call" | custom-call | flops 301989888 | bytes 2097152 | tf_op jit(solution)/shard_map/pallas_call | solution.py:308
  (3 shorter events, 0.1 us)
Async XLA Ops:
  0.0 6.3 %collective-permute-start = (bf16[64,256]{1,0:T(8,128)(2,1)}, bf16[64,256]{1,0:T(8,128)(2,1)S(1)}, u32[]{:S(2)}, u32[]{:S(2)}) collective-permute-start(bf16[64,256]{1,0:T(8,128)(2,1)} %bitcast.9), channel_id=1, source_target_pairs={{0,4},{1,8},{4,0},{5,12},{8,1},{9,13},{12,5},{13,9},{2,6},{3,10},{... | collective-permute-start | bytes 98312 | tf_op jit(solution)/shard_map/ppermute | solution.py:338
  3.0 3.3 %collective-permute-start.1 = (bf16[64,256]{1,0:T(8,128)(2,1)}, bf16[64,256]{1,0:T(8,128)(2,1)S(1)}, u32[]{:S(2)}, u32[]{:S(2)}) collective-permute-start(bf16[64,256]{1,0:T(8,128)(2,1)} %bitcast.10), channel_id=1, source_target_pairs={{0,0},{1,12},{4,4},{5,8},{8,5},{9,9},{12,1},{13,13},{2,2},{3,14},{... | collective-permute-start | bytes 98312 | tf_op jit(solution)/shard_map/ppermute | solution.py:338
  4.4 1.5 %copy-start.1 = (bf16[3,3,3,128,256]{4,3,2,1,0:T(8,128)(2,1)S(1)}, bf16[3,3,3,128,256]{4,3,2,1,0:T(8,128)(2,1)}, u32[]{:S(2)}) copy-start(bf16[3,3,3,128,256]{4,3,2,1,0:T(8,128)(2,1)} %weight_ref.3) | copy-start | bytes 5308420
  6.3 4.0 %collective-permute-start.2 = (bf16[2,64,128]{2,1,0:T(8,128)(2,1)S(1)}, bf16[2,64,128]{2,1,0:T(8,128)(2,1)S(1)}, u32[]{:S(2)}, u32[]{:S(2)}) collective-permute-start(bf16[2,64,128]{2,1,0:T(8,128)(2,1)S(1)} %shard_map.74.own_ref), channel_id=1, source_target_pairs={{0,2},{2,0},{1,3},{3,1},{4,6},{6,4},{5,7},{7,5},{8,10},{10,8},{9,1... | collective-permute-start | bytes 98312 | tf_op jit(solution)/shard_map/ppermute | solution.py:341
  10.3 14.7 %copy-start.3 = (f32[256]{0:T(256)S(1)}, f32[256]{0:T(256)}, u32[]{:S(2)}) copy-start(f32[256]{0:T(256)} %param.9) | copy-start | bytes 3076
  10.3 14.7 %copy-start.4 = (f32[256]{0:T(256)S(1)}, f32[256]{0:T(256)}, u32[]{:S(2)}) copy-start(f32[256]{0:T(256)} %param.10) | copy-start | bytes 3076
  10.3 14.7 %copy-start.5 = (f32[256]{0:T(256)S(1)}, f32[256]{0:T(256)}, u32[]{:S(2)}) copy-start(f32[256]{0:T(256)} %param.11) | copy-start | bytes 3076
  10.3 23.4 %copy-start = (bf16[3,3,512,256]{3,2,1,0:T(8,128)(2,1)S(1)}, bf16[3,3,512,256]{3,2,1,0:T(8,128)(2,1)}, u32[]{:S(2)}) copy-start(bf16[3,3,512,256]{3,2,1,0:T(8,128)(2,1)} %weight_ref.5) | copy-start | bytes 7077892
  10.4 23.4 %copy-start.2 = (f32[256]{0:T(256)S(1)}, f32[256]{0:T(256)}, u32[]{:S(2)}) copy-start(f32[256]{0:T(256)} %param.13) | copy-start | bytes 3076
  10.4 4.9 %collective-permute-start.3 = (bf16[2,2,64,128]{3,2,1,0:T(8,128)(2,1)S(1)}, bf16[2,2,64,128]{3,2,1,0:T(8,128)(2,1)S(1)}, u32[]{:S(2)}, u32[]{:S(2)}) collective-permute-start(bf16[2,2,64,128]{3,2,1,0:T(8,128)(2,1)S(1)} %shard_map.75.near_ref), channel_id=1, source_target_pairs={{0,1},{1,0},{2,3},{3,2},{4,5},{5,4},{6,7},{7,6},{8,9},{9,8},{10,11... | collective-permute-start | bytes 196616 | tf_op jit(solution)/shard_map/ppermute | solution.py:341
  16.0 7.8 %collective-permute-start.4 = (bf16[256,128]{1,0:T(8,128)(2,1)S(1)}, bf16[256,128]{1,0:T(8,128)(2,1)S(1)}, u32[]{:S(2)}, u32[]{:S(2)}) collective-permute-start(bf16[256,128]{1,0:T(8,128)(2,1)S(1)} %get-tuple-element.14), channel_id=1, source_target_pairs={{0,8},{4,12},{8,0},{12,4},{1,9},{5,13},{9,1},{13,5},{2,10},{6,14},... | collective-permute-start | bytes 196616 | tf_op jit(solution)/shard_map/ppermute | solution.py:341
  16.7 7.0 %collective-permute-start.5 = (bf16[256,128]{1,0:T(8,128)(2,1)S(1)}, bf16[256,128]{1,0:T(8,128)(2,1)S(1)}, u32[]{:S(2)}, u32[]{:S(2)}) collective-permute-start(bf16[256,128]{1,0:T(8,128)(2,1)S(1)} %get-tuple-element.15), channel_id=1, source_target_pairs={{0,12},{4,8},{8,4},{12,0},{1,13},{5,9},{9,5},{13,1},{2,14},{6,10},... | collective-permute-start | bytes 196616 | tf_op jit(solution)/shard_map/ppermute | solution.py:341
  19.2 5.9 %collective-permute-start.6 = (bf16[256,128]{1,0:T(8,128)(2,1)S(1)}, bf16[256,128]{1,0:T(8,128)(2,1)S(1)}, u32[]{:S(2)}, u32[]{:S(2)}) collective-permute-start(bf16[256,128]{1,0:T(8,128)(2,1)S(1)} %get-tuple-element.16), channel_id=1, source_target_pairs={{0,4},{4,0},{8,12},{12,8},{1,5},{5,1},{9,13},{13,9},{2,6},{6,2},{1... | collective-permute-start | bytes 196616 | tf_op jit(solution)/shard_map/ppermute | solution.py:341
  25.4 4.5 %collective-permute-start.7 = (bf16[3,32,128]{2,1,0:T(8,128)(2,1)S(1)}, bf16[3,32,128]{2,1,0:T(8,128)(2,1)S(1)}, u32[]{:S(2)}, u32[]{:S(2)}) collective-permute-start(bf16[3,32,128]{2,1,0:T(8,128)(2,1)S(1)} %get-tuple-element.18), channel_id=1, source_target_pairs={{0,4},{4,0},{8,12},{12,8},{1,5},{5,1},{9,13},{13,9},{2,6},{6,2},{1... | collective-permute-start | bytes 73736 | tf_op jit(solution)/shard_map/ppermute | solution.py:341
  26.1 4.8 %collective-permute-start.8 = (bf16[3,32,128]{2,1,0:T(8,128)(2,1)S(1)}, bf16[3,32,128]{2,1,0:T(8,128)(2,1)S(1)}, u32[]{:S(2)}, u32[]{:S(2)}) collective-permute-start(bf16[3,32,128]{2,1,0:T(8,128)(2,1)S(1)} %get-tuple-element.19), channel_id=1, source_target_pairs={{0,8},{4,12},{8,0},{12,4},{1,9},{5,13},{9,1},{13,5},{2,10},{6,14},... | collective-permute-start | bytes 73736 | tf_op jit(solution)/shard_map/ppermute | solution.py:341
  28.0 5.6 %collective-permute-start.9 = (bf16[3,32,128]{2,1,0:T(8,128)(2,1)S(1)}, bf16[3,32,128]{2,1,0:T(8,128)(2,1)S(1)}, u32[]{:S(2)}, u32[]{:S(2)}) collective-permute-start(bf16[3,32,128]{2,1,0:T(8,128)(2,1)S(1)} %get-tuple-element.20), channel_id=1, source_target_pairs={{0,12},{4,8},{8,4},{12,0},{1,13},{5,9},{9,5},{13,1},{2,14},{6,10},... | collective-permute-start | bytes 73736 | tf_op jit(solution)/shard_map/ppermute | solution.py:341
  33.6 1.4 %collective-permute-start.10 = (bf16[3,4,16,256]{3,2,1,0:T(8,128)(2,1)S(1)}, bf16[3,4,16,256]{3,2,1,0:T(8,128)(2,1)S(1)}, u32[]{:S(2)}, u32[]{:S(2)}) collective-permute-start(bf16[3,4,16,256]{3,2,1,0:T(8,128)(2,1)S(1)} %shard_map.79.cells_ref), channel_id=1, source_target_pairs={{0,1},{1,0},{2,3},{3,2},{4,5},{5,4},{6,7},{7,6},{8,9},{9,8},{10,11... | collective-permute-start | bytes 294920 | tf_op jit(solution)/shard_map/ppermute | solution.py:379

commit v12 on v5

--- a/solution.py
+++ b/solution.py
@@ -241,8 +241,8 @@
 def cells_kernel(*refs):
     got, cells_ref, tiles = refs[:4], refs[4], refs[5]
     tm, _, _ = placed_at()
-    for m in range(len(got)):
-        tiles[tm ^ m] = got[m][...].astype(jnp.float32)
+    for ref, m in zip(got, (0, 3, 2, 1)):
+        tiles[tm ^ m] = ref[...].astype(jnp.float32)
     reach, wide, tall, half = cells_ref.shape
     depth = tiles.shape[3]
     los = half // depth
@@ -367,7 +367,7 @@
         moved=1 << 19,
     )
     tiles = [tiles[0]] + [
-        lax.ppermute(tiles[m], "tm", [(i, i ^ m) for i in range(spans)]) for m in range(1, spans)
+        lax.ppermute(tiles[m], "tm", [(i, i ^ m) for i in range(spans)]) for m in range(spans - 1, 0, -1)
     ]
 
     near = run(

time: 35.5 us -> 36.1 us (1.017)
  waiting for transfers between devices: 10.6 us -> 12.2 us
  starting transfers between devices: 19.2 us -> 18.3 us
    ppermute x3, waiting for transfers between devices: 1.93 us -> 3.5 us  [small_plan(): lax.ppermute(tiles[m], 'tm', [(i, i ^ m) for i in range(spans)])]
    ppermute x3, starting transfers between devices: 4.45 us -> 3.55 us  [small_plan(): lax.ppermute(tiles[m], 'tm', [(i, i ^ m) for i in range(spans)])]
  transfers between devices with their start and end apart: 12 -> 12, of which waited for: 7 -> 8; matrix products, arithmetic and copies ran while one was open for 0% -> 0% of each run, Pallas kernels for 4% -> 4%
where the time goes in v12:
time: 36.1 us; the launch traced here: 35.9 us
  starting transfers between devices  18.3 us (51%)
  waiting for transfers between devices  12.2 us (34%)
  Pallas kernels  3.78 us (10%)
  local copies, waits for them, and re-layouts  1.51 us (4%)
    ppermute x3, starting transfers between devices, small_plan(): lax.ppermute(own, ('space', 'chan'), [(i, i ^ m) for i in range(spaces *...  6.63 us
    ppermute x2, starting transfers between devices, small_plan(): got.append(lax.ppermute(cells_in, ('tm', 'chan'), pairs))  4.43 us
    pallas_call x8, Pallas kernels, run(): pl.pallas_call(kernel, out_shape=shapes, in_specs=[vmem] * len(operands),...  3.78 us
    ppermute x3, waiting for transfers between devices, small_plan(): lax.ppermute(own, ('space', 'chan'), [(i, i ^ m) for i in range(spaces *...  3.66 us
    ppermute x3, starting transfers between devices, small_plan(): lax.ppermute(tiles[m], 'tm', [(i, i ^ m) for i in range(spans)])  3.55 us
    ppermute x3, waiting for transfers between devices, small_plan(): lax.ppermute(tiles[m], 'tm', [(i, i ^ m) for i in range(spans)])  3.5 us
    ppermute x2, waiting for transfers between devices, small_plan(): lax.ppermute(value, 'tm', [(i, i ^ m) for i in range(spans)])  3.08 us
    ppermute x2, starting transfers between devices, small_plan(): lax.ppermute(value, 'tm', [(i, i ^ m) for i in range(spans)])  2.2 us
  transfers between devices with their start and end apart: 12, of which 8 were waited for; matrix products, arithmetic and copies ran while one was open for 0% of the time, Pallas kernels for 4%

profile of v12, /device:TPU:0, one launch (start us, length us, event | category | flops | bytes accessed | tf_op | source)
XLA Modules:
  0.0 35.9 jit_solution(7158435840343551346)
XLA Ops:
  0.0 3.0 %collective-permute-start = (bf16[64,256]{1,0:T(8,128)(2,1)}, bf16[64,256]{1,0:T(8,128)(2,1)S(1)}, u32[]{:S(2)}, u32[]{:S(2)}) collective-permute-start(bf16[64,256]{1,0:T(8,128)(2,1)} %bitcast.9), channel_id=1, source_target_pairs={{0,4},{1,8},{4,0},{5,12},{8,1},{9,13},{12,5},{13,9},{2,6},{3,10},{... | collective-permute-start | bytes 98312 | tf_op jit(solution)/shard_map/ppermute | solution.py:335
  3.0 1.4 %collective-permute-start.1 = (bf16[64,256]{1,0:T(8,128)(2,1)}, bf16[64,256]{1,0:T(8,128)(2,1)S(1)}, u32[]{:S(2)}, u32[]{:S(2)}) collective-permute-start(bf16[64,256]{1,0:T(8,128)(2,1)} %bitcast.10), channel_id=1, source_target_pairs={{0,0},{1,12},{4,4},{5,8},{8,5},{9,9},{12,1},{13,13},{2,2},{3,14},{... | collective-permute-start | bytes 98312 | tf_op jit(solution)/shard_map/ppermute | solution.py:335
  4.4 0.0 copy-start.1
  4.4 1.5 %copy-done.1 = bf16[3,3,3,128,256]{4,3,2,1,0:T(8,128)(2,1)S(1)} copy-done((bf16[3,3,3,128,256]{4,3,2,1,0:T(8,128)(2,1)S(1)}, bf16[3,3,3,128,256]{4,3,2,1,0:T(8,128)(2,1)}, u32[]{:S(2)}) %copy-start.1) | copy-done | bytes 1769496
  5.9 0.4 %shard_map.73.after_ref.weight_ref = bf16[3,3,3,128,256]{4,3,2,1,0:T(8,128)(2,1)S(1)} custom-call(bf16[3,3,3,128,256]{4,3,2,1,0:T(8,128)(2,1)S(1)} %copy-done.1), custom_call_target="tpu_custom_call" | custom-call | bytes 4194304 | tf_op jit(solution)/shard_map/pallas_call | solution.py:305
  6.3 0.0 collective-permute-done.first_ref
  6.3 0.0 collective-permute-done.1.second_ref
  6.3 0.0 copy-start.3
  6.3 0.0 copy-start.4
  6.4 0.0 copy-start.5
  6.4 0.0 copy-start
  6.4 0.0 copy-start.2
  6.4 5.1 %collective-permute-start.2 = (bf16[2,64,128]{2,1,0:T(8,128)(2,1)S(1)}, bf16[2,64,128]{2,1,0:T(8,128)(2,1)S(1)}, u32[]{:S(2)}, u32[]{:S(2)}) collective-permute-start(bf16[2,64,128]{2,1,0:T(8,128)(2,1)S(1)} %shard_map.74.own_ref), channel_id=1, source_target_pairs={{0,1},{1,0},{2,3},{3,2},{4,5},{5,4},{6,7},{7,6},{8,9},{9,8},{10,11... | collective-permute-start | bytes 98312 | tf_op jit(solution)/shard_map/ppermute | solution.py:339
  11.5 1.5 %collective-permute-start.3 = (bf16[2,64,128]{2,1,0:T(8,128)(2,1)S(1)}, bf16[2,64,128]{2,1,0:T(8,128)(2,1)S(1)}, u32[]{:S(2)}, u32[]{:S(2)}) collective-permute-start(bf16[2,64,128]{2,1,0:T(8,128)(2,1)S(1)} %shard_map.74.own_ref), channel_id=1, source_target_pairs={{0,2},{1,3},{2,0},{3,1},{4,6},{5,7},{6,4},{7,5},{8,10},{9,11},{10,... | collective-permute-start | bytes 98312 | tf_op jit(solution)/shard_map/ppermute | solution.py:339
  13.0 0.0 collective-permute-start.4
  13.0 0.0 collective-permute-done.2.core_ref
  13.0 2.4 %collective-permute-done.3.row_ref = bf16[2,64,128]{2,1,0:T(8,128)(2,1)S(1)} collective-permute-done((bf16[2,64,128]{2,1,0:T(8,128)(2,1)S(1)}, bf16[2,64,128]{2,1,0:T(8,128)(2,1)S(1)}, u32[]{:S(2)}, u32[]{:S(2)}) %collective-permute-start.3) | collective-permute-done | bytes 32800 | tf_op jit(solution)/shard_map/ppermute | solution.py:339
  15.4 1.2 %collective-permute-done.4.both_ref = bf16[2,64,128]{2,1,0:T(8,128)(2,1)S(1)} collective-permute-done((bf16[2,64,128]{2,1,0:T(8,128)(2,1)S(1)}, bf16[2,64,128]{2,1,0:T(8,128)(2,1)S(1)}, u32[]{:S(2)}, u32[]{:S(2)}) %collective-permute-start.4) | collective-permute-done | bytes 32800 | tf_op jit(solution)/shard_map/ppermute | solution.py:339
  16.7 0.7 %shard_map.76 = (bf16[256,128]{1,0:T(8,128)(2,1)S(1)}, bf16[256,128]{1,0:T(8,128)(2,1)S(1)}) custom-call(bf16[2,64,128]{2,1,0:T(8,128)(2,1)S(1)} %shard_map.74.own_ref, bf16[2,64,128]{2,1,0:T(8,128)(2,1)S(1)} %collective-permute-done.2.core_ref, bf16[2,64,128]{2,1,0:T(8,128)(2,1)S(1)} %collective-permute-done.3.row_ref, ...), custom_call_target="tpu_custom_call" | custom-call | flops 452984832 | bytes 3145728 | tf_op jit(solution)/shard_map/pallas_call | solution.py:305
  17.4 0.1 collective-permute-start.5
  17.5 2.1 %collective-permute-start.6 = (bf16[256,128]{1,0:T(8,128)(2,1)S(1)}, bf16[256,128]{1,0:T(8,128)(2,1)S(1)}, u32[]{:S(2)}, u32[]{:S(2)}) collective-permute-start(bf16[256,128]{1,0:T(8,128)(2,1)S(1)} %get-tuple-element.15), channel_id=1, source_target_pairs={{0,12},{4,8},{8,4},{12,0},{1,13},{5,9},{9,5},{13,1},{2,14},{6,10},... | collective-permute-start | bytes 196616 | tf_op jit(solution)/shard_map/ppermute | solution.py:353
  19.6 0.7 %shard_map.75 = (f32[256,128]{1,0:T(8,128)S(1)}, bf16[256,128]{1,0:T(8,128)(2,1)S(1)}) custom-call(bf16[2,64,128]{2,1,0:T(8,128)(2,1)S(1)} %shard_map.74.own_ref, bf16[2,64,128]{2,1,0:T(8,128)(2,1)S(1)} %collective-permute-done.2.core_ref, bf16[2,64,128]{2,1,0:T(8,128)(2,1)S(1)} %collective-permute-done.3.row_ref, ...), custom_call_target="tpu_custom_call" | custom-call | flops 452984832 | bytes 3145728 | tf_op jit(solution)/shard_map/pallas_call | solution.py:305
  20.3 1.4 %collective-permute-start.7 = (bf16[256,128]{1,0:T(8,128)(2,1)S(1)}, bf16[256,128]{1,0:T(8,128)(2,1)S(1)}, u32[]{:S(2)}, u32[]{:S(2)}) collective-permute-start(bf16[256,128]{1,0:T(8,128)(2,1)S(1)} %get-tuple-element.16), channel_id=1, source_target_pairs={{0,4},{4,0},{8,12},{12,8},{1,5},{5,1},{9,13},{13,9},{2,6},{6,2},{1... | collective-permute-start | bytes 196616 | tf_op jit(solution)/shard_map/ppermute | solution.py:358
  21.7 3.1 %collective-permute-done.5.refs_1_ = bf16[256,128]{1,0:T(8,128)(2,1)S(1)} collective-permute-done((bf16[256,128]{1,0:T(8,128)(2,1)S(1)}, bf16[256,128]{1,0:T(8,128)(2,1)S(1)}, u32[]{:S(2)}, u32[]{:S(2)}) %collective-permute-start.5) | collective-permute-done | bytes 65568 | tf_op jit(solution)/shard_map/ppermute | solution.py:353
  24.8 0.0 collective-permute-done.6.refs_2_
  24.8 1.2 %collective-permute-done.7.refs_3_ = bf16[256,128]{1,0:T(8,128)(2,1)S(1)} collective-permute-done((bf16[256,128]{1,0:T(8,128)(2,1)S(1)}, bf16[256,128]{1,0:T(8,128)(2,1)S(1)}, u32[]{:S(2)}, u32[]{:S(2)}) %collective-permute-start.7) | collective-permute-done | bytes 65568 | tf_op jit(solution)/shard_map/ppermute | solution.py:358
  25.9 0.0 copy-done.3
  25.9 0.0 copy-done.4
  25.9 0.0 copy-done.5
  26.0 0.3 shard_map.77
  26.3 0.7 %collective-permute-start.10 = (bf16[3,32,128]{2,1,0:T(8,128)(2,1)S(1)}, bf16[3,32,128]{2,1,0:T(8,128)(2,1)S(1)}, u32[]{:S(2)}, u32[]{:S(2)}) collective-permute-start(bf16[3,32,128]{2,1,0:T(8,128)(2,1)S(1)} %get-tuple-element.20), channel_id=1, source_target_pairs={{0,4},{4,0},{8,12},{12,8},{1,5},{5,1},{9,13},{13,9},{2,6},{6,2},{1... | collective-permute-start | bytes 73736 | tf_op jit(solution)/shard_map/ppermute | solution.py:370
  27.0 1.4 %collective-permute-start.8 = (bf16[3,32,128]{2,1,0:T(8,128)(2,1)S(1)}, bf16[3,32,128]{2,1,0:T(8,128)(2,1)S(1)}, u32[]{:S(2)}, u32[]{:S(2)}) collective-permute-start(bf16[3,32,128]{2,1,0:T(8,128)(2,1)S(1)} %get-tuple-element.18), channel_id=1, source_target_pairs={{0,12},{4,8},{8,4},{12,0},{1,13},{5,9},{9,5},{13,1},{2,14},{6,10},... | collective-permute-start | bytes 73736 | tf_op jit(solution)/shard_map/ppermute | solution.py:370
  28.4 1.5 %collective-permute-start.9 = (bf16[3,32,128]{2,1,0:T(8,128)(2,1)S(1)}, bf16[3,32,128]{2,1,0:T(8,128)(2,1)S(1)}, u32[]{:S(2)}, u32[]{:S(2)}) collective-permute-start(bf16[3,32,128]{2,1,0:T(8,128)(2,1)S(1)} %get-tuple-element.19), channel_id=1, source_target_pairs={{0,8},{4,12},{8,0},{12,4},{1,9},{5,13},{9,1},{13,5},{2,10},{6,14},... | collective-permute-start | bytes 73736 | tf_op jit(solution)/shard_map/ppermute | solution.py:370
  29.9 0.3 collective-permute-done.10.refs_3_
  30.2 2.4 %collective-permute-done.8.refs_1_ = bf16[3,32,128]{2,1,0:T(8,128)(2,1)S(1)} collective-permute-done((bf16[3,32,128]{2,1,0:T(8,128)(2,1)S(1)}, bf16[3,32,128]{2,1,0:T(8,128)(2,1)S(1)}, u32[]{:S(2)}, u32[]{:S(2)}) %collective-permute-start.8) | collective-permute-done | bytes 24608 | tf_op jit(solution)/shard_map/ppermute | solution.py:370
  32.6 0.7 %collective-permute-done.9.refs_2_ = bf16[3,32,128]{2,1,0:T(8,128)(2,1)S(1)} collective-permute-done((bf16[3,32,128]{2,1,0:T(8,128)(2,1)S(1)}, bf16[3,32,128]{2,1,0:T(8,128)(2,1)S(1)}, u32[]{:S(2)}, u32[]{:S(2)}) %collective-permute-start.9) | collective-permute-done | bytes 24608 | tf_op jit(solution)/shard_map/ppermute | solution.py:370
  33.4 0.1 collective-permute-start.11
  33.5 0.0 copy-done
  33.5 0.0 copy-done.2
  33.5 0.5 %shard_map.79.total_ref = f32[256,256]{1,0:T(8,128)S(1)} custom-call(bf16[3,4,16,256]{3,2,1,0:T(8,128)(2,1)S(1)} %shard_map.78.cells_ref, bf16[3,3,512,256]{3,2,1,0:T(8,128)(2,1)S(1)} %copy-done, f32[1,256]{1,0:T(1,128)S(1)} %bitcast.5), custom_call_target="tpu_custom_call" | custom-call | flops 301989888 | bytes 2097152 | tf_op jit(solution)/shard_map/pallas_call | solution.py:305
  34.0 0.8 %collective-permute-done.11.cells_ref = bf16[3,4,16,256]{3,2,1,0:T(8,128)(2,1)S(1)} collective-permute-done((bf16[3,4,16,256]{3,2,1,0:T(8,128)(2,1)S(1)}, bf16[3,4,16,256]{3,2,1,0:T(8,128)(2,1)S(1)}, u32[]{:S(2)}, u32[]{:S(2)}) %collective-permute-start.11) | collective-permute-done | bytes 98336 | tf_op jit(solution)/shard_map/ppermute | solution.py:380
  34.8 1.2 %shard_map.80 = bf16[2,8,4,4,256]{4,3,2,1,0:T(4,128)(2,1)} custom-call(bf16[3,4,16,256]{3,2,1,0:T(8,128)(2,1)S(1)} %collective-permute-done.11.cells_ref, bf16[3,3,512,256]{3,2,1,0:T(8,128)(2,1)S(1)} %copy-done, f32[256,256]{1,0:T(8,128)S(1)} %shard_map.79.total_ref), custom_call_target="tpu_custom_call" | custom-call | flops 301989888 | bytes 2097152 | tf_op jit(solution)/shard_map/pallas_call | solution.py:305
  (2 shorter events, 0.1 us)
Async XLA Ops:
  0.0 6.3 %collective-permute-start = (bf16[64,256]{1,0:T(8,128)(2,1)}, bf16[64,256]{1,0:T(8,128)(2,1)S(1)}, u32[]{:S(2)}, u32[]{:S(2)}) collective-permute-start(bf16[64,256]{1,0:T(8,128)(2,1)} %bitcast.9), channel_id=1, source_target_pairs={{0,4},{1,8},{4,0},{5,12},{8,1},{9,13},{12,5},{13,9},{2,6},{3,10},{... | collective-permute-start | bytes 98312 | tf_op jit(solution)/shard_map/ppermute | solution.py:335
  3.0 3.3 %collective-permute-start.1 = (bf16[64,256]{1,0:T(8,128)(2,1)}, bf16[64,256]{1,0:T(8,128)(2,1)S(1)}, u32[]{:S(2)}, u32[]{:S(2)}) collective-permute-start(bf16[64,256]{1,0:T(8,128)(2,1)} %bitcast.10), channel_id=1, source_target_pairs={{0,0},{1,12},{4,4},{5,8},{8,5},{9,9},{12,1},{13,13},{2,2},{3,14},{... | collective-permute-start | bytes 98312 | tf_op jit(solution)/shard_map/ppermute | solution.py:335
  4.4 1.5 %copy-start.1 = (bf16[3,3,3,128,256]{4,3,2,1,0:T(8,128)(2,1)S(1)}, bf16[3,3,3,128,256]{4,3,2,1,0:T(8,128)(2,1)}, u32[]{:S(2)}) copy-start(bf16[3,3,3,128,256]{4,3,2,1,0:T(8,128)(2,1)} %weight_ref.3) | copy-start | bytes 5308420
  6.3 19.6 %copy-start.3 = (f32[256]{0:T(256)S(1)}, f32[256]{0:T(256)}, u32[]{:S(2)}) copy-start(f32[256]{0:T(256)} %param.9) | copy-start | bytes 3076
  6.3 19.6 %copy-start.4 = (f32[256]{0:T(256)S(1)}, f32[256]{0:T(256)}, u32[]{:S(2)}) copy-start(f32[256]{0:T(256)} %param.10) | copy-start | bytes 3076
  6.4 19.6 %copy-start.5 = (f32[256]{0:T(256)S(1)}, f32[256]{0:T(256)}, u32[]{:S(2)}) copy-start(f32[256]{0:T(256)} %param.11) | copy-start | bytes 3076
  6.4 27.1 %copy-start = (bf16[3,3,512,256]{3,2,1,0:T(8,128)(2,1)S(1)}, bf16[3,3,512,256]{3,2,1,0:T(8,128)(2,1)}, u32[]{:S(2)}) copy-start(bf16[3,3,512,256]{3,2,1,0:T(8,128)(2,1)} %weight_ref.5) | copy-start | bytes 7077892
  6.4 27.1 %copy-start.2 = (f32[256]{0:T(256)S(1)}, f32[256]{0:T(256)}, u32[]{:S(2)}) copy-start(f32[256]{0:T(256)} %param.13) | copy-start | bytes 3076
  6.4 6.6 %collective-permute-start.2 = (bf16[2,64,128]{2,1,0:T(8,128)(2,1)S(1)}, bf16[2,64,128]{2,1,0:T(8,128)(2,1)S(1)}, u32[]{:S(2)}, u32[]{:S(2)}) collective-permute-start(bf16[2,64,128]{2,1,0:T(8,128)(2,1)S(1)} %shard_map.74.own_ref), channel_id=1, source_target_pairs={{0,1},{1,0},{2,3},{3,2},{4,5},{5,4},{6,7},{7,6},{8,9},{9,8},{10,11... | collective-permute-start | bytes 98312 | tf_op jit(solution)/shard_map/ppermute | solution.py:339
  11.5 3.9 %collective-permute-start.3 = (bf16[2,64,128]{2,1,0:T(8,128)(2,1)S(1)}, bf16[2,64,128]{2,1,0:T(8,128)(2,1)S(1)}, u32[]{:S(2)}, u32[]{:S(2)}) collective-permute-start(bf16[2,64,128]{2,1,0:T(8,128)(2,1)S(1)} %shard_map.74.own_ref), channel_id=1, source_target_pairs={{0,2},{1,3},{2,0},{3,1},{4,6},{5,7},{6,4},{7,5},{8,10},{9,11},{10,... | collective-permute-start | bytes 98312 | tf_op jit(solution)/shard_map/ppermute | solution.py:339
  13.0 3.7 %collective-permute-start.4 = (bf16[2,64,128]{2,1,0:T(8,128)(2,1)S(1)}, bf16[2,64,128]{2,1,0:T(8,128)(2,1)S(1)}, u32[]{:S(2)}, u32[]{:S(2)}) collective-permute-start(bf16[2,64,128]{2,1,0:T(8,128)(2,1)S(1)} %shard_map.74.own_ref), channel_id=1, source_target_pairs={{0,3},{1,2},{2,1},{3,0},{4,7},{5,6},{6,5},{7,4},{8,11},{9,10},{10,... | collective-permute-start | bytes 98312 | tf_op jit(solution)/shard_map/ppermute | solution.py:339
  17.4 7.4 %collective-permute-start.5 = (bf16[256,128]{1,0:T(8,128)(2,1)S(1)}, bf16[256,128]{1,0:T(8,128)(2,1)S(1)}, u32[]{:S(2)}, u32[]{:S(2)}) collective-permute-start(bf16[256,128]{1,0:T(8,128)(2,1)S(1)} %get-tuple-element.14), channel_id=1, source_target_pairs={{0,8},{4,12},{8,0},{12,4},{1,9},{5,13},{9,1},{13,5},{2,10},{6,14},... | collective-permute-start | bytes 196616 | tf_op jit(solution)/shard_map/ppermute | solution.py:353
  17.5 7.3 %collective-permute-start.6 = (bf16[256,128]{1,0:T(8,128)(2,1)S(1)}, bf16[256,128]{1,0:T(8,128)(2,1)S(1)}, u32[]{:S(2)}, u32[]{:S(2)}) collective-permute-start(bf16[256,128]{1,0:T(8,128)(2,1)S(1)} %get-tuple-element.15), channel_id=1, source_target_pairs={{0,12},{4,8},{8,4},{12,0},{1,13},{5,9},{9,5},{13,1},{2,14},{6,10},... | collective-permute-start | bytes 196616 | tf_op jit(solution)/shard_map/ppermute | solution.py:353
  20.3 5.7 %collective-permute-start.7 = (bf16[256,128]{1,0:T(8,128)(2,1)S(1)}, bf16[256,128]{1,0:T(8,128)(2,1)S(1)}, u32[]{:S(2)}, u32[]{:S(2)}) collective-permute-start(bf16[256,128]{1,0:T(8,128)(2,1)S(1)} %get-tuple-element.16), channel_id=1, source_target_pairs={{0,4},{4,0},{8,12},{12,8},{1,5},{5,1},{9,13},{13,9},{2,6},{6,2},{1... | collective-permute-start | bytes 196616 | tf_op jit(solution)/shard_map/ppermute | solution.py:358
  26.3 3.9 %collective-permute-start.10 = (bf16[3,32,128]{2,1,0:T(8,128)(2,1)S(1)}, bf16[3,32,128]{2,1,0:T(8,128)(2,1)S(1)}, u32[]{:S(2)}, u32[]{:S(2)}) collective-permute-start(bf16[3,32,128]{2,1,0:T(8,128)(2,1)S(1)} %get-tuple-element.20), channel_id=1, source_target_pairs={{0,4},{4,0},{8,12},{12,8},{1,5},{5,1},{9,13},{13,9},{2,6},{6,2},{1... | collective-permute-start | bytes 73736 | tf_op jit(solution)/shard_map/ppermute | solution.py:370
  27.0 5.6 %collective-permute-start.8 = (bf16[3,32,128]{2,1,0:T(8,128)(2,1)S(1)}, bf16[3,32,128]{2,1,0:T(8,128)(2,1)S(1)}, u32[]{:S(2)}, u32[]{:S(2)}) collective-permute-start(bf16[3,32,128]{2,1,0:T(8,128)(2,1)S(1)} %get-tuple-element.18), channel_id=1, source_target_pairs={{0,12},{4,8},{8,4},{12,0},{1,13},{5,9},{9,5},{13,1},{2,14},{6,10},... | collective-permute-start | bytes 73736 | tf_op jit(solution)/shard_map/ppermute | solution.py:370
  28.4 5.0 %collective-permute-start.9 = (bf16[3,32,128]{2,1,0:T(8,128)(2,1)S(1)}, bf16[3,32,128]{2,1,0:T(8,128)(2,1)S(1)}, u32[]{:S(2)}, u32[]{:S(2)}) collective-permute-start(bf16[3,32,128]{2,1,0:T(8,128)(2,1)S(1)} %get-tuple-element.19), channel_id=1, source_target_pairs={{0,8},{4,12},{8,0},{12,4},{1,9},{5,13},{9,1},{13,5},{2,10},{6,14},... | collective-permute-start | bytes 73736 | tf_op jit(solution)/shard_map/ppermute | solution.py:370
  33.4 1.4 %collective-permute-start.11 = (bf16[3,4,16,256]{3,2,1,0:T(8,128)(2,1)S(1)}, bf16[3,4,16,256]{3,2,1,0:T(8,128)(2,1)S(1)}, u32[]{:S(2)}, u32[]{:S(2)}) collective-permute-start(bf16[3,4,16,256]{3,2,1,0:T(8,128)(2,1)S(1)} %shard_map.78.cells_ref), channel_id=1, source_target_pairs={{0,1},{1,0},{2,3},{3,2},{4,5},{5,4},{6,7},{7,6},{8,9},{9,8},{10,11... | collective-permute-start | bytes 294920 | tf_op jit(solution)/shard_map/ppermute | solution.py:380
